TPU v7x, 256 devices: a whole 4x4x8 slice. The times are simulated.
256 devices in a mesh: gx: 8 (over z), gy: 32 (over y, x, core).
Axes of the slice: x: 4, y: 4, z: 8, core: 2. Of those that a mesh axis runs over, the one named last changes fastest.
Arguments:
- probes: float32 [4, 16, 512, 1024], P(None, None, 'gy', 'gx'), may hold values from -6 to 6
- winds: float32 [2, 4, 512, 1024], P(None, None, 'gy', 'gx'), may hold values from -0.4 to 0.4
- diffusivity: float32 [4, 512, 1024], P(None, 'gy', 'gx'), may hold values from 0.04 to 0.15
- mixing: float32 [512, 1024], P('gy', 'gx'), may hold values from 0.02 to 0.2
- prior_scale: float32 [4, 512, 1024], P(None, 'gy', 'gx'), may hold values from 0.3 to 3
- obs_weight: float32 [4, 512, 1024], P(None, 'gy', 'gx'), may hold values from 0.3 to 3
Outputs:
- basis: float32 [4, 16, 512, 1024], P(None, None, 'gy', 'gx')
- factor: float32 [16, 16], replicated
All inputs are finite; a program needn't handle non-finite values.
Results may differ from a plain program's by a relative error of at most 0.0003.
Values sent between devices are 32-bit elements; how exact they have to be, the bound alone decides.
No kernel may reach another device: no remote copies, remote signals or barrier semaphores. Data moves between devices by JAX's collectives and lax.ppermute only.
A program may use at most 64 MiB of HBM per device.

v0:
```python
import jax
import jax.numpy as jnp
from jax import lax
from jax.sharding import PartitionSpec as P

STEPS = 4


def padded(block, sides, width):
    for axis, dim in sides:
        count = lax.axis_size(axis)
        forward = [(i, i + 1) for i in range(count - 1)]
        backward = [(target, source) for source, target in forward]
        low = lax.ppermute(
            lax.slice_in_dim(block, block.shape[dim] - width, None, axis=dim), axis, forward
        )
        high = lax.ppermute(lax.slice_in_dim(block, 0, width, axis=dim), axis, backward)
        block = jnp.concatenate([low, block, high], axis=dim)
    return block


def vertical(field):
    above = jnp.concatenate([field[1:], field[-1:]], axis=0)
    below = jnp.concatenate([field[:1], field[:-1]], axis=0)
    return above + below - 2.0 * field


def forward_step(extended, coefs):
    center = extended[..., 1:-1, 1:-1]
    east = extended[..., 1:-1, 2:]
    west = extended[..., 1:-1, :-2]
    north = extended[..., 2:, 1:-1]
    south = extended[..., :-2, 1:-1]
    kappa = coefs[0][:, None]
    wind_x = coefs[1][:, None]
    wind_y = coefs[2][:, None]
    rate = coefs[3][:, None]
    return (
        center
        + kappa * (east + west + north + south - 4.0 * center)
        - wind_x * (east - west)
        - wind_y * (north - south)
        + rate * vertical(center)
    )


def adjoint_step(extended, coefs):
    kappa_g = coefs[0][:, None] * extended
    wind_xg = coefs[1][:, None] * extended
    wind_yg = coefs[2][:, None] * extended
    rate = coefs[3][:, None, 1:-1, 1:-1]
    center = extended[..., 1:-1, 1:-1]
    spread = (
        kappa_g[..., 1:-1, 2:]
        + kappa_g[..., 1:-1, :-2]
        + kappa_g[..., 2:, 1:-1]
        + kappa_g[..., :-2, 1:-1]
        - 4.0 * kappa_g[..., 1:-1, 1:-1]
    )
    carried = (
        wind_xg[..., 1:-1, 2:]
        - wind_xg[..., 1:-1, :-2]
        + wind_yg[..., 2:, 1:-1]
        - wind_yg[..., :-2, 1:-1]
    )
    return center + spread + carried + rate * vertical(center)


def gram_sum(local):
    return lax.psum(local, ("gx", "gy"))


def upper_factor(gram):
    count = gram.shape[0]
    positions = jnp.arange(count, dtype=jnp.int32)
    factor_rows = []
    for index in range(count):
        residual_row = gram[index]
        for earlier in factor_rows:
            residual_row = residual_row - earlier[index] * earlier
        pivot = jnp.sqrt(residual_row[index])
        factor_rows.append(
            jnp.where(positions >= index, residual_row / pivot, jnp.zeros_like(residual_row))
        )
    return jnp.stack(factor_rows)


def upper_inverse(upper):
    count = upper.shape[0]
    eye = jnp.eye(count, dtype=upper.dtype)
    solved = [None] * count
    for index in range(count - 1, -1, -1):
        row_value = eye[index]
        for later in range(index + 1, count):
            row_value = row_value - upper[index, later] * solved[later]
        solved[index] = row_value / upper[index, index]
    return jnp.stack(solved)


def cholesky_pass(matrix):
    local = jnp.einsum("lkyx,lmyx->km", matrix, matrix, precision=lax.Precision.HIGHEST)
    gram = gram_sum(local)
    upper = upper_factor(gram)
    inverse = upper_inverse(upper)
    result = jnp.einsum("lkyx,km->lmyx", matrix, inverse, precision=lax.Precision.HIGHEST)
    return (result, upper)


def body(probes, winds, diffusivity, mixing, prior_scale, obs_weight):
    coefs = jnp.stack(
        [diffusivity, winds[0], winds[1], jnp.broadcast_to(mixing, diffusivity.shape)]
    )
    source = prior_scale[:, None] * probes
    rows = probes.shape[2]
    cols = probes.shape[3]
    total = jnp.zeros_like(source)
    coefs_one = padded(coefs, (("gx", 3), ("gy", 2)), 1)
    state = jnp.zeros_like(source)
    for step in range(STEPS):
        extended = padded(state + source, (("gx", 3), ("gy", 2)), 1)
        state = forward_step(extended, coefs)
    weighted = obs_weight[:, None] * state
    for step in range(STEPS):
        extended = padded(weighted, (("gx", 3), ("gy", 2)), 1)
        weighted = adjoint_step(extended, coefs_one)
        total = total + weighted
    image = prior_scale[:, None] * total
    first, upper_one = cholesky_pass(image)
    second, upper_two = cholesky_pass(first)
    count = probes.shape[0] * rows * cols * lax.axis_size("gx") * lax.axis_size("gy")
    scale = jnp.sqrt(jnp.float32(count))
    factor = jnp.dot(upper_two, upper_one, precision=lax.Precision.HIGHEST) / scale
    return (second * scale, factor)


def solution(mesh):
    placed = (
        P(None, None, "gy", "gx"),
        P(None, None, "gy", "gx"),
        P(None, "gy", "gx"),
        P("gy", "gx"),
        P(None, "gy", "gx"),
        P(None, "gy", "gx"),
    )
    return jax.shard_map(
        body,
        mesh=mesh,
        in_specs=placed,
        out_specs=(P(None, None, "gy", "gx"), P()),
        check_vma=False,
    )
```

profile of v0, /device:TPU:1, one launch (start us, length us, event | category | flops | bytes accessed | tf_op | source)
XLA Modules:
  0.0 1064.3 jit_solution(12363108878769122408)
XLA Ops:
  3.3 5.0 collective-permute-start.1
  13.4 6.4 collective-permute-done.16
  20.0 6.4 collective-permute-start.18
  38.2 4.9 collective-permute-start.5
  43.1 8.5 collective-permute-done.4
  56.0 4.6 collective-permute-start.7
  64.4 4.8 collective-permute-start.9
  69.2 7.4 collective-permute-done.8
  80.8 5.5 collective-permute-start.11
  90.1 4.8 collective-permute-start.13
  95.0 6.6 collective-permute-done.12
  105.7 8.1 collective-permute-start.15
  116.2 4.9 collective-permute-start.20
  122.5 5.2 collective-permute-done.20
  127.6 5.5 collective-permute-done.21
  133.6 10.3 collective-permute-start.22
  151.7 5.3 collective-permute-start.24
  158.5 8.4 collective-permute-done.24
  166.8 5.8 collective-permute-done.25
  184.3 4.6 collective-permute-start.28
  190.2 8.4 collective-permute-done.28
  198.6 4.4 collective-permute-done.29
  220.3 8.4 collective-permute-done.32
  245.8 78.6 %psum.14 = f32[16,16]{1,0:T(8,128)S(1)} all-reduce(f32[16,16]{1,0:T(8,128)S(1)} %convolution_bitcast_fusion.2), channel_id=1, replica_groups=mesh['gx'=8,'gy'=32] {'gx','gy'}, use_global_device_ids=true, to_apply=%region_0.0 | all-reduce | flops 256 | bytes 2048 | tf_op jit(solution)/shard_map/psum | solution.py:70
  351.7 4.4 multiply_subtract_fusion.18
  358.0 4.9 multiply_subtract_fusion.17
  364.9 5.5 multiply_subtract_fusion.16
  372.4 6.1 multiply_subtract_fusion.15
  380.5 6.9 multiply_subtract_fusion.14
  389.2 7.5 multiply_subtract_fusion.13
  398.7 8.2 multiply_subtract_fusion.12
  408.7 8.3 multiply_subtract_fusion.11
  419.1 9.5 multiply_subtract_fusion.10
  430.0 74.1 %compare_select_fusion.3 = (f32[1,16]{1,0:T(1,128)S(1)}, f32[1,16]{1,0:T(1,128)S(1)}, f32[1,16]{1,0:T(1,128)S(1)}, f32[1,16]{1,0:T(1,128)S(1)}, f32[1,16]{1,0:T(...) fusion(f32[]{:T(128)} %bitcast.184, ...), kind=kLoop, calls=%fused_computation.179 | loop fusion | flops 4528 | bytes 2456 | tf_op jit(solution)/shard_map/jit(_where)/select_n | solution.py:83
  511.7 65.3 %subtract_divide_fusion.15 = (f32[1,16]{1,0:T(1,128)S(1)}, f32[1,16]{1,0:T(1,128)S(1)}, f32[1,16]{1,0:T(1,128)S(1)}, f32[1,16]{1,0:T(1,128)S(1)}, f32[1,16]{1,0:...) fusion(f32[]{:T(128)} %bitcast.307, ...), kind=kLoop, calls=%fused_computation.571 | loop fusion | flops 3136 | bytes 2276 | tf_op jit(solution)/shard_map/div | solution.py:96
  577.0 77.2 %fusion.186 = (f32[1,16]{1,0:T(1,128)S(1)}, f32[16]{0:T(128)S(1)}) fusion(f32[1,16]{1,0:T(1,128)S(1)} %get-tuple-element.51, f32[1,16]{1,0:T(1,128)S(1)} %get-tuple-element.50, f32[1,16]{1,0:T(1,128)S(1)} %get-tuple-element.49, f32[1,16]{1,0:T(1,128)S(1)} %get-tuple-element.48, f32[16,16]{1,0:T(8,128)S(1)} %fusion.47, f32[]{:T(128)} %bitcast.338, ...), kind=kLoop, calls=%fused_computation.592 | loop fusion | flops 3776 | bytes 1648 | tf_op jit(solution)/shard_map/stack | solution.py:97
  655.8 73.8 %psum.15 = f32[16,16]{1,0:T(8,128)S(1)} all-reduce(f32[16,16]{1,0:T(8,128)S(1)} %convolution_bitcast_fusion.1), channel_id=1, replica_groups=mesh['gx'=8,'gy'=32] {'gx','gy'}, use_global_device_ids=true, to_apply=%region_1.2 | all-reduce | flops 256 | bytes 2048 | tf_op jit(solution)/shard_map/psum | solution.py:70
  763.2 4.9 multiply_subtract_fusion.7
  770.1 5.5 multiply_subtract_fusion.6
  777.6 6.1 multiply_subtract_fusion.5
  785.6 6.9 multiply_subtract_fusion.4
  794.3 7.5 multiply_subtract_fusion.3
  803.8 8.2 multiply_subtract_fusion.2
  813.9 8.3 multiply_subtract_fusion.1
  824.2 9.5 multiply_subtract_fusion
  835.1 74.1 %compare_select_fusion.2 = (f32[1,16]{1,0:T(1,128)S(1)}, f32[1,16]{1,0:T(1,128)S(1)}, f32[1,16]{1,0:T(1,128)S(1)}, f32[1,16]{1,0:T(1,128)S(1)}, f32[1,16]{1,0:T(...) fusion(f32[]{:T(128)} %bitcast.509, ...), kind=kLoop, calls=%fused_computation.178 | loop fusion | flops 4528 | bytes 2456 | tf_op jit(solution)/shard_map/jit(_where)/select_n | solution.py:83
  919.5 65.3 %subtract_divide_fusion.4 = (f32[1,16]{1,0:T(1,128)S(1)}, f32[1,16]{1,0:T(1,128)S(1)}, f32[1,16]{1,0:T(1,128)S(1)}, f32[1,16]{1,0:T(1,128)S(1)}, f32[1,16]{1,0:T...) fusion(f32[]{:T(128)} %bitcast.632, ...), kind=kLoop, calls=%fused_computation.550 | loop fusion | flops 3136 | bytes 2276 | tf_op jit(solution)/shard_map/div | solution.py:96
  984.7 77.2 %fusion.187 = (f32[1,16]{1,0:T(1,128)S(1)}, f32[16]{0:T(128)S(1)}) fusion(f32[1,16]{1,0:T(1,128)S(1)} %get-tuple-element.18, f32[1,16]{1,0:T(1,128)S(1)} %get-tuple-element.17, f32[1,16]{1,0:T(1,128)S(1)} %get-tuple-element.16, f32[1,16]{1,0:T(1,128)S(1)} %get-tuple-element.15, f32[16,16]{1,0:T(8,128)S(1)} %fusion.47, f32[]{:T(128)} %bitcast.663, ...), kind=kLoop, calls=%fused_computation.593 | loop fusion | flops 3776 | bytes 1648 | tf_op jit(solution)/shard_map/stack | solution.py:97
  (258 shorter events, 193.2 us)
Async XLA Ops:
  0.6 7.7 copy-start.2
  0.6 7.7 copy-start.4
  0.7 7.7 copy-start.1
  2.0 26.4 %collective-permute-start = (f32[4,16,16,1]{3,2,1,0:T(8,128)S(1)}, f32[4,16,16,1]{3,2,1,0:T(8,128)S(1)}, u32[]{:S(2)}, u32[]{:S(2)}) collective-permute-start(f32[4,16,16,1]{3,2,1,0:T(8,128)S(1)} %get-tuple-element.141), channel_id=1, source_target_pairs={{32,0},{64,32},{96,64},{128,96},{160,128},{192,160},{224,192},{33,... | collective-permute-start | bytes 12296 | tf_op jit(solution)/shard_map/ppermute | solution.py:17
  3.3 25.1 %collective-permute-start.1 = (f32[4,16,16,1]{3,2,1,0:T(8,128)S(1)}, f32[4,16,16,1]{3,2,1,0:T(8,128)S(1)}, u32[]{:S(2)}, u32[]{:S(2)}) collective-permute-start(f32[4,16,16,1]{3,2,1,0:T(8,128)S(1)} %get-tuple-element.140), channel_id=1, source_target_pairs={{0,32},{32,64},{64,96},{96,128},{128,160},{160,192},{192,224},{1,3... | collective-permute-start | bytes 12296 | tf_op jit(solution)/shard_map/ppermute | solution.py:14
  8.5 11.3 %collective-permute-start.16 = (f32[4,4,16,1]{3,2,1,0:T(8,128)S(1)}, f32[4,4,16,1]{3,2,1,0:T(8,128)S(1)}, u32[]{:S(2)}, u32[]{:S(2)}) collective-permute-start(f32[4,4,16,1]{3,2,1,0:T(8,128)S(1)} %get-tuple-element.152), channel_id=1, source_target_pairs={{0,32},{32,64},{64,96},{96,128},{128,160},{160,192},{192,224},{1,3... | collective-permute-start | bytes 3080 | tf_op jit(solution)/shard_map/ppermute | solution.py:14
  12.0 7.8 collective-permute-start.17
  20.0 14.4 %collective-permute-start.18 = (f32[4,4,1,130]{3,2,1,0:T(1,128)S(1)}, f32[4,4,1,130]{3,2,1,0:T(1,128)S(1)}, u32[]{:S(2)}, u32[]{:S(2)}) collective-permute-start(f32[4,4,1,130]{3,2,1,0:T(1,128)S(1)} %get-tuple-element.150), channel_id=1, source_target_pairs={{0,1},{1,2},{2,3},{3,4},{4,5},{5,6},{6,7},{7,8},{8,9},{9,10},{10,1... | collective-permute-start | bytes 24968 | tf_op jit(solution)/shard_map/ppermute | solution.py:14
  26.4 8.0 collective-permute-start.19
  28.8 5.9 collective-permute-start.2
  30.8 5.0 collective-permute-start.3
  36.8 14.8 %collective-permute-start.4 = (f32[4,16,16,1]{3,2,1,0:T(8,128)S(1)}, f32[4,16,16,1]{3,2,1,0:T(8,128)S(1)}, u32[]{:S(2)}, u32[]{:S(2)}) collective-permute-start(f32[4,16,16,1]{3,2,1,0:T(8,128)S(1)} %get-tuple-element.135), channel_id=1, source_target_pairs={{32,0},{64,32},{96,64},{128,96},{160,128},{192,160},{224,192},{33,... | collective-permute-start | bytes 12296 | tf_op jit(solution)/shard_map/ppermute | solution.py:17
  38.1 23.7 %copy-start = (f32[4,16,16,128]{3,2,1,0:T(8,128)S(1)}, f32[4,16,16,128]{3,2,1,0:T(8,128)}, u32[]{:S(2)}) copy-start(f32[4,16,16,128]{3,2,1,0:T(8,128)} %param.6) | copy-start | bytes 1572868
  38.2 23.7 %copy-start.3 = (f32[4,16,128]{2,1,0:T(8,128)S(1)}, f32[4,16,128]{2,1,0:T(8,128)}, u32[]{:S(2)}) copy-start(f32[4,16,128]{2,1,0:T(8,128)} %param.10) | copy-start | bytes 98308
  38.2 15.4 %collective-permute-start.5 = (f32[4,16,16,1]{3,2,1,0:T(8,128)S(1)}, f32[4,16,16,1]{3,2,1,0:T(8,128)S(1)}, u32[]{:S(2)}, u32[]{:S(2)}) collective-permute-start(f32[4,16,16,1]{3,2,1,0:T(8,128)S(1)} %get-tuple-element.134), channel_id=1, source_target_pairs={{0,32},{32,64},{64,96},{96,128},{128,160},{160,192},{192,224},{1,3... | collective-permute-start | bytes 12296 | tf_op jit(solution)/shard_map/ppermute | solution.py:14
  54.0 6.6 collective-permute-start.6
  56.0 5.9 collective-permute-start.7
  63.1 13.6 %collective-permute-start.8 = (f32[4,16,16,1]{3,2,1,0:T(8,128)S(1)}, f32[4,16,16,1]{3,2,1,0:T(8,128)S(1)}, u32[]{:S(2)}, u32[]{:S(2)}) collective-permute-start(f32[4,16,16,1]{3,2,1,0:T(8,128)S(1)} %get-tuple-element.129), channel_id=1, source_target_pairs={{32,0},{64,32},{96,64},{128,96},{160,128},{192,160},{224,192},{33,... | collective-permute-start | bytes 12296 | tf_op jit(solution)/shard_map/ppermute | solution.py:17
  64.4 14.0 %collective-permute-start.9 = (f32[4,16,16,1]{3,2,1,0:T(8,128)S(1)}, f32[4,16,16,1]{3,2,1,0:T(8,128)S(1)}, u32[]{:S(2)}, u32[]{:S(2)}) collective-permute-start(f32[4,16,16,1]{3,2,1,0:T(8,128)S(1)} %get-tuple-element.128), channel_id=1, source_target_pairs={{0,32},{32,64},{64,96},{96,128},{128,160},{160,192},{192,224},{1,3... | collective-permute-start | bytes 12296 | tf_op jit(solution)/shard_map/ppermute | solution.py:14
  78.9 7.5 collective-permute-start.10
  80.8 6.9 collective-permute-start.11
  88.8 12.7 %collective-permute-start.12 = (f32[4,16,16,1]{3,2,1,0:T(8,128)S(1)}, f32[4,16,16,1]{3,2,1,0:T(8,128)S(1)}, u32[]{:S(2)}, u32[]{:S(2)}) collective-permute-start(f32[4,16,16,1]{3,2,1,0:T(8,128)S(1)} %get-tuple-element.123), channel_id=1, source_target_pairs={{32,0},{64,32},{96,64},{128,96},{160,128},{192,160},{224,192},{33,... | collective-permute-start | bytes 12296 | tf_op jit(solution)/shard_map/ppermute | solution.py:17
  90.1 25.0 %copy-start.5 = (f32[4,16,128]{2,1,0:T(8,128)S(1)}, f32[4,16,128]{2,1,0:T(8,128)}, u32[]{:S(2)}) copy-start(f32[4,16,128]{2,1,0:T(8,128)} %param.11) | copy-start | bytes 98308
  90.1 13.2 %collective-permute-start.13 = (f32[4,16,16,1]{3,2,1,0:T(8,128)S(1)}, f32[4,16,16,1]{3,2,1,0:T(8,128)S(1)}, u32[]{:S(2)}, u32[]{:S(2)}) collective-permute-start(f32[4,16,16,1]{3,2,1,0:T(8,128)S(1)} %get-tuple-element.122), channel_id=1, source_target_pairs={{0,32},{32,64},{64,96},{96,128},{128,160},{160,192},{192,224},{1,3... | collective-permute-start | bytes 12296 | tf_op jit(solution)/shard_map/ppermute | solution.py:14
  103.8 10.1 collective-permute-start.14
  105.7 9.4 collective-permute-start.15
  116.2 11.4 %collective-permute-start.20 = (f32[4,16,16,1]{3,2,1,0:T(8,128)S(1)}, f32[4,16,16,1]{3,2,1,0:T(8,128)S(1)}, u32[]{:S(2)}, u32[]{:S(2)}) collective-permute-start(f32[4,16,16,1]{3,2,1,0:T(8,128)S(1)} %get-tuple-element.120), channel_id=1, source_target_pairs={{0,32},{32,64},{64,96},{96,128},{128,160},{160,192},{192,224},{1,3... | collective-permute-start | bytes 12296 | tf_op jit(solution)/shard_map/ppermute | solution.py:14
  121.1 12.0 %collective-permute-start.21 = (f32[4,16,16,1]{3,2,1,0:T(8,128)S(1)}, f32[4,16,16,1]{3,2,1,0:T(8,128)S(1)}, u32[]{:S(2)}, u32[]{:S(2)}) collective-permute-start(f32[4,16,16,1]{3,2,1,0:T(8,128)S(1)} %get-tuple-element.121), channel_id=1, source_target_pairs={{32,0},{64,32},{96,64},{128,96},{160,128},{192,160},{224,192},{33,... | collective-permute-start | bytes 12296 | tf_op jit(solution)/shard_map/ppermute | solution.py:17
  133.6 12.4 %collective-permute-start.22 = (f32[4,16,1,130]{3,2,1,0:T(1,128)S(1)}, f32[4,16,1,130]{3,2,1,0:T(1,128)S(1)}, u32[]{:S(2)}, u32[]{:S(2)}) collective-permute-start(f32[4,16,1,130]{3,2,1,0:T(1,128)S(1)} %get-tuple-element.88), channel_id=1, source_target_pairs={{0,1},{1,2},{2,3},{3,4},{4,5},{5,6},{6,7},{7,8},{8,9},{9,10},{10,1... | collective-permute-start | bytes 99848 | tf_op jit(solution)/shard_map/ppermute | solution.py:14
  143.9 5.6 collective-permute-start.23
  151.7 15.1 %collective-permute-start.24 = (f32[4,16,16,1]{3,2,1,0:T(8,128)S(1)}, f32[4,16,16,1]{3,2,1,0:T(8,128)S(1)}, u32[]{:S(2)}, u32[]{:S(2)}) collective-permute-start(f32[4,16,16,1]{3,2,1,0:T(8,128)S(1)} %get-tuple-element.114), channel_id=1, source_target_pairs={{0,32},{32,64},{64,96},{96,128},{128,160},{160,192},{192,224},{1,3... | collective-permute-start | bytes 12296 | tf_op jit(solution)/shard_map/ppermute | solution.py:14
  157.1 15.5 %collective-permute-start.25 = (f32[4,16,16,1]{3,2,1,0:T(8,128)S(1)}, f32[4,16,16,1]{3,2,1,0:T(8,128)S(1)}, u32[]{:S(2)}, u32[]{:S(2)}) collective-permute-start(f32[4,16,16,1]{3,2,1,0:T(8,128)S(1)} %get-tuple-element.115), channel_id=1, source_target_pairs={{32,0},{64,32},{96,64},{128,96},{160,128},{192,160},{224,192},{33,... | collective-permute-start | bytes 12296 | tf_op jit(solution)/shard_map/ppermute | solution.py:17
  173.1 5.4 collective-permute-start.26
  176.5 5.6 collective-permute-start.27
  184.3 14.3 %collective-permute-start.28 = (f32[4,16,16,1]{3,2,1,0:T(8,128)S(1)}, f32[4,16,16,1]{3,2,1,0:T(8,128)S(1)}, u32[]{:S(2)}, u32[]{:S(2)}) collective-permute-start(f32[4,16,16,1]{3,2,1,0:T(8,128)S(1)} %get-tuple-element.108), channel_id=1, source_target_pairs={{0,32},{32,64},{64,96},{96,128},{128,160},{160,192},{192,224},{1,3... | collective-permute-start | bytes 12296 | tf_op jit(solution)/shard_map/ppermute | solution.py:14
  188.9 14.1 %collective-permute-start.29 = (f32[4,16,16,1]{3,2,1,0:T(8,128)S(1)}, f32[4,16,16,1]{3,2,1,0:T(8,128)S(1)}, u32[]{:S(2)}, u32[]{:S(2)}) collective-permute-start(f32[4,16,16,1]{3,2,1,0:T(8,128)S(1)} %get-tuple-element.109), channel_id=1, source_target_pairs={{32,0},{64,32},{96,64},{128,96},{160,128},{192,160},{224,192},{33,... | collective-permute-start | bytes 12296 | tf_op jit(solution)/shard_map/ppermute | solution.py:17
  203.5 5.7 collective-permute-start.30
  207.2 5.6 collective-permute-start.31
  215.0 13.7 %collective-permute-start.32 = (f32[4,16,16,1]{3,2,1,0:T(8,128)S(1)}, f32[4,16,16,1]{3,2,1,0:T(8,128)S(1)}, u32[]{:S(2)}, u32[]{:S(2)}) collective-permute-start(f32[4,16,16,1]{3,2,1,0:T(8,128)S(1)} %get-tuple-element.102), channel_id=1, source_target_pairs={{0,32},{32,64},{64,96},{96,128},{128,160},{160,192},{192,224},{1,3... | collective-permute-start | bytes 12296 | tf_op jit(solution)/shard_map/ppermute | solution.py:14
  219.0 13.9 %collective-permute-start.33 = (f32[4,16,16,1]{3,2,1,0:T(8,128)S(1)}, f32[4,16,16,1]{3,2,1,0:T(8,128)S(1)}, u32[]{:S(2)}, u32[]{:S(2)}) collective-permute-start(f32[4,16,16,1]{3,2,1,0:T(8,128)S(1)} %get-tuple-element.103), channel_id=1, source_target_pairs={{32,0},{64,32},{96,64},{128,96},{160,128},{192,160},{224,192},{33,... | collective-permute-start | bytes 12296 | tf_op jit(solution)/shard_map/ppermute | solution.py:17
  233.3 6.1 collective-permute-start.34
  237.4 5.6 collective-permute-start.35
where the time goes:
time: 1070 us; the launch traced here: 1060 us
  other arithmetic  599 us (56%)
  blocking collectives  152 us (14%)
  starting transfers between devices  121 us (11%)
  waiting for transfers between devices  103 us (10%)
  local copies, waits for them, and re-layouts  61.3 us (6%)
  between operations  23.4 us (2%)
    another operation x2, other arithmetic, upper_inverse(): return jnp.stack(solved)  154 us
    psum x2, blocking collectives, gram_sum(): return lax.psum(local, ('gx', 'gy'))  152 us
    sub x30, other arithmetic, upper_factor(): residual_row = residual_row - earlier[index] * earlier  149 us
    select_n x32, other arithmetic, upper_factor(): jnp.where(positions >= index, residual_row / pivot, jnp.zeros_like(residu...  148 us
    div x2, other arithmetic, upper_inverse(): solved[index] = row_value / upper[index, index]  131 us
    ppermute x18, starting transfers between devices, padded(): lax.ppermute(lax.slice_in_dim(block, block.shape[dim] - width, None, axis...  91.6 us
    ppermute x18, waiting for transfers between devices, padded(): lax.ppermute(lax.slice_in_dim(block, 0, width, axis=dim), axis, backward)  56.6 us
    ppermute x18, waiting for transfers between devices, padded(): lax.ppermute(lax.slice_in_dim(block, block.shape[dim] - width, None, axis...  46.8 us
  transfers between devices with their start and end apart: 36, of which 23 were waited for; matrix products, arithmetic and copies ran while one was open for 0% of the time, Pallas kernels for 0%

commit v1 on v0

v1 whole, which is shorter than its diff:
```python
import math
import jax
import jax.numpy as jnp
from jax import lax
from jax.experimental import pallas as pl
from jax.experimental.pallas import tpu as pltpu
from jax.sharding import PartitionSpec as P

STEPS = 4
LEVELS = 4
PROBES = 16
HALO = 2 * STEPS
LANES = 128
ROWS = 16
EXT = ROWS + 2 * HALO
F32 = jnp.float32

FIELDS = 17
GROUPS = 3
EAST, WEST, NORTH, SOUTH, CENTER, RATE, OBS, DERIVED = 0, 4, 8, 12, 16, 20, 21, 25
X_PARTS = ROWS + 2 * GROUPS
Y_SOURCE, Y_HALO, Y_COEF, Y_COEF_HALO, Y_PARTS = 0, 64, 72, 89, 92
SLICES = 4


def lane_ids():
    return lax.broadcasted_iota(jnp.int32, (8, LANES), 1)


def roll_lanes(value, shift):
    shift = shift % LANES
    return value if shift == 0 else pltpu.roll(value, shift, value.ndim - 1)


def raw_field(refs, field, rows):
    diffusivity, winds, obs, mixing = refs
    if field < 4:
        return diffusivity[field, rows, :]
    if field < 8:
        return winds[0, field - 4, rows, :]
    if field < 12:
        return winds[1, field - 8, rows, :]
    if field < 16:
        return obs[field - 12, rows, :]
    return mixing[rows, :]


def pack_kernel(probes, winds, diffusivity, mixing, prior, obs, source, east, west):
    lanes = lane_ids()
    half = lanes // 8

    def put(held, value, slot):
        to_east, to_west = held
        to_east = jnp.where(half == 2 * slot + 1, roll_lanes(value, 16 * slot + 8 - (LANES - HALO)), to_east)
        to_west = jnp.where(half == 2 * slot, roll_lanes(value, 16 * slot), to_west)
        return to_east, to_west

    zero = jnp.zeros((8, LANES), F32)

    def row(y, carry):
        held = (zero, zero)
        for level in range(LEVELS):
            scale = prior[level, pl.ds(y, 1), :]
            for part in range(2):
                value = probes[level, pl.ds(part * 8 * ROWS + y, 8, stride=ROWS), :] * scale
                source[y, level, part] = value
                held = put(held, value, 2 * level + part)
        east[y], west[y] = held
        return carry

    lax.fori_loop(0, ROWS, row, 0, unroll=2)
    refs = (diffusivity, winds, obs, mixing)
    for group in range(GROUPS):
        for tile in range(2):
            held = (zero, zero)
            for slot in range(8):
                field = 8 * group + slot
                if field < FIELDS:
                    held = put(held, raw_field(refs, field, pl.ds(8 * tile, 8)), slot)
            east[ROWS + 2 * group + tile], west[ROWS + 2 * group + tile] = held


def merge_kernel(from_west, from_east, source, winds, diffusivity, mixing, obs, halo, north, south):
    inner = lane_ids() % 16 < 8
    for index in range(X_PARTS):
        halo[index] = jnp.where(inner, from_east[index], from_west[index])
    refs = (diffusivity, winds, obs, mixing)
    for tile, out in ((0, south), (1, north)):
        for y in range(8):
            for level in range(LEVELS):
                for part in range(2):
                    out[(y * LEVELS + level) * 2 + part] = source[8 * tile + y, level, part]
            out[Y_HALO + y] = jnp.where(inner, from_east[8 * tile + y], from_west[8 * tile + y])
        for field in range(FIELDS):
            out[Y_COEF + field] = raw_field(refs, field, pl.ds(8 * tile, 8))
        for group in range(GROUPS):
            index = ROWS + 2 * group + tile
            out[Y_COEF_HALO + group] = jnp.where(inner, from_east[index], from_west[index])


def strip_of(lanes, first, second, halo_first, halo_second, slot_first, slot_second):
    value = roll_lanes(first, 24)
    value = jnp.where(lanes >= 24, roll_lanes(halo_first, 24 - 16 * slot_first), value)
    value = jnp.where(lanes >= 40, roll_lanes(first, 40), value)
    value = jnp.where(lanes >= 64, roll_lanes(second, 88), value)
    value = jnp.where(lanes >= 88, roll_lanes(halo_second, 88 - 16 * slot_second), value)
    return jnp.where(lanes >= 104, roll_lanes(second, 104), value)


def two_sum(a, b):
    total = a + b
    other = total - a
    return total, (a - (total - other)) + (b - other)


def stencil_kernel(
    source, halo, winds, diffusivity, mixing, prior, obs, from_south, from_north,
    image, message, start, first, second, adjoints, coefs, slices,
):
    lanes = lane_ids()
    refs = (diffusivity, winds, obs, mixing)

    for tile in range(4):
        if tile in (1, 2):
            main = [raw_field(refs, field, pl.ds(8 * (tile - 1), 8)) for field in range(FIELDS)]
            packed = [halo[ROWS + 2 * group + tile - 1] for group in range(GROUPS)]
        else:
            ref = from_south if tile == 0 else from_north
            main = [ref[Y_COEF + field] for field in range(FIELDS)]
            packed = [ref[Y_COEF_HALO + group] for group in range(GROUPS)]
        strips = [
            strip_of(lanes, main[field], main[field], packed[field // 8], packed[field // 8], field % 8, field % 8)
            for field in range(FIELDS)
        ]
        rows = pl.ds(8 * tile, 8)
        for kind, values in ((0, main), (1, strips)):
            rate = values[16]
            coefs[kind, RATE, rows, :] = rate
            for level in range(LEVELS):
                kappa, wind_x, wind_y = values[level], values[4 + level], values[8 + level]
                coefs[kind, EAST + level, rows, :] = kappa - wind_x
                coefs[kind, WEST + level, rows, :] = kappa + wind_x
                coefs[kind, NORTH + level, rows, :] = kappa - wind_y
                coefs[kind, SOUTH + level, rows, :] = kappa + wind_y
                sides = 1.0 if level in (0, LEVELS - 1) else 2.0
                coefs[kind, CENTER + level, rows, :] = 1.0 - 4.0 * kappa - sides * rate
                coefs[kind, OBS + level, rows, :] = values[12 + level]

    def load_rows(get, get_halo, base):
        def row(y, carry):
            packed = get_halo(y)
            for level in range(LEVELS):
                low, high = get(y, level, 0), get(y, level, 1)
                start[base + y, level, 0] = low
                start[base + y, level, 1] = high
                start[base + y, level, 2] = strip_of(lanes, low, high, packed, packed, 2 * level, 2 * level + 1)
            return carry
        return row

    def beside(ref):
        return (lambda y, level, part: ref[(y * LEVELS + level) * 2 + part]), (lambda y: ref[Y_HALO + y])

    lax.fori_loop(0, HALO, load_rows(*beside(from_south), 0), 0)
    lax.fori_loop(0, ROWS, load_rows(lambda y, level, part: source[y, level, part], lambda y: halo[y], HALO), 0)
    lax.fori_loop(0, HALO, load_rows(*beside(from_north), HALO + ROWS), 0)

    def vertical(values, level):
        if level == 0:
            return values[1]
        if level == LEVELS - 1:
            return values[LEVELS - 2]
        return values[level - 1] + values[level + 1]

    def forward(ref, y, part):
        kind = part // 2
        coef = lambda index: coefs[kind, index, pl.ds(y, 1), :]
        center = [ref[y, level, part] for level in range(LEVELS)]
        rate = coef(RATE)
        out = []
        for level in range(LEVELS):
            value = center[level]
            out.append(
                coef(CENTER + level) * value
                + coef(EAST + level) * roll_lanes(value, -1)
                + coef(WEST + level) * roll_lanes(value, 1)
                + coef(NORTH + level) * ref[y + 1, level, part]
                + coef(SOUTH + level) * ref[y - 1, level, part]
                + rate * vertical(center, level)
            )
        return out

    def adjoint(ref, y, part):
        kind = part // 2
        coef = lambda index, at: coefs[kind, index, pl.ds(at, 1), :]
        center = [ref[y, level, part] for level in range(LEVELS)]
        rate = coef(RATE, y)
        out = []
        for level in range(LEVELS):
            value = center[level]
            out.append(
                coef(CENTER + level, y) * value
                + roll_lanes(coef(WEST + level, y) * value, -1)
                + roll_lanes(coef(EAST + level, y) * value, 1)
                + coef(SOUTH + level, y + 1) * ref[y + 1, level, part]
                + coef(NORTH + level, y - 1) * ref[y - 1, level, part]
                + rate * vertical(center, level)
            )
        return out

    held = [start, first, second, first, second]
    for step in range(1, STEPS + 1):
        def row(y, carry, step=step):
            for part in range(3):
                values = forward(held[step - 1], y, part)
                for level in range(LEVELS):
                    if step < STEPS:
                        value = values[level] + start[y, level, part]
                    else:
                        value = values[level] * coefs[part // 2, OBS + level, pl.ds(y, 1), :]
                    held[step][y, level, part] = value
            return carry
        lax.fori_loop(step, EXT - step, row, 0)

    held = [second] + [adjoints.at[index] for index in range(STEPS - 1)]
    for step in range(1, STEPS):
        def row(y, carry, step=step):
            for part in range(3):
                values = adjoint(held[step - 1], y, part)
                for level in range(LEVELS):
                    held[step][y, level, part] = values[level]
            return carry
        lax.fori_loop(STEPS + step, EXT - STEPS - step, row, 0)

    def last_row(y, most):
        totals = []
        for part in range(3):
            values = adjoint(held[STEPS - 1], y, part)
            totals.append([
                values[level] + held[1][y, level, part] + held[2][y, level, part] + held[3][y, level, part]
                for level in range(LEVELS)
            ])
        most = list(most)
        for level in range(LEVELS):
            scale = prior[level, pl.ds(y - HALO, 1), :]
            strip = totals[2][level]
            for part in range(2):
                value = jnp.where(lanes < HALO, roll_lanes(strip, -40 - 64 * part), totals[part][level])
                value = jnp.where(lanes >= LANES - HALO, roll_lanes(strip, 104 - 64 * part), value)
                value = value * scale
                image[y - HALO, level, part] = value
                most[part] = jnp.maximum(most[part], jnp.abs(value))
        return tuple(most)

    zero = jnp.zeros((8, LANES), F32)
    most = lax.fori_loop(HALO, HALO + ROWS, last_row, (zero, zero))

    magics = []
    for part in range(2):
        top = jnp.broadcast_to(jnp.max(most[part], axis=1, keepdims=True), (8, LANES))
        scaled = top * (2.0**23 + 1.0)
        power = jnp.abs(scaled - scaled * (1.0 - 2.0**-24))
        magics.append([power * (1.5 * 2.0 ** (23 - 6 - 8 * index)) for index in range(SLICES)])

    def slice_row(y, carry):
        for level in range(LEVELS):
            pieces = []
            for part in range(2):
                rest = image[y, level, part]
                own = []
                for index in range(SLICES):
                    magic = magics[part][index]
                    piece = (rest + magic) - magic
                    rest = rest - piece
                    own.append(piece)
                pieces.append(own)
            for index in range(SLICES):
                both = jnp.concatenate([pieces[0][index], pieces[1][index]], axis=0)
                slices[y, pl.ds(PROBES * index, PROBES), pl.ds(LANES * level, LANES)] = both.astype(jnp.bfloat16)
        return carry

    lax.fori_loop(0, ROWS, slice_row, 0)

    width = PROBES * SLICES
    high = jnp.zeros((width, width), F32)
    low = jnp.zeros((width, width), F32)
    for pair in range(ROWS // 2):
        block = jnp.concatenate([slices[2 * pair], slices[2 * pair + 1]], axis=1)
        product = lax.dot_general(block, block, (((1,), (1,)), ((), ())), preferred_element_type=F32)
        high, error = two_sum(high, product)
        low = low + error

    def fold(high, low, blocks):
        total_high, total_low = None, None
        for block_high, block_low in blocks(high, low):
            if total_high is None:
                total_high, total_low = block_high, block_low
            else:
                total_high, error = two_sum(total_high, block_high)
                total_low = total_low + block_low + error
        return total_high, total_low

    def row_blocks(high, low):
        for index in range(SLICES):
            rows = slice(PROBES * index, PROBES * (index + 1))
            yield high[rows], low[rows]

    def lane_blocks(high, low):
        for index in range(SLICES):
            yield roll_lanes(high, -PROBES * index), roll_lanes(low, -PROBES * index)

    high, low = fold(high, low, row_blocks)
    rest = jnp.zeros((PROBES, LANES - width), F32)
    high, low = jnp.concatenate([high, rest], axis=1), jnp.concatenate([low, rest], axis=1)
    high, low = fold(high, low, lane_blocks)
    high, low = two_sum(high, low)

    wide = lax.broadcasted_iota(jnp.int32, (PROBES, LANES), 1)
    both = jnp.where(wide < PROBES, high, roll_lanes(low, PROBES))
    packed = both[0:8]
    for index in range(1, 4):
        value = both[8 * (index // 2) : 8 * (index // 2) + 8]
        if index % 2:
            value = pltpu.roll(value, 4, 0)
        packed = jnp.where(lanes // 32 == index, roll_lanes(value, 32 * index), packed)
    message[...] = jnp.broadcast_to(packed[None, 0:4], message.shape)


def split(a):
    scaled = a * 4097.0
    high = scaled - (scaled - a)
    return high, a - high


def product_error(a, b, product):
    a_high, a_low = a
    b_high, b_low = b
    return ((a_high * b_high - product) + a_high * b_low + a_low * b_high) + a_low * b_low


def factor_kernel(count, received, image, basis, factor):
    lanes = lane_ids()
    upper_half = lax.broadcasted_iota(jnp.int32, (8, LANES), 0) < 4
    zero = jnp.zeros((8, LANES), F32)
    chains = 4

    def add(index, carry):
        sums, errors = carry
        new_sums, new_errors = [], []
        for chain in range(chains):
            total, error = two_sum(sums[chain], received[index * chains + chain])
            new_sums.append(total)
            new_errors.append(errors[chain] + error)
        return tuple(new_sums), tuple(new_errors)

    sums, errors = lax.fori_loop(0, received.shape[0] // chains, add, ((zero,) * chains, (zero,) * chains), unroll=4)
    total, rest = sums[0], errors[0]
    for chain in range(1, chains):
        total, error = two_sum(total, sums[chain])
        rest = rest + errors[chain] + error
    total, error = two_sum(total, pltpu.roll(total, 4, 0))
    rest = rest + pltpu.roll(rest, 4, 0) + error
    rest = rest + roll_lanes(total, -PROBES)

    def unpack(value):
        low = jnp.where(upper_half, value, roll_lanes(value, -32))
        high = jnp.where(upper_half, roll_lanes(value, -64), roll_lanes(value, -96))
        return jnp.concatenate([low, high], axis=0)

    high, low = two_sum(unpack(total), unpack(rest))

    shape = (PROBES, LANES)
    wide = lax.broadcasted_iota(jnp.int32, shape, 1)
    rows = lax.broadcasted_iota(jnp.int32, shape, 0)
    high = jnp.where(wide < PROBES, high, jnp.where(wide == rows + PROBES, 1.0, 0.0))
    low = jnp.where(wide < PROBES, low, 0.0)
    for step in range(PROBES - 1):
        row_high = jnp.broadcast_to(high[step : step + 1], shape)
        row_low = jnp.broadcast_to(low[step : step + 1], shape)
        column_high = jnp.broadcast_to(high[:, step : step + 1], shape)
        column_low = jnp.broadcast_to(low[:, step : step + 1], shape)
        pivot_high = jnp.broadcast_to(row_high[:, step : step + 1], shape)
        pivot_low = jnp.broadcast_to(row_low[:, step : step + 1], shape)
        inverse = 1.0 / pivot_high
        ratio = jnp.where(rows > step, column_high * inverse, 0.0)
        ratio_parts = split(ratio)
        taken = ratio * pivot_high
        remainder = ((column_high - taken) - product_error(ratio_parts, split(pivot_high), taken)) + (
            column_low - ratio * pivot_low
        )
        ratio_low = jnp.where(rows > step, remainder * inverse, 0.0)
        taken = ratio * row_high
        taken_error = product_error(ratio_parts, split(row_high), taken)
        high, error = two_sum(high, -taken)
        low = low + error - taken_error - (ratio * row_low + ratio_low * row_high)
        high, low = two_sum(high, low)

    diagonal = jnp.sum(jnp.where(wide == rows, high, 0.0), axis=1, keepdims=True)
    root = jnp.broadcast_to(jnp.sqrt(diagonal), shape)
    size = math.sqrt(count)
    upper = high / root
    factor[...] = jnp.where(wide >= rows, upper * (1.0 / size), 0.0)[:, :PROBES]
    inverse = upper * size
    columns = [
        jnp.broadcast_to(inverse[:, PROBES + index : PROBES + index + 1], shape) for index in range(PROBES)
    ]

    def row(y, carry):
        for level in range(LEVELS):
            outs = [None, None]
            for index in range(PROBES):
                value = image[y, level, index // 8, pl.ds(index % 8, 1), :]
                for part in range(index // 8, 2):
                    term = columns[index][8 * part : 8 * part + 8] * value
                    outs[part] = term if outs[part] is None else outs[part] + term
            for part in range(2):
                basis[level, pl.ds(part * 8 * ROWS + y, 8, stride=ROWS), :] = outs[part]
        return carry

    lax.fori_loop(0, ROWS, row, 0)


def call(kernel, outs, scratch=()):
    vmem = pl.BlockSpec(memory_space=pltpu.VMEM)

    def run(*operands):
        return pl.pallas_call(
            kernel,
            out_shape=[jax.ShapeDtypeStruct(shape, F32) for shape in outs],
            in_specs=[vmem] * len(operands),
            out_specs=[vmem] * len(outs),
            scratch_shapes=list(scratch),
            compiler_params=pltpu.CompilerParams(vmem_limit_bytes=40 << 20),
        )(*operands)

    return run


def body(probes, winds, diffusivity, mixing, prior_scale, obs_weight):
    tile = (8, LANES)
    size_x, size_y = lax.axis_size("gx"), lax.axis_size("gy")
    devices = size_x * size_y
    count = LEVELS * ROWS * LANES * devices

    def shift(value, axis, step):
        number = lax.axis_size(axis)
        pairs = [(i, i + step) for i in range(number) if 0 <= i + step < number]
        return lax.ppermute(value, axis, pairs)

    flat = probes.reshape(LEVELS, PROBES * ROWS, LANES)
    source, east, west = call(
        pack_kernel, [(ROWS, LEVELS, 2) + tile, (X_PARTS,) + tile, (X_PARTS,) + tile]
    )(flat, winds, diffusivity, mixing, prior_scale, obs_weight)
    from_west = shift(east, "gx", 1)
    from_east = shift(west, "gx", -1)
    halo, north, south = call(
        merge_kernel, [(X_PARTS,) + tile, (Y_PARTS,) + tile, (Y_PARTS,) + tile]
    )(from_west, from_east, source, winds, diffusivity, mixing, obs_weight)
    from_south = shift(north, "gy", 1)
    from_north = shift(south, "gy", -1)
    field = (EXT, LEVELS, 3) + tile
    image, message = call(
        stencil_kernel,
        [(ROWS, LEVELS, 2) + tile, (devices, 4, LANES)],
        [
            pltpu.VMEM(field, F32),
            pltpu.VMEM(field, F32),
            pltpu.VMEM(field, F32),
            pltpu.VMEM((STEPS - 1,) + field, F32),
            pltpu.VMEM((2, DERIVED, EXT, LANES), F32),
            pltpu.VMEM((ROWS, PROBES * SLICES, LEVELS * LANES), jnp.bfloat16),
        ],
    )(source, halo, winds, diffusivity, mixing, prior_scale, obs_weight, from_south, from_north)
    received = lax.all_to_all(message, ("gx", "gy"), 0, 0)
    received = received.reshape((devices // 2,) + tile)
    basis, factor = call(
        lambda *refs: factor_kernel(count, *refs),
        [(LEVELS, PROBES * ROWS, LANES), (PROBES, PROBES)],
    )(received, image)
    return basis.reshape(probes.shape), factor


def solution(mesh):
    placed = (
        P(None, None, "gy", "gx"),
        P(None, None, "gy", "gx"),
        P(None, "gy", "gx"),
        P("gy", "gx"),
        P(None, "gy", "gx"),
        P(None, "gy", "gx"),
    )
    return jax.shard_map(
        body,
        mesh=mesh,
        in_specs=placed,
        out_specs=(P(None, None, "gy", "gx"), P()),
        check_vma=False,
    )
```

time: 1070 us -> 95.7 us (0.09)
  other arithmetic: 599 us -> 0 us
  blocking collectives: 152 us -> 35.4 us
  starting transfers between devices: 121 us -> 12.5 us
  waiting for transfers between devices: 103 us -> 11.1 us
  local copies, waits for them, and re-layouts: 61.3 us -> 4.85 us
  Pallas kernels: 0 us -> 30.6 us
  between operations: 23.4 us -> 0.7 us
    another operation x3 -> x0, other arithmetic: 154 us -> none  [the longest x2 154 us: upper_inverse(): return jnp.stack(solved)]
    psum x2 -> x0, blocking collectives: 152 us -> none  [gram_sum(): return lax.psum(local, ('gx', 'gy'))]
    sub x30 -> x0, other arithmetic: 149 us -> none  [upper_factor(): residual_row = residual_row - earlier[index] * earlier]
    select_n x32 -> x0, other arithmetic: 148 us -> none  [upper_factor(): jnp.where(positions >= index, residual_row / pivot, jnp.zeros_like(residu...]
    div x4 -> x0, other arithmetic: 131 us -> none  [the longest x2 131 us: upper_inverse(): solved[index] = row_value / upper[index, index]]
    ppermute x36 -> x4, starting transfers between devices: 121 us -> 12.5 us  [shift(): return lax.ppermute(value, axis, pairs)]
    ppermute x36 -> x4, waiting for transfers between devices: 103 us -> 11.1 us  [shift(): return lax.ppermute(value, axis, pairs)]
    slice x114 -> x0, local copies, waits for them, and re-layouts: 60.1 us -> none  [the longest x32 19.5 us: upper_factor(): pivot = jnp.sqrt(residual_row[index])]
  transfers between devices with their start and end apart: 36 -> 4, of which waited for: 23 -> 4; matrix products, arithmetic and copies ran while one was open for 0% -> 0% of each run, Pallas kernels for 0% -> 0%
where the time goes in v1:
time: 95.7 us; the launch traced here: 95.2 us
  blocking collectives  35.4 us (37%)
  Pallas kernels  30.6 us (32%)
  starting transfers between devices  12.5 us (13%)
  waiting for transfers between devices  11.1 us (12%)
  local copies, waits for them, and re-layouts  4.85 us (5%)
    all_to_all x1, blocking collectives, body(): received = lax.all_to_all(message, ('gx', 'gy'), 0, 0)  35.4 us
    pallas_call x4, Pallas kernels, run(): pl.pallas_call(kernel, out_shape=[jax.ShapeDtypeStruct(shape, F32) for sh...  30.6 us
    ppermute x4, starting transfers between devices, shift(): return lax.ppermute(value, axis, pairs)  12.5 us
    ppermute x4, waiting for transfers between devices, shift(): return lax.ppermute(value, axis, pairs)  11.1 us
    unnamed x14, local copies, waits for them, and re-layouts  4.85 us
  transfers between devices with their start and end apart: 4, of which 4 were waited for; matrix products, arithmetic and copies ran while one was open for 0% of the time, Pallas kernels for 0%

profile of v1, /device:TPU:1, one launch (start us, length us, event | category | flops | bytes accessed | tf_op | source)
XLA Modules:
  0.0 95.2 jit_solution(15329898630836993783)
XLA Ops:
  0.6 0.0 copy-start
  0.6 0.8 copy-done
  1.5 0.0 copy-start.1
  1.5 1.0 %copy-done.1 = f32[4,16,16,128]{3,2,1,0:T(8,128)S(1)} copy-done((f32[4,16,16,128]{3,2,1,0:T(8,128)S(1)}, f32[4,16,16,128]{3,2,1,0:T(8,128)}, u32[]{:S(2)}) %copy-start.1) | copy-done | bytes 524312
  2.5 0.0 copy-start.2
  2.5 0.8 copy-done.2
  3.3 0.0 copy-start.3
  3.3 0.8 copy-done.3
  4.0 0.0 copy-start.5
  4.0 0.8 copy-done.5
  4.8 0.0 copy-start.6
  4.8 0.7 copy-done.6
  5.5 0.0 copy-start.4
  5.5 1.0 %shard_map.77 = (f32[16,4,2,8,128]{4,3,2,1,0:T(8,128)S(1)}, f32[22,8,128]{2,1,0:T(8,128)S(1)}, f32[22,8,128]{2,1,0:T(8,128)S(1)}) custom-call(f32[4,256,128]{2,1,0:T(8,128)S(1)} %bitcast.4, f32[2,4,16,128]{3,2,1,0:T(8,128)S(1)} %copy-done, f32[4,16,128]{2,1,0:T(8,128)S(1)} %copy-done.2, f32[16,128]{1,0:T(8,128)S(1)} %copy-done.6, ...), custom_call_target="tpu_custom_call" | custom-call | tf_op jit(solution)/shard_map/pallas_call | solution.py:426
  6.5 4.4 %collective-permute-start = (f32[22,8,128]{2,1,0:T(8,128)S(1)}, f32[22,8,128]{2,1,0:T(8,128)S(1)}, u32[]{:S(2)}, u32[]{:S(2)}) collective-permute-start(f32[22,8,128]{2,1,0:T(8,128)S(1)} %get-tuple-element.13), channel_id=1, source_target_pairs={{0,32},{32,64},{64,96},{96,128},{128,160},{160,192},{192,224},{1,3... | collective-permute-start | bytes 270344 | tf_op jit(solution)/shard_map/ppermute | solution.py:447
  10.8 1.3 %collective-permute-start.1 = (f32[22,8,128]{2,1,0:T(8,128)S(1)}, f32[22,8,128]{2,1,0:T(8,128)S(1)}, u32[]{:S(2)}, u32[]{:S(2)}) collective-permute-start(f32[22,8,128]{2,1,0:T(8,128)S(1)} %get-tuple-element.14), channel_id=1, source_target_pairs={{32,0},{64,32},{96,64},{128,96},{160,128},{192,160},{224,192},{33,... | collective-permute-start | bytes 270344 | tf_op jit(solution)/shard_map/ppermute | solution.py:447
  12.1 0.2 collective-permute-done.from_west
  12.4 3.9 %collective-permute-done.1.from_east = f32[22,8,128]{2,1,0:T(8,128)S(1)} collective-permute-done((f32[22,8,128]{2,1,0:T(8,128)S(1)}, f32[22,8,128]{2,1,0:T(8,128)S(1)}, u32[]{:S(2)}, u32[]{:S(2)}) %collective-permute-start.1) | collective-permute-done | bytes 90144 | tf_op jit(solution)/shard_map/ppermute | solution.py:447
  16.3 0.0 copy-done.4
  16.3 0.1 shard_map.78
  16.4 4.9 %collective-permute-start.2 = (f32[92,8,128]{2,1,0:T(8,128)S(1)}, f32[92,8,128]{2,1,0:T(8,128)S(1)}, u32[]{:S(2)}, u32[]{:S(2)}) collective-permute-start(f32[92,8,128]{2,1,0:T(8,128)S(1)} %get-tuple-element.16), channel_id=1, source_target_pairs={{0,1},{1,2},{2,3},{3,4},{4,5},{5,6},{6,7},{7,8},{8,9},{9,10},{10,1... | collective-permute-start | bytes 1130504 | tf_op jit(solution)/shard_map/ppermute | solution.py:447
  21.3 1.9 %collective-permute-start.3 = (f32[92,8,128]{2,1,0:T(8,128)S(1)}, f32[92,8,128]{2,1,0:T(8,128)S(1)}, u32[]{:S(2)}, u32[]{:S(2)}) collective-permute-start(f32[92,8,128]{2,1,0:T(8,128)S(1)} %get-tuple-element.17), channel_id=1, source_target_pairs={{1,0},{2,1},{3,2},{4,3},{5,4},{6,5},{7,6},{8,7},{9,8},{10,9},{11,1... | collective-permute-start | bytes 1130504 | tf_op jit(solution)/shard_map/ppermute | solution.py:447
  23.2 2.6 %collective-permute-done.2.from_south = f32[92,8,128]{2,1,0:T(8,128)S(1)} collective-permute-done((f32[92,8,128]{2,1,0:T(8,128)S(1)}, f32[92,8,128]{2,1,0:T(8,128)S(1)}, u32[]{:S(2)}, u32[]{:S(2)}) %collective-permute-start.2) | collective-permute-done | bytes 376864 | tf_op jit(solution)/shard_map/ppermute | solution.py:447
  25.8 4.4 %collective-permute-done.3.from_north = f32[92,8,128]{2,1,0:T(8,128)S(1)} collective-permute-done((f32[92,8,128]{2,1,0:T(8,128)S(1)}, f32[92,8,128]{2,1,0:T(8,128)S(1)}, u32[]{:S(2)}, u32[]{:S(2)}) %collective-permute-start.3) | collective-permute-done | bytes 376864 | tf_op jit(solution)/shard_map/ppermute | solution.py:447
  30.2 24.5 %shard_map.79 = (f32[16,4,2,8,128]{4,3,2,1,0:T(8,128)S(1)}, f32[256,4,128]{2,1,0:T(4,128)S(1)}) custom-call(f32[16,4,2,8,128]{4,3,2,1,0:T(8,128)S(1)} %get-tuple-element.12.source, f32[22,8,128]{2,1,0:T(8,128)S(1)} %get-tuple-element.15.halo, f32[2,4,16,128]{3,2,1,0:T(8,128)S(1)} %copy-done, f32[4,16,128]{2,1,0:T(8,128)S(1)} %copy-done.2, ...), custom_call_target="tpu_custom_call" | custom-call | tf_op jit(solution)/shard_map/pallas_call | solution.py:426
  54.8 35.4 %all_to_all.5 = f32[256,4,128]{2,1,0:T(4,128)S(1)} all-to-all(f32[256,4,128]{2,1,0:T(4,128)S(1)} %get-tuple-element.18), channel_id=1, replica_groups=mesh['gx'=8,'gy'=32] {'gx','gy'}, dimensions={0} | all-to-all | bytes 1048576 | tf_op jit(solution)/shard_map/all_to_all | solution.py:473
  90.1 5.1 %shard_map.80 = (f32[4,256,128]{2,1,0:T(8,128)}, f32[16,16]{1,0:T(8,128)}) custom-call(f32[128,8,128]{2,1,0:T(8,128)S(1)} %bitcast.3, f32[16,4,2,8,128]{4,3,2,1,0:T(8,128)S(1)} %get-tuple-element.19.refs_1_), custom_call_target="tpu_custom_call" | custom-call | tf_op jit(solution)/shard_map/pallas_call | solution.py:426
Async XLA Ops:
  0.6 0.8 copy-start
  1.5 1.0 %copy-start.1 = (f32[4,16,16,128]{3,2,1,0:T(8,128)S(1)}, f32[4,16,16,128]{3,2,1,0:T(8,128)}, u32[]{:S(2)}) copy-start(f32[4,16,16,128]{3,2,1,0:T(8,128)} %param.6) | copy-start | bytes 1572868
  2.5 0.8 copy-start.2
  3.3 0.8 copy-start.3
  4.0 0.8 copy-start.5
  4.8 0.7 copy-start.6
  5.5 10.8 %copy-start.4 = (f32[4,16,128]{2,1,0:T(8,128)S(1)}, f32[4,16,128]{2,1,0:T(8,128)}, u32[]{:S(2)}) copy-start(f32[4,16,128]{2,1,0:T(8,128)} %obs.5) | copy-start | bytes 98308
  6.5 5.9 %collective-permute-start = (f32[22,8,128]{2,1,0:T(8,128)S(1)}, f32[22,8,128]{2,1,0:T(8,128)S(1)}, u32[]{:S(2)}, u32[]{:S(2)}) collective-permute-start(f32[22,8,128]{2,1,0:T(8,128)S(1)} %get-tuple-element.13), channel_id=1, source_target_pairs={{0,32},{32,64},{64,96},{96,128},{128,160},{160,192},{192,224},{1,3... | collective-permute-start | bytes 270344 | tf_op jit(solution)/shard_map/ppermute | solution.py:447
  10.8 5.5 %collective-permute-start.1 = (f32[22,8,128]{2,1,0:T(8,128)S(1)}, f32[22,8,128]{2,1,0:T(8,128)S(1)}, u32[]{:S(2)}, u32[]{:S(2)}) collective-permute-start(f32[22,8,128]{2,1,0:T(8,128)S(1)} %get-tuple-element.14), channel_id=1, source_target_pairs={{32,0},{64,32},{96,64},{128,96},{160,128},{192,160},{224,192},{33,... | collective-permute-start | bytes 270344 | tf_op jit(solution)/shard_map/ppermute | solution.py:447
  16.4 9.5 %collective-permute-start.2 = (f32[92,8,128]{2,1,0:T(8,128)S(1)}, f32[92,8,128]{2,1,0:T(8,128)S(1)}, u32[]{:S(2)}, u32[]{:S(2)}) collective-permute-start(f32[92,8,128]{2,1,0:T(8,128)S(1)} %get-tuple-element.16), channel_id=1, source_target_pairs={{0,1},{1,2},{2,3},{3,4},{4,5},{5,6},{6,7},{7,8},{8,9},{9,10},{10,1... | collective-permute-start | bytes 1130504 | tf_op jit(solution)/shard_map/ppermute | solution.py:447
  21.3 8.9 %collective-permute-start.3 = (f32[92,8,128]{2,1,0:T(8,128)S(1)}, f32[92,8,128]{2,1,0:T(8,128)S(1)}, u32[]{:S(2)}, u32[]{:S(2)}) collective-permute-start(f32[92,8,128]{2,1,0:T(8,128)S(1)} %get-tuple-element.17), channel_id=1, source_target_pairs={{1,0},{2,1},{3,2},{4,3},{5,4},{6,5},{7,6},{8,7},{9,8},{10,9},{11,1... | collective-permute-start | bytes 1130504 | tf_op jit(solution)/shard_map/ppermute | solution.py:447

commit v2 on v1

--- a/solution.py
+++ b/solution.py
@@ -32,20 +32,23 @@
     return value if shift == 0 else pltpu.roll(value, shift, value.ndim - 1)
 
 
-def raw_field(refs, field, rows):
-    diffusivity, winds, obs, mixing = refs
-    if field < 4:
-        return diffusivity[field, rows, :]
-    if field < 8:
-        return winds[0, field - 4, rows, :]
-    if field < 12:
-        return winds[1, field - 8, rows, :]
-    if field < 16:
-        return obs[field - 12, rows, :]
-    return mixing[rows, :]
-
-
-def pack_kernel(probes, winds, diffusivity, mixing, prior, obs, source, east, west):
+def pack_kernel(
+    probes_in, winds_in, diffusivity_in, mixing_in, prior_in, obs_in,
+    source, east, west, fields, prior, probes, sems,
+):
+    coef_copies = [
+        pltpu.make_async_copy(diffusivity_in, fields.at[pl.ds(0, 4)], sems.at[0]),
+        pltpu.make_async_copy(winds_in.at[0], fields.at[pl.ds(4, 4)], sems.at[1]),
+        pltpu.make_async_copy(winds_in.at[1], fields.at[pl.ds(8, 4)], sems.at[2]),
+        pltpu.make_async_copy(obs_in, fields.at[pl.ds(12, 4)], sems.at[3]),
+        pltpu.make_async_copy(mixing_in, fields.at[16], sems.at[4]),
+    ]
+    source_copies = [
+        pltpu.make_async_copy(probes_in, probes, sems.at[5]),
+        pltpu.make_async_copy(prior_in, prior, sems.at[6]),
+    ]
+    for copy in source_copies + coef_copies:
+        copy.start()
     lanes = lane_ids()
     half = lanes // 8
 
@@ -68,23 +71,25 @@
         east[y], west[y] = held
         return carry
 
-    lax.fori_loop(0, ROWS, row, 0, unroll=2)
-    refs = (diffusivity, winds, obs, mixing)
+    for copy in coef_copies:
+        copy.wait()
     for group in range(GROUPS):
         for tile in range(2):
             held = (zero, zero)
             for slot in range(8):
                 field = 8 * group + slot
                 if field < FIELDS:
-                    held = put(held, raw_field(refs, field, pl.ds(8 * tile, 8)), slot)
+                    held = put(held, fields[field, pl.ds(8 * tile, 8), :], slot)
             east[ROWS + 2 * group + tile], west[ROWS + 2 * group + tile] = held
-
-
-def merge_kernel(from_west, from_east, source, winds, diffusivity, mixing, obs, halo, north, south):
+    for copy in source_copies:
+        copy.wait()
+    lax.fori_loop(0, ROWS, row, 0, unroll=True)
+
+
+def merge_kernel(from_west, from_east, source, fields, halo, north, south):
     inner = lane_ids() % 16 < 8
     for index in range(X_PARTS):
         halo[index] = jnp.where(inner, from_east[index], from_west[index])
-    refs = (diffusivity, winds, obs, mixing)
     for tile, out in ((0, south), (1, north)):
         for y in range(8):
             for level in range(LEVELS):
@@ -92,7 +97,7 @@
                     out[(y * LEVELS + level) * 2 + part] = source[8 * tile + y, level, part]
             out[Y_HALO + y] = jnp.where(inner, from_east[8 * tile + y], from_west[8 * tile + y])
         for field in range(FIELDS):
-            out[Y_COEF + field] = raw_field(refs, field, pl.ds(8 * tile, 8))
+            out[Y_COEF + field] = fields[field, pl.ds(8 * tile, 8), :]
         for group in range(GROUPS):
             index = ROWS + 2 * group + tile
             out[Y_COEF_HALO + group] = jnp.where(inner, from_east[index], from_west[index])
@@ -114,15 +119,14 @@
 
 
 def stencil_kernel(
-    source, halo, winds, diffusivity, mixing, prior, obs, from_south, from_north,
+    source, halo, fields, prior, from_south, from_north,
     image, message, start, first, second, adjoints, coefs, slices,
 ):
     lanes = lane_ids()
-    refs = (diffusivity, winds, obs, mixing)
 
     for tile in range(4):
         if tile in (1, 2):
-            main = [raw_field(refs, field, pl.ds(8 * (tile - 1), 8)) for field in range(FIELDS)]
+            main = [fields[field, pl.ds(8 * (tile - 1), 8), :] for field in range(FIELDS)]
             packed = [halo[ROWS + 2 * group + tile - 1] for group in range(GROUPS)]
         else:
             ref = from_south if tile == 0 else from_north
@@ -160,9 +164,9 @@
     def beside(ref):
         return (lambda y, level, part: ref[(y * LEVELS + level) * 2 + part]), (lambda y: ref[Y_HALO + y])
 
-    lax.fori_loop(0, HALO, load_rows(*beside(from_south), 0), 0)
-    lax.fori_loop(0, ROWS, load_rows(lambda y, level, part: source[y, level, part], lambda y: halo[y], HALO), 0)
-    lax.fori_loop(0, HALO, load_rows(*beside(from_north), HALO + ROWS), 0)
+    lax.fori_loop(0, HALO, load_rows(*beside(from_south), 0), 0, unroll=True)
+    lax.fori_loop(0, ROWS, load_rows(lambda y, level, part: source[y, level, part], lambda y: halo[y], HALO), 0, unroll=True)
+    lax.fori_loop(0, HALO, load_rows(*beside(from_north), HALO + ROWS), 0, unroll=True)
 
     def vertical(values, level):
         if level == 0:
@@ -171,80 +175,124 @@
             return values[LEVELS - 2]
         return values[level - 1] + values[level + 1]
 
-    def forward(ref, y, part):
-        kind = part // 2
-        coef = lambda index: coefs[kind, index, pl.ds(y, 1), :]
-        center = [ref[y, level, part] for level in range(LEVELS)]
-        rate = coef(RATE)
-        out = []
-        for level in range(LEVELS):
-            value = center[level]
-            out.append(
-                coef(CENTER + level) * value
-                + coef(EAST + level) * roll_lanes(value, -1)
-                + coef(WEST + level) * roll_lanes(value, 1)
-                + coef(NORTH + level) * ref[y + 1, level, part]
-                + coef(SOUTH + level) * ref[y - 1, level, part]
-                + rate * vertical(center, level)
-            )
-        return out
-
-    def adjoint(ref, y, part):
-        kind = part // 2
-        coef = lambda index, at: coefs[kind, index, pl.ds(at, 1), :]
-        center = [ref[y, level, part] for level in range(LEVELS)]
-        rate = coef(RATE, y)
-        out = []
-        for level in range(LEVELS):
-            value = center[level]
-            out.append(
-                coef(CENTER + level, y) * value
-                + roll_lanes(coef(WEST + level, y) * value, -1)
-                + roll_lanes(coef(EAST + level, y) * value, 1)
-                + coef(SOUTH + level, y + 1) * ref[y + 1, level, part]
-                + coef(NORTH + level, y - 1) * ref[y - 1, level, part]
-                + rate * vertical(center, level)
-            )
-        return out
-
+    def coefs_at(kind, y):
+        return lambda index: coefs[kind, index, pl.ds(y, 1), :]
+
+    def load(ref, y, parts):
+        return tuple(tuple(ref[y, level, part] for level in range(LEVELS)) for part in parts)
+
+    def forward(ref, low, high, parts, emit):
+        def row(y, carry):
+            before, center = carry
+            after = load(ref, y + 1, parts)
+            coef = coefs_at(parts[0] // 2, y)
+            rate = coef(RATE)
+            own = [[coef(base + level) for base in (CENTER, EAST, WEST, NORTH, SOUTH)] for level in range(LEVELS)]
+            results = []
+            for index in range(len(parts)):
+                values = []
+                for level in range(LEVELS):
+                    value = center[index][level]
+                    middle, east, west, north, south = own[level]
+                    values.append(
+                        (middle * value + rate * vertical(center[index], level))
+                        + (north * after[index][level] + south * before[index][level])
+                        + (east * roll_lanes(value, -1) + west * roll_lanes(value, 1))
+                    )
+                results.append(values)
+            emit(y, parts, coef, results)
+            return center, after
+
+        lax.fori_loop(low, high, row, (load(ref, low - 1, parts), load(ref, low, parts)), unroll=True)
+
+    def adjoint(ref, low, high, parts, emit, state):
+        def spread(y, pushed):
+            center = load(ref, y, parts)
+            coef = coefs_at(parts[0] // 2, y)
+            rate = coef(RATE)
+            own = [[coef(base + level) for base in (CENTER, EAST, WEST, NORTH)] for level in range(LEVELS)]
+            partial, push = [], []
+            for index in range(len(parts)):
+                values, pushes = [], []
+                for level in range(LEVELS):
+                    value = center[index][level]
+                    middle, east, west, north = own[level]
+                    values.append(
+                        (middle * value + rate * vertical(center[index], level))
+                        + (roll_lanes(west * value, -1) + roll_lanes(east * value, 1))
+                        + pushed[index][level]
+                    )
+                    pushes.append(north * value)
+                partial.append(tuple(values))
+                push.append(tuple(pushes))
+            return center, tuple(partial), tuple(push)
+
+        def pull(y, center, partial):
+            coef = coefs_at(parts[0] // 2, y)
+            south = [coef(SOUTH + level) for level in range(LEVELS)]
+            return [
+                [partial[index][level] + south[level] * center[index][level] for level in range(LEVELS)]
+                for index in range(len(parts))
+            ]
+
+        below = load(ref, low - 1, parts)
+        coef = coefs_at(parts[0] // 2, low - 1)
+        north = [coef(NORTH + level) for level in range(LEVELS)]
+        push = tuple(tuple(north[level] * values[level] for level in range(LEVELS)) for values in below)
+        center, partial, push = spread(low, push)
+
+        def row(y, carry):
+            partial, push, state = carry
+            center, new_partial, push = spread(y + 1, push)
+            state = emit(y, parts, pull(y + 1, center, partial), state)
+            return new_partial, push, state
+
+        partial, push, state = lax.fori_loop(low, high - 1, row, (partial, push, state), unroll=True)
+        return emit(high - 1, parts, pull(high, load(ref, high, parts), partial), state)
+
+    groups = ((2,), (0, 1))
     held = [start, first, second, first, second]
     for step in range(1, STEPS + 1):
-        def row(y, carry, step=step):
-            for part in range(3):
-                values = forward(held[step - 1], y, part)
-                for level in range(LEVELS):
+        def emit(y, parts, coef, results, step=step):
+            for level in range(LEVELS):
+                for index, part in enumerate(parts):
+                    value = results[index][level]
                     if step < STEPS:
-                        value = values[level] + start[y, level, part]
+                        value = value + start[y, level, part]
                     else:
-                        value = values[level] * coefs[part // 2, OBS + level, pl.ds(y, 1), :]
+                        value = value * coef(OBS + level)
                     held[step][y, level, part] = value
-            return carry
-        lax.fori_loop(step, EXT - step, row, 0)
+
+        for parts in groups:
+            forward(held[step - 1], step, EXT - step, parts, emit)
 
     held = [second] + [adjoints.at[index] for index in range(STEPS - 1)]
     for step in range(1, STEPS):
-        def row(y, carry, step=step):
-            for part in range(3):
-                values = adjoint(held[step - 1], y, part)
+        def emit(y, parts, results, state, step=step):
+            for index, part in enumerate(parts):
                 for level in range(LEVELS):
-                    held[step][y, level, part] = values[level]
-            return carry
-        lax.fori_loop(STEPS + step, EXT - STEPS - step, row, 0)
-
-    def last_row(y, most):
-        totals = []
-        for part in range(3):
-            values = adjoint(held[STEPS - 1], y, part)
-            totals.append([
-                values[level] + held[1][y, level, part] + held[2][y, level, part] + held[3][y, level, part]
-                for level in range(LEVELS)
-            ])
+                    held[step][y, level, part] = results[index][level]
+            return state
+
+        for parts in groups:
+            adjoint(held[step - 1], STEPS + step, EXT - STEPS - step, parts, emit, ())
+
+    def total_of(y, part, level, value):
+        return (held[1][y, level, part] + held[2][y, level, part]) + (held[3][y, level, part] + value)
+
+    def emit_strip(y, parts, results, state):
+        for level in range(LEVELS):
+            first[y, level, 2] = total_of(y, 2, level, results[0][level])
+        return state
+
+    def emit_image(y, parts, results, most):
         most = list(most)
         for level in range(LEVELS):
             scale = prior[level, pl.ds(y - HALO, 1), :]
-            strip = totals[2][level]
+            strip = first[y, level, 2]
             for part in range(2):
-                value = jnp.where(lanes < HALO, roll_lanes(strip, -40 - 64 * part), totals[part][level])
+                value = total_of(y, part, level, results[part][level])
+                value = jnp.where(lanes < HALO, roll_lanes(strip, -40 - 64 * part), value)
                 value = jnp.where(lanes >= LANES - HALO, roll_lanes(strip, 104 - 64 * part), value)
                 value = value * scale
                 image[y - HALO, level, part] = value
@@ -252,7 +300,8 @@
         return tuple(most)
 
     zero = jnp.zeros((8, LANES), F32)
-    most = lax.fori_loop(HALO, HALO + ROWS, last_row, (zero, zero))
+    adjoint(held[STEPS - 1], HALO, HALO + ROWS, (2,), emit_strip, ())
+    most = adjoint(held[STEPS - 1], HALO, HALO + ROWS, (0, 1), emit_image, (zero, zero))
 
     magics = []
     for part in range(2):
@@ -278,7 +327,7 @@
                 slices[y, pl.ds(PROBES * index, PROBES), pl.ds(LANES * level, LANES)] = both.astype(jnp.bfloat16)
         return carry
 
-    lax.fori_loop(0, ROWS, slice_row, 0)
+    lax.fori_loop(0, ROWS, slice_row, 0, unroll=True)
 
     width = PROBES * SLICES
     high = jnp.zeros((width, width), F32)
@@ -337,28 +386,31 @@
     return ((a_high * b_high - product) + a_high * b_low + a_low * b_high) + a_low * b_low
 
 
-def factor_kernel(count, received, image, basis, factor):
-    lanes = lane_ids()
-    upper_half = lax.broadcasted_iota(jnp.int32, (8, LANES), 0) < 4
+def summed(received):
     zero = jnp.zeros((8, LANES), F32)
     chains = 4
-
-    def add(index, carry):
-        sums, errors = carry
-        new_sums, new_errors = [], []
-        for chain in range(chains):
-            total, error = two_sum(sums[chain], received[index * chains + chain])
-            new_sums.append(total)
-            new_errors.append(errors[chain] + error)
-        return tuple(new_sums), tuple(new_errors)
-
-    sums, errors = lax.fori_loop(0, received.shape[0] // chains, add, ((zero,) * chains, (zero,) * chains), unroll=4)
+    sums, errors = [zero] * chains, [zero] * chains
+    for index in range(received.shape[0]):
+        chain = index % chains
+        sums[chain], error = two_sum(sums[chain], received[index])
+        errors[chain] = errors[chain] + error
     total, rest = sums[0], errors[0]
     for chain in range(1, chains):
         total, error = two_sum(total, sums[chain])
         rest = rest + errors[chain] + error
     total, error = two_sum(total, pltpu.roll(total, 4, 0))
-    rest = rest + pltpu.roll(rest, 4, 0) + error
+    return total, rest + pltpu.roll(rest, 4, 0) + error
+
+
+def sum_kernel(received, message):
+    total, rest = summed(received)
+    total = total + jnp.where(lane_ids() % 32 < PROBES, 0.0, roll_lanes(rest, PROBES))
+    message[...] = jnp.broadcast_to(total[None, 0:4], message.shape)
+
+
+def factor_kernel(count, received, image, basis, factor):
+    upper_half = lax.broadcasted_iota(jnp.int32, (8, LANES), 0) < 4
+    total, rest = summed(received)
     rest = rest + roll_lanes(total, -PROBES)
 
     def unpack(value):
@@ -416,20 +468,20 @@
                 basis[level, pl.ds(part * 8 * ROWS + y, 8, stride=ROWS), :] = outs[part]
         return carry
 
-    lax.fori_loop(0, ROWS, row, 0)
-
-
-def call(kernel, outs, scratch=()):
+    lax.fori_loop(0, ROWS, row, 0, unroll=True)
+
+
+def call(kernel, outs, scratch=(), inputs=pltpu.VMEM, grant=40):
     vmem = pl.BlockSpec(memory_space=pltpu.VMEM)
 
     def run(*operands):
         return pl.pallas_call(
             kernel,
             out_shape=[jax.ShapeDtypeStruct(shape, F32) for shape in outs],
-            in_specs=[vmem] * len(operands),
+            in_specs=[pl.BlockSpec(memory_space=inputs)] * len(operands),
             out_specs=[vmem] * len(outs),
             scratch_shapes=list(scratch),
-            compiler_params=pltpu.CompilerParams(vmem_limit_bytes=40 << 20),
+            compiler_params=pltpu.CompilerParams(vmem_limit_bytes=grant << 20),
         )(*operands)
 
     return run
@@ -438,29 +490,35 @@
 def body(probes, winds, diffusivity, mixing, prior_scale, obs_weight):
     tile = (8, LANES)
     size_x, size_y = lax.axis_size("gx"), lax.axis_size("gy")
-    devices = size_x * size_y
-    count = LEVELS * ROWS * LANES * devices
+    count = LEVELS * ROWS * LANES * size_x * size_y
 
     def shift(value, axis, step):
         number = lax.axis_size(axis)
         pairs = [(i, i + step) for i in range(number) if 0 <= i + step < number]
         return lax.ppermute(value, axis, pairs)
 
-    flat = probes.reshape(LEVELS, PROBES * ROWS, LANES)
-    source, east, west = call(
-        pack_kernel, [(ROWS, LEVELS, 2) + tile, (X_PARTS,) + tile, (X_PARTS,) + tile]
-    )(flat, winds, diffusivity, mixing, prior_scale, obs_weight)
+    def exchange(message, axis):
+        received = lax.all_to_all(message, axis, 0, 0)
+        return received.reshape((message.shape[0] // 2,) + tile)
+
+    flat = (LEVELS, PROBES * ROWS, LANES)
+    source, east, west, fields, prior = call(
+        pack_kernel,
+        [(ROWS, LEVELS, 2) + tile, (X_PARTS,) + tile, (X_PARTS,) + tile, (FIELDS, ROWS, LANES), (LEVELS, ROWS, LANES)],
+        [pltpu.VMEM(flat, F32), pltpu.SemaphoreType.DMA((7,))],
+        pltpu.HBM,
+    )(*(pltpu.with_memory_space_constraint(a, pltpu.HBM) for a in (probes.reshape(flat), winds, diffusivity, mixing, prior_scale, obs_weight)))
     from_west = shift(east, "gx", 1)
     from_east = shift(west, "gx", -1)
     halo, north, south = call(
         merge_kernel, [(X_PARTS,) + tile, (Y_PARTS,) + tile, (Y_PARTS,) + tile]
-    )(from_west, from_east, source, winds, diffusivity, mixing, obs_weight)
+    )(from_west, from_east, source, fields)
     from_south = shift(north, "gy", 1)
     from_north = shift(south, "gy", -1)
     field = (EXT, LEVELS, 3) + tile
     image, message = call(
         stencil_kernel,
-        [(ROWS, LEVELS, 2) + tile, (devices, 4, LANES)],
+        [(ROWS, LEVELS, 2) + tile, (size_x, 4, LANES)],
         [
             pltpu.VMEM(field, F32),
             pltpu.VMEM(field, F32),
@@ -469,12 +527,13 @@
             pltpu.VMEM((2, DERIVED, EXT, LANES), F32),
             pltpu.VMEM((ROWS, PROBES * SLICES, LEVELS * LANES), jnp.bfloat16),
         ],
-    )(source, halo, winds, diffusivity, mixing, prior_scale, obs_weight, from_south, from_north)
-    received = lax.all_to_all(message, ("gx", "gy"), 0, 0)
-    received = received.reshape((devices // 2,) + tile)
+    )(source, halo, fields, prior, from_south, from_north)
+    received = exchange(message, "gx")
+    (message,) = call(sum_kernel, [(size_y, 4, LANES)])(received)
+    received = exchange(message, "gy")
     basis, factor = call(
         lambda *refs: factor_kernel(count, *refs),
-        [(LEVELS, PROBES * ROWS, LANES), (PROBES, PROBES)],
+        [flat, (PROBES, PROBES)],
     )(received, image)
     return basis.reshape(probes.shape), factor
 

time: 95.7 us -> 68.1 us (0.71)
  Pallas kernels: 30.6 us -> 13.1 us
  blocking collectives: 35.4 us -> 30.3 us
  local copies, waits for them, and re-layouts: 4.85 us -> 0 us
    pallas_call x4 -> x5, Pallas kernels: 30.6 us -> 13.1 us  [run(): pl.pallas_call(kernel, out_shape=[jax.ShapeDtypeStruct(shape, F32) for sh...]
    all_to_all x1 -> x2, blocking collectives: 35.4 us -> 30.3 us  [exchange(): received = lax.all_to_all(message, axis, 0, 0)]
    unnamed x14 -> x0, local copies, waits for them, and re-layouts: 4.85 us -> none
where the time goes in v2:
time: 68.1 us; the launch traced here: 67.8 us
  blocking collectives  30.3 us (44%)
  Pallas kernels  13.1 us (19%)
  starting transfers between devices  12.5 us (18%)
  waiting for transfers between devices  11.1 us (16%)
    all_to_all x2, blocking collectives, exchange(): received = lax.all_to_all(message, axis, 0, 0)  30.3 us
    pallas_call x5, Pallas kernels, run(): pl.pallas_call(kernel, out_shape=[jax.ShapeDtypeStruct(shape, F32) for sh...  13.1 us
    ppermute x4, starting transfers between devices, shift(): return lax.ppermute(value, axis, pairs)  12.5 us
    ppermute x4, waiting for transfers between devices, shift(): return lax.ppermute(value, axis, pairs)  11.1 us
  transfers between devices with their start and end apart: 4, of which 4 were waited for; matrix products, arithmetic and copies ran while one was open for 0% of the time, Pallas kernels for 0%

profile of v2, /device:TPU:1, one launch (start us, length us, event | category | flops | bytes accessed | tf_op | source)
XLA Modules:
  0.0 67.8 jit_solution(16718814314666491779)
XLA Ops:
  0.6 1.5 %shard_map.77 = (f32[16,4,2,8,128]{4,3,2,1,0:T(8,128)S(1)}, f32[22,8,128]{2,1,0:T(8,128)S(1)}, f32[22,8,128]{2,1,0:T(8,128)S(1)}, f32[17,16,128]{2,1,0:T(8,128)S(1)}, f32[4,16,128]{2,1,0:T(8,128)S(1)}) custom-call(f32[4,256,128]{2,1,0:T(8,128)} %bitcast.6, f32[2,4,16,128]{3,2,1,0:T(8,128)} %winds_in.1, f32[4,16,128]{2,1,0:T(8,128)} %diffusivity_in.1, ...), custom_call_target="tpu_custom_call" | custom-call | tf_op jit(solution)/shard_map/pallas_call | solution.py:478
  2.1 4.4 %collective-permute-start = (f32[22,8,128]{2,1,0:T(8,128)S(1)}, f32[22,8,128]{2,1,0:T(8,128)S(1)}, u32[]{:S(2)}, u32[]{:S(2)}) collective-permute-start(f32[22,8,128]{2,1,0:T(8,128)S(1)} %get-tuple-element.15), channel_id=1, source_target_pairs={{0,32},{32,64},{64,96},{96,128},{128,160},{160,192},{192,224},{1,3... | collective-permute-start | bytes 270344 | tf_op jit(solution)/shard_map/ppermute | solution.py:498
  6.5 1.3 %collective-permute-start.1 = (f32[22,8,128]{2,1,0:T(8,128)S(1)}, f32[22,8,128]{2,1,0:T(8,128)S(1)}, u32[]{:S(2)}, u32[]{:S(2)}) collective-permute-start(f32[22,8,128]{2,1,0:T(8,128)S(1)} %get-tuple-element.16), channel_id=1, source_target_pairs={{32,0},{64,32},{96,64},{128,96},{160,128},{192,160},{224,192},{33,... | collective-permute-start | bytes 270344 | tf_op jit(solution)/shard_map/ppermute | solution.py:498
  7.8 0.2 collective-permute-done.from_west
  8.1 3.9 %collective-permute-done.1.from_east = f32[22,8,128]{2,1,0:T(8,128)S(1)} collective-permute-done((f32[22,8,128]{2,1,0:T(8,128)S(1)}, f32[22,8,128]{2,1,0:T(8,128)S(1)}, u32[]{:S(2)}, u32[]{:S(2)}) %collective-permute-start.1) | collective-permute-done | bytes 90144 | tf_op jit(solution)/shard_map/ppermute | solution.py:498
  12.0 0.1 shard_map.78
  12.0 4.9 %collective-permute-start.2 = (f32[92,8,128]{2,1,0:T(8,128)S(1)}, f32[92,8,128]{2,1,0:T(8,128)S(1)}, u32[]{:S(2)}, u32[]{:S(2)}) collective-permute-start(f32[92,8,128]{2,1,0:T(8,128)S(1)} %get-tuple-element.20), channel_id=1, source_target_pairs={{0,1},{1,2},{2,3},{3,4},{4,5},{5,6},{6,7},{7,8},{8,9},{9,10},{10,1... | collective-permute-start | bytes 1130504 | tf_op jit(solution)/shard_map/ppermute | solution.py:498
  17.0 1.9 %collective-permute-start.3 = (f32[92,8,128]{2,1,0:T(8,128)S(1)}, f32[92,8,128]{2,1,0:T(8,128)S(1)}, u32[]{:S(2)}, u32[]{:S(2)}) collective-permute-start(f32[92,8,128]{2,1,0:T(8,128)S(1)} %get-tuple-element.21), channel_id=1, source_target_pairs={{1,0},{2,1},{3,2},{4,3},{5,4},{6,5},{7,6},{8,7},{9,8},{10,9},{11,1... | collective-permute-start | bytes 1130504 | tf_op jit(solution)/shard_map/ppermute | solution.py:498
  18.9 2.6 %collective-permute-done.2.from_south = f32[92,8,128]{2,1,0:T(8,128)S(1)} collective-permute-done((f32[92,8,128]{2,1,0:T(8,128)S(1)}, f32[92,8,128]{2,1,0:T(8,128)S(1)}, u32[]{:S(2)}, u32[]{:S(2)}) %collective-permute-start.2) | collective-permute-done | bytes 376864 | tf_op jit(solution)/shard_map/ppermute | solution.py:498
  21.5 4.4 %collective-permute-done.3.from_north = f32[92,8,128]{2,1,0:T(8,128)S(1)} collective-permute-done((f32[92,8,128]{2,1,0:T(8,128)S(1)}, f32[92,8,128]{2,1,0:T(8,128)S(1)}, u32[]{:S(2)}, u32[]{:S(2)}) %collective-permute-start.3) | collective-permute-done | bytes 376864 | tf_op jit(solution)/shard_map/ppermute | solution.py:498
  25.9 7.9 %shard_map.79 = (f32[16,4,2,8,128]{4,3,2,1,0:T(8,128)S(1)}, f32[8,4,128]{2,1,0:T(4,128)S(1)}) custom-call(f32[16,4,2,8,128]{4,3,2,1,0:T(8,128)S(1)} %get-tuple-element.14.source, f32[22,8,128]{2,1,0:T(8,128)S(1)} %get-tuple-element.18.halo, f32[17,16,128]{2,1,0:T(8,128)S(1)} %get-tuple-element.17.fields, f32[4,16,128]{2,1,0:T(8,128)S(1)} %get-tuple-element.19.prior, ...), custom_call_target="tpu_custom_call" | custom-call | tf_op jit(solution)/shard_map/pallas_call | solution.py:478
  33.8 14.5 %all_to_all.10 = f32[8,4,128]{2,1,0:T(4,128)S(1)} all-to-all(f32[8,4,128]{2,1,0:T(4,128)S(1)} %get-tuple-element.22), channel_id=1, replica_groups=mesh['gx'=8,'gy'=32] {'gx'}, dimensions={0} | all-to-all | bytes 32768 | tf_op jit(solution)/shard_map/all_to_all | solution.py:501
  48.3 0.1 shard_map.80
  48.4 15.9 %all_to_all.11 = f32[32,4,128]{2,1,0:T(4,128)S(1)} all-to-all(f32[32,4,128]{2,1,0:T(4,128)S(1)} %shard_map.80), channel_id=1, replica_groups=mesh['gx'=8,'gy'=32] {'gy'}, dimensions={0} | all-to-all | bytes 131072 | tf_op jit(solution)/shard_map/all_to_all | solution.py:501
  64.2 3.6 %shard_map.81 = (f32[4,256,128]{2,1,0:T(8,128)}, f32[16,16]{1,0:T(8,128)}) custom-call(f32[16,8,128]{2,1,0:T(8,128)S(1)} %bitcast.4, f32[16,4,2,8,128]{4,3,2,1,0:T(8,128)S(1)} %get-tuple-element.23.refs_1_), custom_call_target="tpu_custom_call" | custom-call | tf_op jit(solution)/shard_map/pallas_call | solution.py:478
Async XLA Ops:
  2.1 5.9 %collective-permute-start = (f32[22,8,128]{2,1,0:T(8,128)S(1)}, f32[22,8,128]{2,1,0:T(8,128)S(1)}, u32[]{:S(2)}, u32[]{:S(2)}) collective-permute-start(f32[22,8,128]{2,1,0:T(8,128)S(1)} %get-tuple-element.15), channel_id=1, source_target_pairs={{0,32},{32,64},{64,96},{96,128},{128,160},{160,192},{192,224},{1,3... | collective-permute-start | bytes 270344 | tf_op jit(solution)/shard_map/ppermute | solution.py:498
  6.5 5.5 %collective-permute-start.1 = (f32[22,8,128]{2,1,0:T(8,128)S(1)}, f32[22,8,128]{2,1,0:T(8,128)S(1)}, u32[]{:S(2)}, u32[]{:S(2)}) collective-permute-start(f32[22,8,128]{2,1,0:T(8,128)S(1)} %get-tuple-element.16), channel_id=1, source_target_pairs={{32,0},{64,32},{96,64},{128,96},{160,128},{192,160},{224,192},{33,... | collective-permute-start | bytes 270344 | tf_op jit(solution)/shard_map/ppermute | solution.py:498
  12.0 9.5 %collective-permute-start.2 = (f32[92,8,128]{2,1,0:T(8,128)S(1)}, f32[92,8,128]{2,1,0:T(8,128)S(1)}, u32[]{:S(2)}, u32[]{:S(2)}) collective-permute-start(f32[92,8,128]{2,1,0:T(8,128)S(1)} %get-tuple-element.20), channel_id=1, source_target_pairs={{0,1},{1,2},{2,3},{3,4},{4,5},{5,6},{6,7},{7,8},{8,9},{9,10},{10,1... | collective-permute-start | bytes 1130504 | tf_op jit(solution)/shard_map/ppermute | solution.py:498
  17.0 8.9 %collective-permute-start.3 = (f32[92,8,128]{2,1,0:T(8,128)S(1)}, f32[92,8,128]{2,1,0:T(8,128)S(1)}, u32[]{:S(2)}, u32[]{:S(2)}) collective-permute-start(f32[92,8,128]{2,1,0:T(8,128)S(1)} %get-tuple-element.21), channel_id=1, source_target_pairs={{1,0},{2,1},{3,2},{4,3},{5,4},{6,5},{7,6},{8,7},{9,8},{10,9},{11,1... | collective-permute-start | bytes 1130504 | tf_op jit(solution)/shard_map/ppermute | solution.py:498

commit v3 on v2

v3 whole, which is shorter than its diff:
```python
import math
import jax
import jax.numpy as jnp
from jax import lax
from jax.experimental import pallas as pl
from jax.experimental.pallas import tpu as pltpu
from jax.sharding import PartitionSpec as P

STEPS = 4
LEVELS = 4
PROBES = 16
HALO = 2 * STEPS
LANES = 128
ROWS = 16
EXT = ROWS + 2 * HALO
F32 = jnp.float32

FIELDS = 17
GROUPS = 3
EAST, WEST, NORTH, SOUTH, CENTER, RATE, OBS, DERIVED = 0, 4, 8, 12, 16, 20, 21, 25
X_PARTS = ROWS + 2 * GROUPS
Y_SOURCE, Y_HALO, Y_COEF, Y_COEF_HALO, Y_PARTS = 0, 64, 72, 89, 92
SLICES = 4


def lane_ids():
    return lax.broadcasted_iota(jnp.int32, (8, LANES), 1)


def roll_lanes(value, shift):
    shift = shift % LANES
    return value if shift == 0 else pltpu.roll(value, shift, value.ndim - 1)


def pack_kernel(
    probes_in, winds_in, diffusivity_in, mixing_in, prior_in, obs_in,
    source, east, west, fields, prior, probes, sems,
):
    coef_copies = [
        pltpu.make_async_copy(diffusivity_in, fields.at[pl.ds(0, 4)], sems.at[0]),
        pltpu.make_async_copy(winds_in.at[0], fields.at[pl.ds(4, 4)], sems.at[1]),
        pltpu.make_async_copy(winds_in.at[1], fields.at[pl.ds(8, 4)], sems.at[2]),
        pltpu.make_async_copy(obs_in, fields.at[pl.ds(12, 4)], sems.at[3]),
        pltpu.make_async_copy(mixing_in, fields.at[16], sems.at[4]),
    ]
    source_copies = [
        pltpu.make_async_copy(probes_in, probes, sems.at[5]),
        pltpu.make_async_copy(prior_in, prior, sems.at[6]),
    ]
    for copy in source_copies + coef_copies:
        copy.start()
    lanes = lane_ids()
    half = lanes // 8

    def put(held, value, slot):
        to_east, to_west = held
        to_east = jnp.where(half == 2 * slot + 1, roll_lanes(value, 16 * slot + 8 - (LANES - HALO)), to_east)
        to_west = jnp.where(half == 2 * slot, roll_lanes(value, 16 * slot), to_west)
        return to_east, to_west

    zero = jnp.zeros((8, LANES), F32)

    def row(y, carry):
        held = (zero, zero)
        for level in range(LEVELS):
            scale = prior[level, pl.ds(y, 1), :]
            for part in range(2):
                value = probes[level, pl.ds(part * 8 * ROWS + y, 8, stride=ROWS), :] * scale
                source[y, level, part] = value
                held = put(held, value, 2 * level + part)
        east[y], west[y] = held
        return carry

    for copy in coef_copies:
        copy.wait()
    for group in range(GROUPS):
        for tile in range(2):
            held = (zero, zero)
            for slot in range(8):
                field = 8 * group + slot
                if field < FIELDS:
                    held = put(held, fields[field, pl.ds(8 * tile, 8), :], slot)
            east[ROWS + 2 * group + tile], west[ROWS + 2 * group + tile] = held
    for copy in source_copies:
        copy.wait()
    lax.fori_loop(0, ROWS, row, 0, unroll=True)


def merge_kernel(from_west, from_east, source, fields, halo, north, south):
    inner = lane_ids() % 16 < 8
    for index in range(X_PARTS):
        halo[index] = jnp.where(inner, from_east[index], from_west[index])
    for tile, out in ((0, south), (1, north)):
        for y in range(8):
            for level in range(LEVELS):
                for part in range(2):
                    out[(y * LEVELS + level) * 2 + part] = source[8 * tile + y, level, part]
            out[Y_HALO + y] = jnp.where(inner, from_east[8 * tile + y], from_west[8 * tile + y])
        for field in range(FIELDS):
            out[Y_COEF + field] = fields[field, pl.ds(8 * tile, 8), :]
        for group in range(GROUPS):
            index = ROWS + 2 * group + tile
            out[Y_COEF_HALO + group] = jnp.where(inner, from_east[index], from_west[index])


def strip_of(lanes, first, second, halo_first, halo_second, slot_first, slot_second):
    value = roll_lanes(first, 24)
    value = jnp.where(lanes >= 24, roll_lanes(halo_first, 24 - 16 * slot_first), value)
    value = jnp.where(lanes >= 40, roll_lanes(first, 40), value)
    value = jnp.where(lanes >= 64, roll_lanes(second, 88), value)
    value = jnp.where(lanes >= 88, roll_lanes(halo_second, 88 - 16 * slot_second), value)
    return jnp.where(lanes >= 104, roll_lanes(second, 104), value)


def two_sum(a, b):
    total = a + b
    other = total - a
    return total, (a - (total - other)) + (b - other)


def derive(coefs, rows, kind, values):
    rate = values[16]
    coefs[kind, RATE, rows, :] = rate
    for level in range(LEVELS):
        kappa, wind_x, wind_y = values[level], values[4 + level], values[8 + level]
        coefs[kind, EAST + level, rows, :] = kappa - wind_x
        coefs[kind, WEST + level, rows, :] = kappa + wind_x
        coefs[kind, NORTH + level, rows, :] = kappa - wind_y
        coefs[kind, SOUTH + level, rows, :] = kappa + wind_y
        sides = 1.0 if level in (0, LEVELS - 1) else 2.0
        coefs[kind, CENTER + level, rows, :] = 1.0 - 4.0 * kappa - sides * rate
        coefs[kind, OBS + level, rows, :] = values[12 + level]


def derive_both(coefs, tile, main, packed):
    lanes = lane_ids()
    strips = [
        strip_of(lanes, main[field], main[field], packed[field // 8], packed[field // 8], field % 8, field % 8)
        for field in range(FIELDS)
    ]
    for kind, values in ((0, main), (1, strips)):
        derive(coefs, slice(8 * tile, 8 * tile + 8), kind, values)


def vertical(values, level):
    if level == 0:
        return values[1]
    if level == LEVELS - 1:
        return values[LEVELS - 2]
    return values[level - 1] + values[level + 1]


def forward(get, coef_of, low, high, parts, emit):
    def load(y):
        return [[get(y, level, part) for level in range(LEVELS)] for part in parts]

    before, center = load(low - 1), load(low)
    for y in range(low, high):
        after = load(y + 1)
        coef = lambda index: coef_of(parts[0] // 2, index, y)
        rate = coef(RATE)
        results = [[None] * LEVELS for part in parts]
        for level in range(LEVELS):
            middle, east, west, north, south = [coef(base + level) for base in (CENTER, EAST, WEST, NORTH, SOUTH)]
            for index in range(len(parts)):
                value = center[index][level]
                results[index][level] = (
                    (middle * value + rate * vertical(center[index], level))
                    + (north * after[index][level] + south * before[index][level])
                    + (east * roll_lanes(value, -1) + west * roll_lanes(value, 1))
                )
        emit(y, parts, results)
        before, center = center, after


def adjoint(get, coef_of, low, high, parts, emit):
    def load(y):
        return [[get(y, level, part) for level in range(LEVELS)] for part in parts]

    def taken(base, y, values):
        own = [coef_of(parts[0] // 2, base + level, y) for level in range(LEVELS)]
        return [[own[level] * row[level] for level in range(LEVELS)] for row in values]

    pushed = taken(NORTH, low - 1, load(low - 1))
    partial = None
    for y in range(low, high + 1):
        center = load(y)
        if partial is not None:
            pulled = taken(SOUTH, y, center)
            emit(y - 1, parts, [
                [partial[index][level] + pulled[index][level] for level in range(LEVELS)] for index in range(len(parts))
            ])
        if y == high:
            break
        coef = lambda index: coef_of(parts[0] // 2, index, y)
        rate = coef(RATE)
        partial = [[None] * LEVELS for part in parts]
        for level in range(LEVELS):
            middle, east, west = [coef(base + level) for base in (CENTER, EAST, WEST)]
            for index in range(len(parts)):
                value = center[index][level]
                partial[index][level] = (
                    (middle * value + rate * vertical(center[index], level))
                    + (roll_lanes(west * value, -1) + roll_lanes(east * value, 1))
                    + pushed[index][level]
                )
        pushed = taken(NORTH, y, center)


GROUPED = ((2,), (0, 1))


def advance(step, low, high, get, put, coef_of):
    def emit(y, parts, results):
        for index, part in enumerate(parts):
            for level in range(LEVELS):
                value = results[index][level]
                if step < STEPS:
                    value = value + get(0, y, level, part)
                elif step == STEPS:
                    value = value * coef_of(part // 2, OBS + level, y)
                put(step, y, level, part, value)

    before = lambda y, level, part: get(step - 1, y, level, part)
    for parts in GROUPED:
        (forward if step <= STEPS else adjoint)(before, coef_of, low, high, parts, emit)


def inner_kernel(source, halo, fields, inner, coefs):
    lanes = lane_ids()
    for tile in range(2):
        main = [fields[field, 8 * tile : 8 * tile + 8, :] for field in range(FIELDS)]
        derive_both(coefs, tile, main, [halo[ROWS + 2 * group + tile] for group in range(GROUPS)])
    for y in range(ROWS):
        packed = halo[y]
        for level in range(LEVELS):
            low, high = source[y, level, 0], source[y, level, 1]
            inner[0, y, level, 0] = low
            inner[0, y, level, 1] = high
            inner[0, y, level, 2] = strip_of(lanes, low, high, packed, packed, 2 * level, 2 * level + 1)

    def get(step, y, level, part):
        return inner[step, y - HALO, level, part]

    def put(step, y, level, part, value):
        inner[step, y - HALO, level, part] = value

    def coef_of(kind, index, y):
        return coefs[kind, index, y - HALO : y - HALO + 1, :]

    for step in range(1, HALO):
        advance(step, HALO + step, HALO + ROWS - step, get, put, coef_of)


def stencil_kernel(inner, coefs, prior, from_south, from_north, image, message, outer, outer_coefs, slices):
    lanes = lane_ids()
    for tile, ref in ((0, from_south), (1, from_north)):
        main = [ref[Y_COEF + field] for field in range(FIELDS)]
        derive_both(outer_coefs, tile, main, [ref[Y_COEF_HALO + group] for group in range(GROUPS)])
        for y in range(HALO):
            packed = ref[Y_HALO + y]
            for level in range(LEVELS):
                low, high = ref[(y * LEVELS + level) * 2], ref[(y * LEVELS + level) * 2 + 1]
                outer[0, HALO * tile + y, level, 0] = low
                outer[0, HALO * tile + y, level, 1] = high
                outer[0, HALO * tile + y, level, 2] = strip_of(lanes, low, high, packed, packed, 2 * level, 2 * level + 1)

    def place(step, y):
        if y < HALO + step:
            return outer, y - step
        if y >= HALO + ROWS - step:
            return outer, HALO + y - (HALO + ROWS - step)
        return inner, y - HALO

    def get(step, y, level, part):
        ref, row = place(step, y)
        return ref[step, row, level, part]

    def put(step, y, level, part, value):
        ref, row = place(step, y)
        ref[step, row, level, part] = value

    def coef_of(kind, index, y):
        if y < HALO:
            return outer_coefs[kind, index, y : y + 1, :]
        if y >= HALO + ROWS:
            return outer_coefs[kind, index, y - ROWS : y - ROWS + 1, :]
        return coefs[kind, index, y - HALO : y - HALO + 1, :]

    for step in range(1, HALO):
        advance(step, step, step + HALO, get, put, coef_of)
        advance(step, EXT - HALO - step, EXT - step, get, put, coef_of)

    zero = jnp.zeros((8, LANES), F32)
    most = [zero, zero]

    def total_of(y, part, level, value):
        first, second, third = [get(step, y, level, part) for step in range(STEPS + 1, 2 * STEPS)]
        return (first + second) + (third + value)

    def emit_last(y, parts, results):
        for level in range(LEVELS):
            if parts == (2,):
                outer[2 * STEPS, y - HALO, level, 2] = total_of(y, 2, level, results[0][level])
                continue
            scale = prior[level, y - HALO : y - HALO + 1, :]
            strip = outer[2 * STEPS, y - HALO, level, 2]
            for part in parts:
                value = total_of(y, part, level, results[part][level])
                value = jnp.where(lanes < HALO, roll_lanes(strip, -40 - 64 * part), value)
                value = jnp.where(lanes >= LANES - HALO, roll_lanes(strip, 104 - 64 * part), value)
                value = value * scale
                image[y - HALO, level, part] = value
                most[part] = jnp.maximum(most[part], jnp.abs(value))

    for parts in GROUPED:
        adjoint(lambda y, level, part: get(2 * STEPS - 1, y, level, part), coef_of, HALO, HALO + ROWS, parts, emit_last)

    magics = []
    for part in range(2):
        top = jnp.broadcast_to(jnp.max(most[part], axis=1, keepdims=True), (8, LANES))
        scaled = top * (2.0**23 + 1.0)
        power = jnp.abs(scaled - scaled * (1.0 - 2.0**-24))
        magics.append([power * (1.5 * 2.0 ** (23 - 6 - 8 * index)) for index in range(SLICES)])

    def slice_row(y, carry):
        for level in range(LEVELS):
            pieces = []
            for part in range(2):
                rest = image[y, level, part]
                own = []
                for index in range(SLICES):
                    magic = magics[part][index]
                    piece = (rest + magic) - magic
                    rest = rest - piece
                    own.append(piece)
                pieces.append(own)
            for index in range(SLICES):
                both = jnp.concatenate([pieces[0][index], pieces[1][index]], axis=0)
                slices[y, pl.ds(PROBES * index, PROBES), pl.ds(LANES * level, LANES)] = both.astype(jnp.bfloat16)
        return carry

    lax.fori_loop(0, ROWS, slice_row, 0, unroll=True)

    width = PROBES * SLICES
    high = jnp.zeros((width, width), F32)
    low = jnp.zeros((width, width), F32)
    for pair in range(ROWS // 2):
        block = jnp.concatenate([slices[2 * pair], slices[2 * pair + 1]], axis=1)
        product = lax.dot_general(block, block, (((1,), (1,)), ((), ())), preferred_element_type=F32)
        high, error = two_sum(high, product)
        low = low + error

    def fold(high, low, blocks):
        total_high, total_low = None, None
        for block_high, block_low in blocks(high, low):
            if total_high is None:
                total_high, total_low = block_high, block_low
            else:
                total_high, error = two_sum(total_high, block_high)
                total_low = total_low + block_low + error
        return total_high, total_low

    def row_blocks(high, low):
        for index in range(SLICES):
            rows = slice(PROBES * index, PROBES * (index + 1))
            yield high[rows], low[rows]

    def lane_blocks(high, low):
        for index in range(SLICES):
            yield roll_lanes(high, -PROBES * index), roll_lanes(low, -PROBES * index)

    high, low = fold(high, low, row_blocks)
    rest = jnp.zeros((PROBES, LANES - width), F32)
    high, low = jnp.concatenate([high, rest], axis=1), jnp.concatenate([low, rest], axis=1)
    high, low = fold(high, low, lane_blocks)
    high, low = two_sum(high, low)

    wide = lax.broadcasted_iota(jnp.int32, (PROBES, LANES), 1)
    both = jnp.where(wide < PROBES, high, roll_lanes(low, PROBES))
    packed = both[0:8]
    for index in range(1, 4):
        value = both[8 * (index // 2) : 8 * (index // 2) + 8]
        if index % 2:
            value = pltpu.roll(value, 4, 0)
        packed = jnp.where(lanes // 32 == index, roll_lanes(value, 32 * index), packed)
    message[...] = jnp.broadcast_to(packed[None, 0:4], message.shape)


def split(a):
    scaled = a * 4097.0
    high = scaled - (scaled - a)
    return high, a - high


def product_error(a, b, product):
    a_high, a_low = a
    b_high, b_low = b
    return ((a_high * b_high - product) + a_high * b_low + a_low * b_high) + a_low * b_low


def summed(received):
    zero = jnp.zeros((8, LANES), F32)
    chains = 4
    sums, errors = [zero] * chains, [zero] * chains
    for index in range(received.shape[0]):
        chain = index % chains
        sums[chain], error = two_sum(sums[chain], received[index])
        errors[chain] = errors[chain] + error
    total, rest = sums[0], errors[0]
    for chain in range(1, chains):
        total, error = two_sum(total, sums[chain])
        rest = rest + errors[chain] + error
    total, error = two_sum(total, pltpu.roll(total, 4, 0))
    return total, rest + pltpu.roll(rest, 4, 0) + error


def sum_kernel(received, message):
    total, rest = summed(received)
    total = total + jnp.where(lane_ids() % 32 < PROBES, 0.0, roll_lanes(rest, PROBES))
    message[...] = jnp.broadcast_to(total[None, 0:4], message.shape)


def factor_kernel(count, received, image, basis, factor, held, sems):
    upper_half = lax.broadcasted_iota(jnp.int32, (8, LANES), 0) < 4
    total, rest = summed(received)
    rest = rest + roll_lanes(total, -PROBES)

    def unpack(value):
        low = jnp.where(upper_half, value, roll_lanes(value, -32))
        high = jnp.where(upper_half, roll_lanes(value, -64), roll_lanes(value, -96))
        return jnp.concatenate([low, high], axis=0)

    high, low = two_sum(unpack(total), unpack(rest))

    shape = (PROBES, LANES)
    wide = lax.broadcasted_iota(jnp.int32, shape, 1)
    rows = lax.broadcasted_iota(jnp.int32, shape, 0)
    high = jnp.where(wide < PROBES, high, jnp.where(wide == rows + PROBES, 1.0, 0.0))
    low = jnp.where(wide < PROBES, low, 0.0)

    def column(index):
        return [jnp.broadcast_to(value[:, index : index + 1], shape) for value in (high, low)]

    def row_of(value, index):
        return jnp.broadcast_to(value[index : index + 1], shape)

    own_high, own_low = column(0)
    for step in range(PROBES - 1):
        next_high, next_low = column(step + 1)
        pivot_high, pivot_low = row_of(own_high, step), row_of(own_low, step)
        inverse = 1.0 / pivot_high
        ratio = jnp.where(rows > step, own_high * inverse, 0.0)
        ratio_parts = split(ratio)
        taken = ratio * pivot_high
        remainder = ((own_high - taken) - product_error(ratio_parts, split(pivot_high), taken)) + (
            own_low - ratio * pivot_low
        )
        ratio_low = jnp.where(rows > step, remainder * inverse, 0.0)

        def reduce(high, low):
            row_high, row_low = row_of(high, step), row_of(low, step)
            taken = ratio * row_high
            error_taken = product_error(ratio_parts, split(row_high), taken)
            high, error = two_sum(high, -taken)
            low = low + error - error_taken - (ratio * row_low + ratio_low * row_high)
            return two_sum(high, low)

        own_high, own_low = reduce(next_high, next_low)
        high, low = reduce(high, low)

    diagonal = jnp.sum(jnp.where(wide == rows, high, 0.0), axis=1, keepdims=True)
    root = jnp.broadcast_to(jnp.sqrt(diagonal), shape)
    size = math.sqrt(count)
    upper = high / root
    factor[...] = jnp.where(wide >= rows, upper * (1.0 / size), 0.0)[:, :PROBES]
    inverse = upper * size
    columns = [
        jnp.broadcast_to(inverse[:, PROBES + index : PROBES + index + 1], shape) for index in range(PROBES)
    ]

    copies = []
    for level in range(LEVELS):
        for y in range(ROWS):
            outs = [None, None]
            for index in range(PROBES):
                value = image[y, level, index // 8, index % 8 : index % 8 + 1, :]
                for part in range(index // 8, 2):
                    term = columns[index][8 * part : 8 * part + 8] * value
                    outs[part] = term if outs[part] is None else outs[part] + term
            for part in range(2):
                held[level, pl.ds(part * 8 * ROWS + y, 8, stride=ROWS), :] = outs[part]
        copies.append(pltpu.make_async_copy(held.at[level], basis.at[level], sems.at[level]))
        copies[-1].start()
    for copy in copies:
        copy.wait()


def call(kernel, outs, scratch=(), inputs=pltpu.VMEM, spaces=None, cost=None):
    def run(*operands):
        return pl.pallas_call(
            kernel,
            out_shape=[jax.ShapeDtypeStruct(shape, F32) for shape in outs],
            in_specs=[pl.BlockSpec(memory_space=inputs)] * len(operands),
            out_specs=[pl.BlockSpec(memory_space=space) for space in spaces or [pltpu.VMEM] * len(outs)],
            scratch_shapes=list(scratch),
            cost_estimate=cost,
            compiler_params=pltpu.CompilerParams(vmem_limit_bytes=40 << 20),
        )(*operands)

    return run


def body(probes, winds, diffusivity, mixing, prior_scale, obs_weight):
    tile = (8, LANES)
    size_x, size_y = lax.axis_size("gx"), lax.axis_size("gy")
    count = LEVELS * ROWS * LANES * size_x * size_y

    def shift(value, axis, step):
        number = lax.axis_size(axis)
        pairs = [(i, i + step) for i in range(number) if 0 <= i + step < number]
        return lax.ppermute(value, axis, pairs)

    def exchange(message, axis):
        received = lax.all_to_all(message, axis, 0, 0)
        return received.reshape((message.shape[0] // 2,) + tile)

    flat = (LEVELS, PROBES * ROWS, LANES)
    source, east, west, fields, prior = call(
        pack_kernel,
        [(ROWS, LEVELS, 2) + tile, (X_PARTS,) + tile, (X_PARTS,) + tile, (FIELDS, ROWS, LANES), (LEVELS, ROWS, LANES)],
        [pltpu.VMEM(flat, F32), pltpu.SemaphoreType.DMA((7,))],
        pltpu.HBM,
    )(*(pltpu.with_memory_space_constraint(a, pltpu.HBM) for a in (probes.reshape(flat), winds, diffusivity, mixing, prior_scale, obs_weight)))
    from_west = shift(east, "gx", 1)
    from_east = shift(west, "gx", -1)
    halo, north, south = call(
        merge_kernel, [(X_PARTS,) + tile, (Y_PARTS,) + tile, (Y_PARTS,) + tile]
    )(from_west, from_east, source, fields)
    from_south = shift(north, "gy", 1)
    from_north = shift(south, "gy", -1)
    field = (ROWS, LEVELS, 3) + tile
    derived = (2, DERIVED, ROWS, LANES)
    values = HALO * math.prod(field)
    inner, coefs = call(
        inner_kernel,
        [(HALO,) + field, derived],
        cost=pl.CostEstimate(flops=20 * values, bytes_accessed=8 * values, transcendentals=0),
    )(source, halo, fields)
    image, message = call(
        stencil_kernel,
        [(ROWS, LEVELS, 2) + tile, (size_x, 4, LANES)],
        [
            pltpu.VMEM((HALO + 1,) + field, F32),
            pltpu.VMEM(derived, F32),
            pltpu.VMEM((ROWS, PROBES * SLICES, LEVELS * LANES), jnp.bfloat16),
        ],
    )(inner, coefs, prior, from_south, from_north)
    received = exchange(message, "gx")
    (message,) = call(sum_kernel, [(size_y, 4, LANES)])(received)
    received = exchange(message, "gy")
    basis, factor = call(
        lambda *refs: factor_kernel(count, *refs),
        [flat, (PROBES, PROBES)],
        [pltpu.VMEM(flat, F32), pltpu.SemaphoreType.DMA((LEVELS,))],
        spaces=[pltpu.HBM, pltpu.VMEM],
    )(received, image)
    return basis.reshape(probes.shape), factor


def solution(mesh):
    placed = (
        P(None, None, "gy", "gx"),
        P(None, None, "gy", "gx"),
        P(None, "gy", "gx"),
        P("gy", "gx"),
        P(None, "gy", "gx"),
        P(None, "gy", "gx"),
    )
    return jax.shard_map(
        body,
        mesh=mesh,
        in_specs=placed,
        out_specs=(P(None, None, "gy", "gx"), P()),
        check_vma=False,
    )
```

time: 68.1 us -> 65.6 us (0.963)
  waiting for transfers between devices: 11.1 us -> 8.87 us
    ppermute x4, waiting for transfers between devices: 11.1 us -> 8.87 us  [shift(): return lax.ppermute(value, axis, pairs)]
    pallas_call x5 -> x6, Pallas kernels: 13.1 us -> 12.9 us  [run(): pl.pallas_call(kernel, out_shape=[jax.ShapeDtypeStruct(shape, F32) for sh...]
  transfers between devices with their start and end apart: 4 -> 4, of which waited for: 4 -> 4; matrix products, arithmetic and copies ran while one was open for 0% -> 0% of each run, Pallas kernels for 0% -> 3%
where the time goes in v3:
time: 65.6 us; the launch traced here: 65.3 us
  blocking collectives  30.3 us (46%)
  Pallas kernels  12.9 us (20%)
  starting transfers between devices  12.5 us (19%)
  waiting for transfers between devices  8.87 us (14%)
  between operations  0.69 us (1%)
    all_to_all x2, blocking collectives, exchange(): received = lax.all_to_all(message, axis, 0, 0)  30.3 us
    pallas_call x6, Pallas kernels, run(): pl.pallas_call(kernel, out_shape=[jax.ShapeDtypeStruct(shape, F32) for sh...  12.9 us
    ppermute x4, starting transfers between devices, shift(): return lax.ppermute(value, axis, pairs)  12.5 us
    ppermute x4, waiting for transfers between devices, shift(): return lax.ppermute(value, axis, pairs)  8.87 us
  transfers between devices with their start and end apart: 4, of which 4 were waited for; matrix products, arithmetic and copies ran while one was open for 0% of the time, Pallas kernels for 3%

profile of v3, /device:TPU:1, one launch (start us, length us, event | category | flops | bytes accessed | tf_op | source)
XLA Modules:
  0.0 65.3 jit_solution(6879955319151984539)
XLA Ops:
  0.6 1.5 %shard_map.77 = (f32[16,4,2,8,128]{4,3,2,1,0:T(8,128)S(1)}, f32[22,8,128]{2,1,0:T(8,128)S(1)}, f32[22,8,128]{2,1,0:T(8,128)S(1)}, f32[17,16,128]{2,1,0:T(8,128)S(1)}, f32[4,16,128]{2,1,0:T(8,128)S(1)}) custom-call(f32[4,256,128]{2,1,0:T(8,128)} %bitcast.6, f32[2,4,16,128]{3,2,1,0:T(8,128)} %winds_in.1, f32[4,16,128]{2,1,0:T(8,128)} %diffusivity_in.1, ...), custom_call_target="tpu_custom_call" | custom-call | tf_op jit(solution)/shard_map/pallas_call | solution.py:501
  2.1 4.4 %collective-permute-start = (f32[22,8,128]{2,1,0:T(8,128)S(1)}, f32[22,8,128]{2,1,0:T(8,128)S(1)}, u32[]{:S(2)}, u32[]{:S(2)}) collective-permute-start(f32[22,8,128]{2,1,0:T(8,128)S(1)} %get-tuple-element.17), channel_id=1, source_target_pairs={{0,32},{32,64},{64,96},{96,128},{128,160},{160,192},{192,224},{1,3... | collective-permute-start | bytes 270344 | tf_op jit(solution)/shard_map/ppermute | solution.py:522
  6.5 1.3 %collective-permute-start.1 = (f32[22,8,128]{2,1,0:T(8,128)S(1)}, f32[22,8,128]{2,1,0:T(8,128)S(1)}, u32[]{:S(2)}, u32[]{:S(2)}) collective-permute-start(f32[22,8,128]{2,1,0:T(8,128)S(1)} %get-tuple-element.18), channel_id=1, source_target_pairs={{32,0},{64,32},{96,64},{128,96},{160,128},{192,160},{224,192},{33,... | collective-permute-start | bytes 270344 | tf_op jit(solution)/shard_map/ppermute | solution.py:522
  7.8 0.2 collective-permute-done.from_west
  8.1 3.9 %collective-permute-done.1.from_east = f32[22,8,128]{2,1,0:T(8,128)S(1)} collective-permute-done((f32[22,8,128]{2,1,0:T(8,128)S(1)}, f32[22,8,128]{2,1,0:T(8,128)S(1)}, u32[]{:S(2)}, u32[]{:S(2)}) %collective-permute-start.1) | collective-permute-done | bytes 90144 | tf_op jit(solution)/shard_map/ppermute | solution.py:522
  12.0 0.1 shard_map.78
  12.0 4.9 %collective-permute-start.2 = (f32[92,8,128]{2,1,0:T(8,128)S(1)}, f32[92,8,128]{2,1,0:T(8,128)S(1)}, u32[]{:S(2)}, u32[]{:S(2)}) collective-permute-start(f32[92,8,128]{2,1,0:T(8,128)S(1)} %get-tuple-element.24), channel_id=1, source_target_pairs={{0,1},{1,2},{2,3},{3,4},{4,5},{5,6},{6,7},{7,8},{8,9},{9,10},{10,1... | collective-permute-start | bytes 1130504 | tf_op jit(solution)/shard_map/ppermute | solution.py:522
  17.0 1.9 %collective-permute-start.3 = (f32[92,8,128]{2,1,0:T(8,128)S(1)}, f32[92,8,128]{2,1,0:T(8,128)S(1)}, u32[]{:S(2)}, u32[]{:S(2)}) collective-permute-start(f32[92,8,128]{2,1,0:T(8,128)S(1)} %get-tuple-element.25), channel_id=1, source_target_pairs={{1,0},{2,1},{3,2},{4,3},{5,4},{6,5},{7,6},{8,7},{9,8},{10,9},{11,1... | collective-permute-start | bytes 1130504 | tf_op jit(solution)/shard_map/ppermute | solution.py:522
  18.9 2.3 %shard_map.79 = (f32[8,16,4,3,8,128]{5,4,3,2,1,0:T(8,128)S(1)}, f32[2,25,16,128]{3,2,1,0:T(8,128)S(1)}) custom-call(f32[16,4,2,8,128]{4,3,2,1,0:T(8,128)S(1)} %get-tuple-element.16.source, f32[22,8,128]{2,1,0:T(8,128)S(1)} %get-tuple-element.20.halo, f32[17,16,128]{2,1,0:T(8,128)S(1)} %get-tuple-element.19.fields), custom_call_target="tpu_custom_call" | custom-call | flops 31457280 | bytes 12582912 | tf_op jit(solution)/shard_map/pallas_call | solution.py:501
  21.2 0.3 collective-permute-done.2.from_south
  21.5 4.4 %collective-permute-done.3.from_north = f32[92,8,128]{2,1,0:T(8,128)S(1)} collective-permute-done((f32[92,8,128]{2,1,0:T(8,128)S(1)}, f32[92,8,128]{2,1,0:T(8,128)S(1)}, u32[]{:S(2)}, u32[]{:S(2)}) %collective-permute-start.3) | collective-permute-done | bytes 376864 | tf_op jit(solution)/shard_map/ppermute | solution.py:522
  25.9 5.7 %shard_map.80 = (f32[16,4,2,8,128]{4,3,2,1,0:T(8,128)S(1)}, f32[8,4,128]{2,1,0:T(4,128)S(1)}) custom-call(f32[8,16,4,3,8,128]{5,4,3,2,1,0:T(8,128)S(1)} %get-tuple-element.21.inner, f32[2,25,16,128]{3,2,1,0:T(8,128)S(1)} %get-tuple-element.22.coefs, f32[4,16,128]{2,1,0:T(8,128)S(1)} %get-tuple-element.23.prior, ...), custom_call_target="tpu_custom_call" | custom-call | tf_op jit(solution)/shard_map/pallas_call | solution.py:501
  31.6 14.5 %all_to_all.10 = f32[8,4,128]{2,1,0:T(4,128)S(1)} all-to-all(f32[8,4,128]{2,1,0:T(4,128)S(1)} %get-tuple-element.26), channel_id=1, replica_groups=mesh['gx'=8,'gy'=32] {'gx'}, dimensions={0} | all-to-all | bytes 32768 | tf_op jit(solution)/shard_map/all_to_all | solution.py:525
  46.0 0.1 shard_map.81
  46.1 15.9 %all_to_all.11 = f32[32,4,128]{2,1,0:T(4,128)S(1)} all-to-all(f32[32,4,128]{2,1,0:T(4,128)S(1)} %shard_map.81), channel_id=1, replica_groups=mesh['gx'=8,'gy'=32] {'gy'}, dimensions={0} | all-to-all | bytes 131072 | tf_op jit(solution)/shard_map/all_to_all | solution.py:525
  62.0 3.3 %shard_map.82 = (f32[4,256,128]{2,1,0:T(8,128)}, f32[16,16]{1,0:T(8,128)}) custom-call(f32[16,8,128]{2,1,0:T(8,128)S(1)} %bitcast.4, f32[16,4,2,8,128]{4,3,2,1,0:T(8,128)S(1)} %get-tuple-element.27.refs_1_), custom_call_target="tpu_custom_call" | custom-call | tf_op jit(solution)/shard_map/pallas_call | solution.py:501
Async XLA Ops:
  2.1 5.9 %collective-permute-start = (f32[22,8,128]{2,1,0:T(8,128)S(1)}, f32[22,8,128]{2,1,0:T(8,128)S(1)}, u32[]{:S(2)}, u32[]{:S(2)}) collective-permute-start(f32[22,8,128]{2,1,0:T(8,128)S(1)} %get-tuple-element.17), channel_id=1, source_target_pairs={{0,32},{32,64},{64,96},{96,128},{128,160},{160,192},{192,224},{1,3... | collective-permute-start | bytes 270344 | tf_op jit(solution)/shard_map/ppermute | solution.py:522
  6.5 5.5 %collective-permute-start.1 = (f32[22,8,128]{2,1,0:T(8,128)S(1)}, f32[22,8,128]{2,1,0:T(8,128)S(1)}, u32[]{:S(2)}, u32[]{:S(2)}) collective-permute-start(f32[22,8,128]{2,1,0:T(8,128)S(1)} %get-tuple-element.18), channel_id=1, source_target_pairs={{32,0},{64,32},{96,64},{128,96},{160,128},{192,160},{224,192},{33,... | collective-permute-start | bytes 270344 | tf_op jit(solution)/shard_map/ppermute | solution.py:522
  12.0 9.5 %collective-permute-start.2 = (f32[92,8,128]{2,1,0:T(8,128)S(1)}, f32[92,8,128]{2,1,0:T(8,128)S(1)}, u32[]{:S(2)}, u32[]{:S(2)}) collective-permute-start(f32[92,8,128]{2,1,0:T(8,128)S(1)} %get-tuple-element.24), channel_id=1, source_target_pairs={{0,1},{1,2},{2,3},{3,4},{4,5},{5,6},{6,7},{7,8},{8,9},{9,10},{10,1... | collective-permute-start | bytes 1130504 | tf_op jit(solution)/shard_map/ppermute | solution.py:522
  17.0 8.9 %collective-permute-start.3 = (f32[92,8,128]{2,1,0:T(8,128)S(1)}, f32[92,8,128]{2,1,0:T(8,128)S(1)}, u32[]{:S(2)}, u32[]{:S(2)}) collective-permute-start(f32[92,8,128]{2,1,0:T(8,128)S(1)} %get-tuple-element.25), channel_id=1, source_target_pairs={{1,0},{2,1},{3,2},{4,3},{5,4},{6,5},{7,6},{8,7},{9,8},{10,9},{11,1... | collective-permute-start | bytes 1130504 | tf_op jit(solution)/shard_map/ppermute | solution.py:522

commit v4 on v3

--- a/solution.py
+++ b/solution.py
@@ -549,16 +549,16 @@
     )(source, halo, fields)
     image, message = call(
         stencil_kernel,
-        [(ROWS, LEVELS, 2) + tile, (size_x, 4, LANES)],
+        [(ROWS, LEVELS, 2) + tile, (size_y, 4, LANES)],
         [
             pltpu.VMEM((HALO + 1,) + field, F32),
             pltpu.VMEM(derived, F32),
             pltpu.VMEM((ROWS, PROBES * SLICES, LEVELS * LANES), jnp.bfloat16),
         ],
     )(inner, coefs, prior, from_south, from_north)
+    received = exchange(message, "gy")
+    (message,) = call(sum_kernel, [(size_x, 4, LANES)])(received)
     received = exchange(message, "gx")
-    (message,) = call(sum_kernel, [(size_y, 4, LANES)])(received)
-    received = exchange(message, "gy")
     basis, factor = call(
         lambda *refs: factor_kernel(count, *refs),
         [flat, (PROBES, PROBES)],

time: 65.6 us -> 65.6 us (level)
  no operation moved by 1% of the time
where the time goes in v4:
time: 65.6 us; the launch traced here: 65.3 us
  blocking collectives  30.3 us (46%)
  Pallas kernels  12.9 us (20%)
  starting transfers between devices  12.5 us (19%)
  waiting for transfers between devices  8.87 us (14%)
  between operations  0.69 us (1%)
    all_to_all x2, blocking collectives, exchange(): received = lax.all_to_all(message, axis, 0, 0)  30.3 us
    pallas_call x6, Pallas kernels, run(): pl.pallas_call(kernel, out_shape=[jax.ShapeDtypeStruct(shape, F32) for sh...  12.9 us
    ppermute x4, starting transfers between devices, shift(): return lax.ppermute(value, axis, pairs)  12.5 us
    ppermute x4, waiting for transfers between devices, shift(): return lax.ppermute(value, axis, pairs)  8.87 us
  transfers between devices with their start and end apart: 4, of which 4 were waited for; matrix products, arithmetic and copies ran while one was open for 0% of the time, Pallas kernels for 3%

profile of v4, /device:TPU:1, one launch (start us, length us, event | category | flops | bytes accessed | tf_op | source)
XLA Modules:
  0.0 65.3 jit_solution(13246580870036829753)
XLA Ops:
  0.6 1.5 %shard_map.77 = (f32[16,4,2,8,128]{4,3,2,1,0:T(8,128)S(1)}, f32[22,8,128]{2,1,0:T(8,128)S(1)}, f32[22,8,128]{2,1,0:T(8,128)S(1)}, f32[17,16,128]{2,1,0:T(8,128)S(1)}, f32[4,16,128]{2,1,0:T(8,128)S(1)}) custom-call(f32[4,256,128]{2,1,0:T(8,128)} %bitcast.6, f32[2,4,16,128]{3,2,1,0:T(8,128)} %winds_in.1, f32[4,16,128]{2,1,0:T(8,128)} %diffusivity_in.1, ...), custom_call_target="tpu_custom_call" | custom-call | tf_op jit(solution)/shard_map/pallas_call | solution.py:501
  2.1 4.4 %collective-permute-start = (f32[22,8,128]{2,1,0:T(8,128)S(1)}, f32[22,8,128]{2,1,0:T(8,128)S(1)}, u32[]{:S(2)}, u32[]{:S(2)}) collective-permute-start(f32[22,8,128]{2,1,0:T(8,128)S(1)} %get-tuple-element.17), channel_id=1, source_target_pairs={{0,32},{32,64},{64,96},{96,128},{128,160},{160,192},{192,224},{1,3... | collective-permute-start | bytes 270344 | tf_op jit(solution)/shard_map/ppermute | solution.py:522
  6.5 1.3 %collective-permute-start.1 = (f32[22,8,128]{2,1,0:T(8,128)S(1)}, f32[22,8,128]{2,1,0:T(8,128)S(1)}, u32[]{:S(2)}, u32[]{:S(2)}) collective-permute-start(f32[22,8,128]{2,1,0:T(8,128)S(1)} %get-tuple-element.18), channel_id=1, source_target_pairs={{32,0},{64,32},{96,64},{128,96},{160,128},{192,160},{224,192},{33,... | collective-permute-start | bytes 270344 | tf_op jit(solution)/shard_map/ppermute | solution.py:522
  7.8 0.2 collective-permute-done.from_west
  8.1 3.9 %collective-permute-done.1.from_east = f32[22,8,128]{2,1,0:T(8,128)S(1)} collective-permute-done((f32[22,8,128]{2,1,0:T(8,128)S(1)}, f32[22,8,128]{2,1,0:T(8,128)S(1)}, u32[]{:S(2)}, u32[]{:S(2)}) %collective-permute-start.1) | collective-permute-done | bytes 90144 | tf_op jit(solution)/shard_map/ppermute | solution.py:522
  12.0 0.1 shard_map.78
  12.0 4.9 %collective-permute-start.2 = (f32[92,8,128]{2,1,0:T(8,128)S(1)}, f32[92,8,128]{2,1,0:T(8,128)S(1)}, u32[]{:S(2)}, u32[]{:S(2)}) collective-permute-start(f32[92,8,128]{2,1,0:T(8,128)S(1)} %get-tuple-element.24), channel_id=1, source_target_pairs={{0,1},{1,2},{2,3},{3,4},{4,5},{5,6},{6,7},{7,8},{8,9},{9,10},{10,1... | collective-permute-start | bytes 1130504 | tf_op jit(solution)/shard_map/ppermute | solution.py:522
  17.0 1.9 %collective-permute-start.3 = (f32[92,8,128]{2,1,0:T(8,128)S(1)}, f32[92,8,128]{2,1,0:T(8,128)S(1)}, u32[]{:S(2)}, u32[]{:S(2)}) collective-permute-start(f32[92,8,128]{2,1,0:T(8,128)S(1)} %get-tuple-element.25), channel_id=1, source_target_pairs={{1,0},{2,1},{3,2},{4,3},{5,4},{6,5},{7,6},{8,7},{9,8},{10,9},{11,1... | collective-permute-start | bytes 1130504 | tf_op jit(solution)/shard_map/ppermute | solution.py:522
  18.9 2.3 %shard_map.79 = (f32[8,16,4,3,8,128]{5,4,3,2,1,0:T(8,128)S(1)}, f32[2,25,16,128]{3,2,1,0:T(8,128)S(1)}) custom-call(f32[16,4,2,8,128]{4,3,2,1,0:T(8,128)S(1)} %get-tuple-element.16.source, f32[22,8,128]{2,1,0:T(8,128)S(1)} %get-tuple-element.20.halo, f32[17,16,128]{2,1,0:T(8,128)S(1)} %get-tuple-element.19.fields), custom_call_target="tpu_custom_call" | custom-call | flops 31457280 | bytes 12582912 | tf_op jit(solution)/shard_map/pallas_call | solution.py:501
  21.2 0.3 collective-permute-done.2.from_south
  21.5 4.4 %collective-permute-done.3.from_north = f32[92,8,128]{2,1,0:T(8,128)S(1)} collective-permute-done((f32[92,8,128]{2,1,0:T(8,128)S(1)}, f32[92,8,128]{2,1,0:T(8,128)S(1)}, u32[]{:S(2)}, u32[]{:S(2)}) %collective-permute-start.3) | collective-permute-done | bytes 376864 | tf_op jit(solution)/shard_map/ppermute | solution.py:522
  25.9 5.7 %shard_map.80 = (f32[16,4,2,8,128]{4,3,2,1,0:T(8,128)S(1)}, f32[32,4,128]{2,1,0:T(4,128)S(1)}) custom-call(f32[8,16,4,3,8,128]{5,4,3,2,1,0:T(8,128)S(1)} %get-tuple-element.21.inner, f32[2,25,16,128]{3,2,1,0:T(8,128)S(1)} %get-tuple-element.22.coefs, f32[4,16,128]{2,1,0:T(8,128)S(1)} %get-tuple-element.23.prior, ...), custom_call_target="tpu_custom_call" | custom-call | tf_op jit(solution)/shard_map/pallas_call | solution.py:501
  31.6 15.9 %all_to_all.10 = f32[32,4,128]{2,1,0:T(4,128)S(1)} all-to-all(f32[32,4,128]{2,1,0:T(4,128)S(1)} %get-tuple-element.26), channel_id=1, replica_groups=mesh['gx'=8,'gy'=32] {'gy'}, dimensions={0} | all-to-all | bytes 131072 | tf_op jit(solution)/shard_map/all_to_all | solution.py:525
  47.5 0.1 shard_map.81
  47.6 14.5 %all_to_all.11 = f32[8,4,128]{2,1,0:T(4,128)S(1)} all-to-all(f32[8,4,128]{2,1,0:T(4,128)S(1)} %shard_map.81), channel_id=1, replica_groups=mesh['gx'=8,'gy'=32] {'gx'}, dimensions={0} | all-to-all | bytes 32768 | tf_op jit(solution)/shard_map/all_to_all | solution.py:525
  62.0 3.2 %shard_map.82 = (f32[4,256,128]{2,1,0:T(8,128)}, f32[16,16]{1,0:T(8,128)}) custom-call(f32[4,8,128]{2,1,0:T(8,128)S(1)} %bitcast.5, f32[16,4,2,8,128]{4,3,2,1,0:T(8,128)S(1)} %get-tuple-element.27.refs_1_), custom_call_target="tpu_custom_call" | custom-call | tf_op jit(solution)/shard_map/pallas_call | solution.py:501
Async XLA Ops:
  2.1 5.9 %collective-permute-start = (f32[22,8,128]{2,1,0:T(8,128)S(1)}, f32[22,8,128]{2,1,0:T(8,128)S(1)}, u32[]{:S(2)}, u32[]{:S(2)}) collective-permute-start(f32[22,8,128]{2,1,0:T(8,128)S(1)} %get-tuple-element.17), channel_id=1, source_target_pairs={{0,32},{32,64},{64,96},{96,128},{128,160},{160,192},{192,224},{1,3... | collective-permute-start | bytes 270344 | tf_op jit(solution)/shard_map/ppermute | solution.py:522
  6.5 5.5 %collective-permute-start.1 = (f32[22,8,128]{2,1,0:T(8,128)S(1)}, f32[22,8,128]{2,1,0:T(8,128)S(1)}, u32[]{:S(2)}, u32[]{:S(2)}) collective-permute-start(f32[22,8,128]{2,1,0:T(8,128)S(1)} %get-tuple-element.18), channel_id=1, source_target_pairs={{32,0},{64,32},{96,64},{128,96},{160,128},{192,160},{224,192},{33,... | collective-permute-start | bytes 270344 | tf_op jit(solution)/shard_map/ppermute | solution.py:522
  12.0 9.5 %collective-permute-start.2 = (f32[92,8,128]{2,1,0:T(8,128)S(1)}, f32[92,8,128]{2,1,0:T(8,128)S(1)}, u32[]{:S(2)}, u32[]{:S(2)}) collective-permute-start(f32[92,8,128]{2,1,0:T(8,128)S(1)} %get-tuple-element.24), channel_id=1, source_target_pairs={{0,1},{1,2},{2,3},{3,4},{4,5},{5,6},{6,7},{7,8},{8,9},{9,10},{10,1... | collective-permute-start | bytes 1130504 | tf_op jit(solution)/shard_map/ppermute | solution.py:522
  17.0 8.9 %collective-permute-start.3 = (f32[92,8,128]{2,1,0:T(8,128)S(1)}, f32[92,8,128]{2,1,0:T(8,128)S(1)}, u32[]{:S(2)}, u32[]{:S(2)}) collective-permute-start(f32[92,8,128]{2,1,0:T(8,128)S(1)} %get-tuple-element.25), channel_id=1, source_target_pairs={{1,0},{2,1},{3,2},{4,3},{5,4},{6,5},{7,6},{8,7},{9,8},{10,9},{11,1... | collective-permute-start | bytes 1130504 | tf_op jit(solution)/shard_map/ppermute | solution.py:522

commit v5 on v4

--- a/solution.py
+++ b/solution.py
@@ -34,7 +34,7 @@
 
 def pack_kernel(
     probes_in, winds_in, diffusivity_in, mixing_in, prior_in, obs_in,
-    source, east, west, fields, prior, probes, sems,
+    source, edges, fields, prior, probes, sems,
 ):
     coef_copies = [
         pltpu.make_async_copy(diffusivity_in, fields.at[pl.ds(0, 4)], sems.at[0]),
@@ -50,57 +50,56 @@
     for copy in source_copies + coef_copies:
         copy.start()
     lanes = lane_ids()
-    half = lanes // 8
 
     def put(held, value, slot):
-        to_east, to_west = held
-        to_east = jnp.where(half == 2 * slot + 1, roll_lanes(value, 16 * slot + 8 - (LANES - HALO)), to_east)
-        to_west = jnp.where(half == 2 * slot, roll_lanes(value, 16 * slot), to_west)
-        return to_east, to_west
+        return jnp.where(lanes // 16 == slot, roll_lanes(value, 16 * slot + HALO), held)
 
     zero = jnp.zeros((8, LANES), F32)
-
-    def row(y, carry):
-        held = (zero, zero)
+    for copy in coef_copies:
+        copy.wait()
+    for group in range(GROUPS):
+        for tile in range(2):
+            held = zero
+            for slot in range(8):
+                field = 8 * group + slot
+                if field < FIELDS:
+                    held = put(held, fields[field, 8 * tile : 8 * tile + 8, :], slot)
+            edges[ROWS + 2 * group + tile] = held
+    for copy in source_copies:
+        copy.wait()
+    for y in range(ROWS):
+        held = zero
         for level in range(LEVELS):
-            scale = prior[level, pl.ds(y, 1), :]
+            scale = prior[level, y : y + 1, :]
             for part in range(2):
                 value = probes[level, pl.ds(part * 8 * ROWS + y, 8, stride=ROWS), :] * scale
                 source[y, level, part] = value
                 held = put(held, value, 2 * level + part)
-        east[y], west[y] = held
-        return carry
-
-    for copy in coef_copies:
-        copy.wait()
-    for group in range(GROUPS):
-        for tile in range(2):
-            held = (zero, zero)
-            for slot in range(8):
-                field = 8 * group + slot
-                if field < FIELDS:
-                    held = put(held, fields[field, pl.ds(8 * tile, 8), :], slot)
-            east[ROWS + 2 * group + tile], west[ROWS + 2 * group + tile] = held
-    for copy in source_copies:
-        copy.wait()
-    lax.fori_loop(0, ROWS, row, 0, unroll=True)
-
-
-def merge_kernel(from_west, from_east, source, fields, halo, north, south):
+        edges[y] = held
+
+
+def is_odd(axis):
+    return lax.axis_index(axis) % 2
+
+
+def merge_kernel(first, second, source, fields, halo, first_out, second_out):
     inner = lane_ids() % 16 < 8
+    odd_x, odd_y = is_odd("gx"), is_odd("gy")
     for index in range(X_PARTS):
-        halo[index] = jnp.where(inner, from_east[index], from_west[index])
-    for tile, out in ((0, south), (1, north)):
+        from_east = jnp.where(odd_x == 0, first[index], second[index])
+        from_west = jnp.where(odd_x == 0, second[index], first[index])
+        halo[index] = jnp.where(inner, roll_lanes(from_east, -HALO), roll_lanes(from_west, HALO))
+    for tile, out in ((1 - odd_y, first_out), (odd_y, second_out)):
+        base = pl.multiple_of(8 * tile, 8)
         for y in range(8):
             for level in range(LEVELS):
                 for part in range(2):
-                    out[(y * LEVELS + level) * 2 + part] = source[8 * tile + y, level, part]
-            out[Y_HALO + y] = jnp.where(inner, from_east[8 * tile + y], from_west[8 * tile + y])
+                    out[(y * LEVELS + level) * 2 + part] = source[base + y, level, part]
+            out[Y_HALO + y] = halo[base + y]
         for field in range(FIELDS):
-            out[Y_COEF + field] = fields[field, pl.ds(8 * tile, 8), :]
+            out[Y_COEF + field] = fields[field, pl.ds(base, 8), :]
         for group in range(GROUPS):
-            index = ROWS + 2 * group + tile
-            out[Y_COEF_HALO + group] = jnp.where(inner, from_east[index], from_west[index])
+            out[Y_COEF_HALO + group] = halo[ROWS + 2 * group + tile]
 
 
 def strip_of(lanes, first, second, halo_first, halo_second, slot_first, slot_second):
@@ -252,15 +251,19 @@
         advance(step, HALO + step, HALO + ROWS - step, get, put, coef_of)
 
 
-def stencil_kernel(inner, coefs, prior, from_south, from_north, image, message, outer, outer_coefs, slices):
+def stencil_kernel(inner, coefs, prior, first, second, image, message, outer, outer_coefs, slices):
     lanes = lane_ids()
-    for tile, ref in ((0, from_south), (1, from_north)):
-        main = [ref[Y_COEF + field] for field in range(FIELDS)]
-        derive_both(outer_coefs, tile, main, [ref[Y_COEF_HALO + group] for group in range(GROUPS)])
+    odd_y = is_odd("gy")
+    for tile in range(2):
+        def beside(index, tile=tile):
+            return jnp.where(odd_y == tile, second[index], first[index])
+
+        main = [beside(Y_COEF + field) for field in range(FIELDS)]
+        derive_both(outer_coefs, tile, main, [beside(Y_COEF_HALO + group) for group in range(GROUPS)])
         for y in range(HALO):
-            packed = ref[Y_HALO + y]
+            packed = beside(Y_HALO + y)
             for level in range(LEVELS):
-                low, high = ref[(y * LEVELS + level) * 2], ref[(y * LEVELS + level) * 2 + 1]
+                low, high = beside((y * LEVELS + level) * 2), beside((y * LEVELS + level) * 2 + 1)
                 outer[0, HALO * tile + y, level, 0] = low
                 outer[0, HALO * tile + y, level, 1] = high
                 outer[0, HALO * tile + y, level, 2] = strip_of(lanes, low, high, packed, packed, 2 * level, 2 * level + 1)
@@ -516,29 +519,25 @@
     size_x, size_y = lax.axis_size("gx"), lax.axis_size("gy")
     count = LEVELS * ROWS * LANES * size_x * size_y
 
-    def shift(value, axis, step):
-        number = lax.axis_size(axis)
-        pairs = [(i, i + step) for i in range(number) if 0 <= i + step < number]
-        return lax.ppermute(value, axis, pairs)
+    def swap(value, axis, start):
+        pairs = [(i, i + 1) for i in range(start, lax.axis_size(axis) - 1, 2)]
+        return lax.ppermute(value, axis, pairs + [(j, i) for i, j in pairs])
 
     def exchange(message, axis):
         received = lax.all_to_all(message, axis, 0, 0)
         return received.reshape((message.shape[0] // 2,) + tile)
 
     flat = (LEVELS, PROBES * ROWS, LANES)
-    source, east, west, fields, prior = call(
+    source, edges, fields, prior = call(
         pack_kernel,
-        [(ROWS, LEVELS, 2) + tile, (X_PARTS,) + tile, (X_PARTS,) + tile, (FIELDS, ROWS, LANES), (LEVELS, ROWS, LANES)],
+        [(ROWS, LEVELS, 2) + tile, (X_PARTS,) + tile, (FIELDS, ROWS, LANES), (LEVELS, ROWS, LANES)],
         [pltpu.VMEM(flat, F32), pltpu.SemaphoreType.DMA((7,))],
         pltpu.HBM,
     )(*(pltpu.with_memory_space_constraint(a, pltpu.HBM) for a in (probes.reshape(flat), winds, diffusivity, mixing, prior_scale, obs_weight)))
-    from_west = shift(east, "gx", 1)
-    from_east = shift(west, "gx", -1)
-    halo, north, south = call(
+    halo, first, second = call(
         merge_kernel, [(X_PARTS,) + tile, (Y_PARTS,) + tile, (Y_PARTS,) + tile]
-    )(from_west, from_east, source, fields)
-    from_south = shift(north, "gy", 1)
-    from_north = shift(south, "gy", -1)
+    )(swap(edges, "gx", 0), swap(edges, "gx", 1), source, fields)
+    first, second = swap(first, "gy", 0), swap(second, "gy", 1)
     field = (ROWS, LEVELS, 3) + tile
     derived = (2, DERIVED, ROWS, LANES)
     values = HALO * math.prod(field)
@@ -555,7 +554,7 @@
             pltpu.VMEM(derived, F32),
             pltpu.VMEM((ROWS, PROBES * SLICES, LEVELS * LANES), jnp.bfloat16),
         ],
-    )(inner, coefs, prior, from_south, from_north)
+    )(inner, coefs, prior, first, second)
     received = exchange(message, "gy")
     (message,) = call(sum_kernel, [(size_x, 4, LANES)])(received)
     received = exchange(message, "gx")

time: 65.6 us -> 60.4 us (0.921)
  waiting for transfers between devices: 8.87 us -> 5.51 us
  starting transfers between devices: 12.5 us -> 11 us
    ppermute x4, waiting for transfers between devices: 8.87 us -> 5.51 us  [swap(): return lax.ppermute(value, axis, pairs + [(j, i) for i, j in pairs])]
    ppermute x4, starting transfers between devices: 12.5 us -> 11 us  [swap(): return lax.ppermute(value, axis, pairs + [(j, i) for i, j in pairs])]
  transfers between devices with their start and end apart: 4 -> 4, of which waited for: 4 -> 2; matrix products, arithmetic and copies ran while one was open for 0% -> 0% of each run, Pallas kernels for 3% -> 4%
where the time goes in v5:
time: 60.4 us; the launch traced here: 60.1 us
  blocking collectives  30.1 us (50%)
  Pallas kernels  12.8 us (21%)
  starting transfers between devices  11 us (18%)
  waiting for transfers between devices  5.51 us (9%)
  between operations  0.68 us (1%)
    all_to_all x2, blocking collectives, exchange(): received = lax.all_to_all(message, axis, 0, 0)  30.1 us
    pallas_call x6, Pallas kernels, run(): pl.pallas_call(kernel, out_shape=[jax.ShapeDtypeStruct(shape, F32) for sh...  12.8 us
    ppermute x4, starting transfers between devices, swap(): return lax.ppermute(value, axis, pairs + [(j, i) for i, j in pairs])  11 us
    ppermute x4, waiting for transfers between devices, swap(): return lax.ppermute(value, axis, pairs + [(j, i) for i, j in pairs])  5.51 us
  transfers between devices with their start and end apart: 4, of which 2 were waited for; matrix products, arithmetic and copies ran while one was open for 0% of the time, Pallas kernels for 4%

profile of v5, /device:TPU:1, one launch (start us, length us, event | category | flops | bytes accessed | tf_op | source)
XLA Modules:
  0.0 60.1 jit_solution(6158443902216284127)
XLA Ops:
  0.6 1.4 %shard_map.77 = (f32[16,4,2,8,128]{4,3,2,1,0:T(8,128)S(1)}, f32[22,8,128]{2,1,0:T(8,128)S(1)}, f32[17,16,128]{2,1,0:T(8,128)S(1)}, f32[4,16,128]{2,1,0:T(8,128)S(1)}) custom-call(f32[4,256,128]{2,1,0:T(8,128)} %bitcast.6, f32[2,4,16,128]{3,2,1,0:T(8,128)} %winds_in.1, f32[4,16,128]{2,1,0:T(8,128)} %diffusivity_in.1, f32[16,128]{1,0:T(8,128)} %mixing_in.1, ...), custom_call_target="tpu_custom_call" | custom-call | tf_op jit(solution)/shard_map/pallas_call | solution.py:504
  2.0 0.7 %collective-permute-start.1 = (f32[22,8,128]{2,1,0:T(8,128)S(1)}, f32[22,8,128]{2,1,0:T(8,128)S(1)}, u32[]{:S(2)}, u32[]{:S(2)}) collective-permute-start(f32[22,8,128]{2,1,0:T(8,128)S(1)} %get-tuple-element.16), channel_id=1, source_target_pairs={{32,64},{96,128},{160,192},{64,32},{128,96},{192,160},{33,65},{97,... | collective-permute-start | bytes 270344 | tf_op jit(solution)/shard_map/ppermute | solution.py:524
  2.7 5.4 %collective-permute-start = (f32[22,8,128]{2,1,0:T(8,128)S(1)}, f32[22,8,128]{2,1,0:T(8,128)S(1)}, u32[]{:S(2)}, u32[]{:S(2)}) collective-permute-start(f32[22,8,128]{2,1,0:T(8,128)S(1)} %get-tuple-element.16), channel_id=1, source_target_pairs={{0,32},{64,96},{128,160},{192,224},{32,0},{96,64},{160,128},{224,1... | collective-permute-start | bytes 270344 | tf_op jit(solution)/shard_map/ppermute | solution.py:524
  8.1 0.0 collective-permute-done.1.second
  8.1 1.9 %collective-permute-done.first = f32[22,8,128]{2,1,0:T(8,128)S(1)} collective-permute-done((f32[22,8,128]{2,1,0:T(8,128)S(1)}, f32[22,8,128]{2,1,0:T(8,128)S(1)}, u32[]{:S(2)}, u32[]{:S(2)}) %collective-permute-start) | collective-permute-done | bytes 90144 | tf_op jit(solution)/shard_map/ppermute | solution.py:524
  10.1 0.1 shard_map.78
  10.2 1.9 %collective-permute-start.2 = (f32[92,8,128]{2,1,0:T(8,128)S(1)}, f32[92,8,128]{2,1,0:T(8,128)S(1)}, u32[]{:S(2)}, u32[]{:S(2)}) collective-permute-start(f32[92,8,128]{2,1,0:T(8,128)S(1)} %get-tuple-element.22), channel_id=1, source_target_pairs={{0,1},{2,3},{4,5},{6,7},{8,9},{10,11},{12,13},{14,15},{16,17},{18,... | collective-permute-start | bytes 1130504 | tf_op jit(solution)/shard_map/ppermute | solution.py:524
  12.1 3.0 %collective-permute-start.3 = (f32[92,8,128]{2,1,0:T(8,128)S(1)}, f32[92,8,128]{2,1,0:T(8,128)S(1)}, u32[]{:S(2)}, u32[]{:S(2)}) collective-permute-start(f32[92,8,128]{2,1,0:T(8,128)S(1)} %get-tuple-element.23), channel_id=1, source_target_pairs={{1,2},{3,4},{5,6},{7,8},{9,10},{11,12},{13,14},{15,16},{17,18},{19... | collective-permute-start | bytes 1130504 | tf_op jit(solution)/shard_map/ppermute | solution.py:524
  15.1 2.3 %shard_map.79 = (f32[8,16,4,3,8,128]{5,4,3,2,1,0:T(8,128)S(1)}, f32[2,25,16,128]{3,2,1,0:T(8,128)S(1)}) custom-call(f32[16,4,2,8,128]{4,3,2,1,0:T(8,128)S(1)} %get-tuple-element.15.source, f32[22,8,128]{2,1,0:T(8,128)S(1)} %get-tuple-element.18.halo, f32[17,16,128]{2,1,0:T(8,128)S(1)} %get-tuple-element.17.fields), custom_call_target="tpu_custom_call" | custom-call | flops 31457280 | bytes 12582912 | tf_op jit(solution)/shard_map/pallas_call | solution.py:504
  17.4 0.0 collective-permute-done.2.first
  17.4 3.6 %collective-permute-done.3.second = f32[92,8,128]{2,1,0:T(8,128)S(1)} collective-permute-done((f32[92,8,128]{2,1,0:T(8,128)S(1)}, f32[92,8,128]{2,1,0:T(8,128)S(1)}, u32[]{:S(2)}, u32[]{:S(2)}) %collective-permute-start.3) | collective-permute-done | bytes 376864 | tf_op jit(solution)/shard_map/ppermute | solution.py:524
  21.0 5.7 %shard_map.80 = (f32[16,4,2,8,128]{4,3,2,1,0:T(8,128)S(1)}, f32[32,4,128]{2,1,0:T(4,128)S(1)}) custom-call(f32[8,16,4,3,8,128]{5,4,3,2,1,0:T(8,128)S(1)} %get-tuple-element.19.inner, f32[2,25,16,128]{3,2,1,0:T(8,128)S(1)} %get-tuple-element.20.coefs, f32[4,16,128]{2,1,0:T(8,128)S(1)} %get-tuple-element.21.prior, ...), custom_call_target="tpu_custom_call" | custom-call | tf_op jit(solution)/shard_map/pallas_call | solution.py:504
  26.7 16.2 %all_to_all.10 = f32[32,4,128]{2,1,0:T(4,128)S(1)} all-to-all(f32[32,4,128]{2,1,0:T(4,128)S(1)} %get-tuple-element.24), channel_id=1, replica_groups=mesh['gx'=8,'gy'=32] {'gy'}, dimensions={0} | all-to-all | bytes 131072 | tf_op jit(solution)/shard_map/all_to_all | solution.py:527
  42.9 0.1 shard_map.81
  43.0 13.9 %all_to_all.11 = f32[8,4,128]{2,1,0:T(4,128)S(1)} all-to-all(f32[8,4,128]{2,1,0:T(4,128)S(1)} %shard_map.81), channel_id=1, replica_groups=mesh['gx'=8,'gy'=32] {'gx'}, dimensions={0} | all-to-all | bytes 32768 | tf_op jit(solution)/shard_map/all_to_all | solution.py:527
  56.9 3.2 %shard_map.82 = (f32[4,256,128]{2,1,0:T(8,128)}, f32[16,16]{1,0:T(8,128)}) custom-call(f32[4,8,128]{2,1,0:T(8,128)S(1)} %bitcast.5, f32[16,4,2,8,128]{4,3,2,1,0:T(8,128)S(1)} %get-tuple-element.25.refs_1_), custom_call_target="tpu_custom_call" | custom-call | tf_op jit(solution)/shard_map/pallas_call | solution.py:504
Async XLA Ops:
  2.0 6.1 %collective-permute-start.1 = (f32[22,8,128]{2,1,0:T(8,128)S(1)}, f32[22,8,128]{2,1,0:T(8,128)S(1)}, u32[]{:S(2)}, u32[]{:S(2)}) collective-permute-start(f32[22,8,128]{2,1,0:T(8,128)S(1)} %get-tuple-element.16), channel_id=1, source_target_pairs={{32,64},{96,128},{160,192},{64,32},{128,96},{192,160},{33,65},{97,... | collective-permute-start | bytes 270344 | tf_op jit(solution)/shard_map/ppermute | solution.py:524
  2.7 7.4 %collective-permute-start = (f32[22,8,128]{2,1,0:T(8,128)S(1)}, f32[22,8,128]{2,1,0:T(8,128)S(1)}, u32[]{:S(2)}, u32[]{:S(2)}) collective-permute-start(f32[22,8,128]{2,1,0:T(8,128)S(1)} %get-tuple-element.16), channel_id=1, source_target_pairs={{0,32},{64,96},{128,160},{192,224},{32,0},{96,64},{160,128},{224,1... | collective-permute-start | bytes 270344 | tf_op jit(solution)/shard_map/ppermute | solution.py:524
  10.2 7.2 %collective-permute-start.2 = (f32[92,8,128]{2,1,0:T(8,128)S(1)}, f32[92,8,128]{2,1,0:T(8,128)S(1)}, u32[]{:S(2)}, u32[]{:S(2)}) collective-permute-start(f32[92,8,128]{2,1,0:T(8,128)S(1)} %get-tuple-element.22), channel_id=1, source_target_pairs={{0,1},{2,3},{4,5},{6,7},{8,9},{10,11},{12,13},{14,15},{16,17},{18,... | collective-permute-start | bytes 1130504 | tf_op jit(solution)/shard_map/ppermute | solution.py:524
  12.1 8.9 %collective-permute-start.3 = (f32[92,8,128]{2,1,0:T(8,128)S(1)}, f32[92,8,128]{2,1,0:T(8,128)S(1)}, u32[]{:S(2)}, u32[]{:S(2)}) collective-permute-start(f32[92,8,128]{2,1,0:T(8,128)S(1)} %get-tuple-element.23), channel_id=1, source_target_pairs={{1,2},{3,4},{5,6},{7,8},{9,10},{11,12},{13,14},{15,16},{17,18},{19... | collective-permute-start | bytes 1130504 | tf_op jit(solution)/shard_map/ppermute | solution.py:524

commit v6 on v5

--- a/solution.py
+++ b/solution.py
@@ -251,29 +251,24 @@
         advance(step, HALO + step, HALO + ROWS - step, get, put, coef_of)
 
 
-def stencil_kernel(inner, coefs, prior, first, second, image, message, outer, outer_coefs, slices):
+def side(tile, received, inner, coefs, prior, image, most_out, outer, outer_coefs):
     lanes = lane_ids()
-    odd_y = is_odd("gy")
-    for tile in range(2):
-        def beside(index, tile=tile):
-            return jnp.where(odd_y == tile, second[index], first[index])
-
-        main = [beside(Y_COEF + field) for field in range(FIELDS)]
-        derive_both(outer_coefs, tile, main, [beside(Y_COEF_HALO + group) for group in range(GROUPS)])
-        for y in range(HALO):
-            packed = beside(Y_HALO + y)
-            for level in range(LEVELS):
-                low, high = beside((y * LEVELS + level) * 2), beside((y * LEVELS + level) * 2 + 1)
-                outer[0, HALO * tile + y, level, 0] = low
-                outer[0, HALO * tile + y, level, 1] = high
-                outer[0, HALO * tile + y, level, 2] = strip_of(lanes, low, high, packed, packed, 2 * level, 2 * level + 1)
+    main = [received[Y_COEF + field] for field in range(FIELDS)]
+    derive_both(outer_coefs, 0, main, [received[Y_COEF_HALO + group] for group in range(GROUPS)])
+    for y in range(HALO):
+        packed = received[Y_HALO + y]
+        for level in range(LEVELS):
+            low, high = received[(y * LEVELS + level) * 2], received[(y * LEVELS + level) * 2 + 1]
+            outer[0, y, level, 0] = low
+            outer[0, y, level, 1] = high
+            outer[0, y, level, 2] = strip_of(lanes, low, high, packed, packed, 2 * level, 2 * level + 1)
+
+    def first_row(step):
+        return EXT - HALO - step if tile else step
 
     def place(step, y):
-        if y < HALO + step:
-            return outer, y - step
-        if y >= HALO + ROWS - step:
-            return outer, HALO + y - (HALO + ROWS - step)
-        return inner, y - HALO
+        base = first_row(step)
+        return (outer, y - base) if base <= y < base + HALO else (inner, y - HALO)
 
     def get(step, y, level, part):
         ref, row = place(step, y)
@@ -284,18 +279,16 @@
         ref[step, row, level, part] = value
 
     def coef_of(kind, index, y):
-        if y < HALO:
-            return outer_coefs[kind, index, y : y + 1, :]
-        if y >= HALO + ROWS:
-            return outer_coefs[kind, index, y - ROWS : y - ROWS + 1, :]
+        base = first_row(0)
+        if base <= y < base + HALO:
+            return outer_coefs[kind, index, y - base : y - base + 1, :]
         return coefs[kind, index, y - HALO : y - HALO + 1, :]
 
     for step in range(1, HALO):
-        advance(step, step, step + HALO, get, put, coef_of)
-        advance(step, EXT - HALO - step, EXT - step, get, put, coef_of)
-
-    zero = jnp.zeros((8, LANES), F32)
-    most = [zero, zero]
+        advance(step, first_row(step), first_row(step) + HALO, get, put, coef_of)
+
+    most = [jnp.zeros((8, LANES), F32)] * 2
+    last = first_row(HALO)
 
     def total_of(y, part, level, value):
         first, second, third = [get(step, y, level, part) for step in range(STEPS + 1, 2 * STEPS)]
@@ -304,29 +297,40 @@
     def emit_last(y, parts, results):
         for level in range(LEVELS):
             if parts == (2,):
-                outer[2 * STEPS, y - HALO, level, 2] = total_of(y, 2, level, results[0][level])
+                outer[HALO, y - last, level, 2] = total_of(y, 2, level, results[0][level])
                 continue
             scale = prior[level, y - HALO : y - HALO + 1, :]
-            strip = outer[2 * STEPS, y - HALO, level, 2]
+            strip = outer[HALO, y - last, level, 2]
             for part in parts:
                 value = total_of(y, part, level, results[part][level])
                 value = jnp.where(lanes < HALO, roll_lanes(strip, -40 - 64 * part), value)
                 value = jnp.where(lanes >= LANES - HALO, roll_lanes(strip, 104 - 64 * part), value)
                 value = value * scale
-                image[y - HALO, level, part] = value
+                image[y - last, level, part] = value
                 most[part] = jnp.maximum(most[part], jnp.abs(value))
 
     for parts in GROUPED:
-        adjoint(lambda y, level, part: get(2 * STEPS - 1, y, level, part), coef_of, HALO, HALO + ROWS, parts, emit_last)
-
+        adjoint(lambda y, level, part: get(HALO - 1, y, level, part), coef_of, last, last + HALO, parts, emit_last)
+    for part in range(2):
+        most_out[part] = most[part]
+
+
+def both_sides(first, args):
+    odd_y = is_odd("gy")
+    for tile in range(2):
+        @pl.when(odd_y == (1 - tile if first else tile))
+        def _(tile=tile):
+            side(tile, *args)
+
+
+def gram_pieces(image, most, slices, high, low):
     magics = []
     for part in range(2):
         top = jnp.broadcast_to(jnp.max(most[part], axis=1, keepdims=True), (8, LANES))
         scaled = top * (2.0**23 + 1.0)
         power = jnp.abs(scaled - scaled * (1.0 - 2.0**-24))
         magics.append([power * (1.5 * 2.0 ** (23 - 6 - 8 * index)) for index in range(SLICES)])
-
-    def slice_row(y, carry):
+    for y in range(HALO):
         for level in range(LEVELS):
             pieces = []
             for part in range(2):
@@ -341,18 +345,27 @@
             for index in range(SLICES):
                 both = jnp.concatenate([pieces[0][index], pieces[1][index]], axis=0)
                 slices[y, pl.ds(PROBES * index, PROBES), pl.ds(LANES * level, LANES)] = both.astype(jnp.bfloat16)
-        return carry
-
-    lax.fori_loop(0, ROWS, slice_row, 0, unroll=True)
-
-    width = PROBES * SLICES
-    high = jnp.zeros((width, width), F32)
-    low = jnp.zeros((width, width), F32)
-    for pair in range(ROWS // 2):
+    for pair in range(HALO // 2):
         block = jnp.concatenate([slices[2 * pair], slices[2 * pair + 1]], axis=1)
         product = lax.dot_general(block, block, (((1,), (1,)), ((), ())), preferred_element_type=F32)
         high, error = two_sum(high, product)
         low = low + error
+    return high, low
+
+
+def near_kernel(inner, coefs, prior, received, image, high_out, low_out, outer, outer_coefs, slices, most):
+    both_sides(True, (received, inner, coefs, prior, image, most, outer, outer_coefs))
+    zero = jnp.zeros(high_out.shape, F32)
+    high_out[...], low_out[...] = gram_pieces(image, most, slices, zero, zero)
+
+
+def far_kernel(
+    inner, coefs, prior, received, high_in, low_in, image, message, outer, outer_coefs, slices, most
+):
+    lanes = lane_ids()
+    both_sides(False, (received, inner, coefs, prior, image, most, outer, outer_coefs))
+    high, low = gram_pieces(image, most, slices, high_in[...], low_in[...])
+    width = PROBES * SLICES
 
     def fold(high, low, blocks):
         total_high, total_low = None, None
@@ -424,7 +437,7 @@
     message[...] = jnp.broadcast_to(total[None, 0:4], message.shape)
 
 
-def factor_kernel(count, received, image, basis, factor, held, sems):
+def factor_kernel(count, received, near, far, basis, factor, held, sems):
     upper_half = lax.broadcasted_iota(jnp.int32, (8, LANES), 0) < 4
     total, rest = summed(received)
     rest = rest + roll_lanes(total, -PROBES)
@@ -483,16 +496,18 @@
     ]
 
     copies = []
+    odd_y = is_odd("gy")
     for level in range(LEVELS):
-        for y in range(ROWS):
-            outs = [None, None]
-            for index in range(PROBES):
-                value = image[y, level, index // 8, index % 8 : index % 8 + 1, :]
-                for part in range(index // 8, 2):
-                    term = columns[index][8 * part : 8 * part + 8] * value
-                    outs[part] = term if outs[part] is None else outs[part] + term
-            for part in range(2):
-                held[level, pl.ds(part * 8 * ROWS + y, 8, stride=ROWS), :] = outs[part]
+        for image, base in ((near, 8 * (1 - odd_y)), (far, 8 * odd_y)):
+            for y in range(HALO):
+                outs = [None, None]
+                for index in range(PROBES):
+                    value = image[y, level, index // 8, index % 8 : index % 8 + 1, :]
+                    for part in range(index // 8, 2):
+                        term = columns[index][8 * part : 8 * part + 8] * value
+                        outs[part] = term if outs[part] is None else outs[part] + term
+                for part in range(2):
+                    held[level, pl.ds(base + (part * 8 * ROWS + y), 8, stride=ROWS), :] = outs[part]
         copies.append(pltpu.make_async_copy(held.at[level], basis.at[level], sems.at[level]))
         copies[-1].start()
     for copy in copies:
@@ -537,7 +552,8 @@
     halo, first, second = call(
         merge_kernel, [(X_PARTS,) + tile, (Y_PARTS,) + tile, (Y_PARTS,) + tile]
     )(swap(edges, "gx", 0), swap(edges, "gx", 1), source, fields)
-    first, second = swap(first, "gy", 0), swap(second, "gy", 1)
+    second = swap(second, "gy", 1)
+    first = swap(first, "gy", 0)
     field = (ROWS, LEVELS, 3) + tile
     derived = (2, DERIVED, ROWS, LANES)
     values = HALO * math.prod(field)
@@ -546,15 +562,21 @@
         [(HALO,) + field, derived],
         cost=pl.CostEstimate(flops=20 * values, bytes_accessed=8 * values, transcendentals=0),
     )(source, halo, fields)
-    image, message = call(
-        stencil_kernel,
-        [(ROWS, LEVELS, 2) + tile, (size_y, 4, LANES)],
-        [
-            pltpu.VMEM((HALO + 1,) + field, F32),
-            pltpu.VMEM(derived, F32),
-            pltpu.VMEM((ROWS, PROBES * SLICES, LEVELS * LANES), jnp.bfloat16),
-        ],
-    )(inner, coefs, prior, first, second)
+    half = (HALO, LEVELS, 2) + tile
+    width = PROBES * SLICES
+    scratch = [
+        pltpu.VMEM((HALO + 1, HALO, LEVELS, 3) + tile, F32),
+        pltpu.VMEM((2, DERIVED, HALO, LANES), F32),
+        pltpu.VMEM((HALO, width, LEVELS * LANES), jnp.bfloat16),
+        pltpu.VMEM((2,) + tile, F32),
+    ]
+    near, high, low = call(
+        near_kernel,
+        [half, (width, width), (width, width)],
+        scratch,
+        cost=pl.CostEstimate(flops=20 * values, bytes_accessed=8 * values, transcendentals=0),
+    )(inner, coefs, prior, first)
+    far, message = call(far_kernel, [half, (size_y, 4, LANES)], scratch)(inner, coefs, prior, second, high, low)
     received = exchange(message, "gy")
     (message,) = call(sum_kernel, [(size_x, 4, LANES)])(received)
     received = exchange(message, "gx")
@@ -563,7 +585,7 @@
         [flat, (PROBES, PROBES)],
         [pltpu.VMEM(flat, F32), pltpu.SemaphoreType.DMA((LEVELS,))],
         spaces=[pltpu.HBM, pltpu.VMEM],
-    )(received, image)
+    )(received, near, far)
     return basis.reshape(probes.shape), factor
 
 

time: 60.4 us -> 57.7 us (0.955)
  waiting for transfers between devices: 5.51 us -> 3.11 us
    ppermute x4, waiting for transfers between devices: 5.51 us -> 3.11 us  [swap(): return lax.ppermute(value, axis, pairs + [(j, i) for i, j in pairs])]
    pallas_call x6 -> x7, Pallas kernels: 12.8 us -> 12.3 us  [run(): pl.pallas_call(kernel, out_shape=[jax.ShapeDtypeStruct(shape, F32) for sh...]
  transfers between devices with their start and end apart: 4 -> 4, of which waited for: 2 -> 2; matrix products, arithmetic and copies ran while one was open for 0% -> 0% of each run, Pallas kernels for 4% -> 8%
where the time goes in v6:
time: 57.7 us; the launch traced here: 57.4 us
  blocking collectives  30.1 us (52%)
  Pallas kernels  12.3 us (21%)
  starting transfers between devices  11 us (19%)
  waiting for transfers between devices  3.11 us (5%)
  between operations  0.85 us (1%)
    all_to_all x2, blocking collectives, exchange(): received = lax.all_to_all(message, axis, 0, 0)  30.1 us
    pallas_call x7, Pallas kernels, run(): pl.pallas_call(kernel, out_shape=[jax.ShapeDtypeStruct(shape, F32) for sh...  12.3 us
    ppermute x4, starting transfers between devices, swap(): return lax.ppermute(value, axis, pairs + [(j, i) for i, j in pairs])  11 us
    ppermute x4, waiting for transfers between devices, swap(): return lax.ppermute(value, axis, pairs + [(j, i) for i, j in pairs])  3.11 us
  transfers between devices with their start and end apart: 4, of which 2 were waited for; matrix products, arithmetic and copies ran while one was open for 0% of the time, Pallas kernels for 8%

profile of v6, /device:TPU:1, one launch (start us, length us, event | category | flops | bytes accessed | tf_op | source)
XLA Modules:
  0.0 57.4 jit_solution(13183745447304002206)
XLA Ops:
  0.6 1.4 %shard_map.77 = (f32[16,4,2,8,128]{4,3,2,1,0:T(8,128)S(1)}, f32[22,8,128]{2,1,0:T(8,128)S(1)}, f32[17,16,128]{2,1,0:T(8,128)S(1)}, f32[4,16,128]{2,1,0:T(8,128)S(1)}) custom-call(f32[4,256,128]{2,1,0:T(8,128)} %bitcast.6, f32[2,4,16,128]{3,2,1,0:T(8,128)} %winds_in.1, f32[4,16,128]{2,1,0:T(8,128)} %diffusivity_in.1, f32[16,128]{1,0:T(8,128)} %mixing_in.1, ...), custom_call_target="tpu_custom_call" | custom-call | tf_op jit(solution)/shard_map/pallas_call | solution.py:519
  2.0 0.7 %collective-permute-start.1 = (f32[22,8,128]{2,1,0:T(8,128)S(1)}, f32[22,8,128]{2,1,0:T(8,128)S(1)}, u32[]{:S(2)}, u32[]{:S(2)}) collective-permute-start(f32[22,8,128]{2,1,0:T(8,128)S(1)} %get-tuple-element.19), channel_id=1, source_target_pairs={{32,64},{96,128},{160,192},{64,32},{128,96},{192,160},{33,65},{97,... | collective-permute-start | bytes 270344 | tf_op jit(solution)/shard_map/ppermute | solution.py:539
  2.7 5.4 %collective-permute-start = (f32[22,8,128]{2,1,0:T(8,128)S(1)}, f32[22,8,128]{2,1,0:T(8,128)S(1)}, u32[]{:S(2)}, u32[]{:S(2)}) collective-permute-start(f32[22,8,128]{2,1,0:T(8,128)S(1)} %get-tuple-element.19), channel_id=1, source_target_pairs={{0,32},{64,96},{128,160},{192,224},{32,0},{96,64},{160,128},{224,1... | collective-permute-start | bytes 270344 | tf_op jit(solution)/shard_map/ppermute | solution.py:539
  8.1 0.0 collective-permute-done.1.second
  8.1 1.9 %collective-permute-done.first = f32[22,8,128]{2,1,0:T(8,128)S(1)} collective-permute-done((f32[22,8,128]{2,1,0:T(8,128)S(1)}, f32[22,8,128]{2,1,0:T(8,128)S(1)}, u32[]{:S(2)}, u32[]{:S(2)}) %collective-permute-start) | collective-permute-done | bytes 90144 | tf_op jit(solution)/shard_map/ppermute | solution.py:539
  10.1 0.1 shard_map.78
  10.2 1.9 %collective-permute-start.3 = (f32[92,8,128]{2,1,0:T(8,128)S(1)}, f32[92,8,128]{2,1,0:T(8,128)S(1)}, u32[]{:S(2)}, u32[]{:S(2)}) collective-permute-start(f32[92,8,128]{2,1,0:T(8,128)S(1)} %get-tuple-element.26), channel_id=1, source_target_pairs={{0,1},{2,3},{4,5},{6,7},{8,9},{10,11},{12,13},{14,15},{16,17},{18,... | collective-permute-start | bytes 1130504 | tf_op jit(solution)/shard_map/ppermute | solution.py:539
  12.1 3.0 %collective-permute-start.2 = (f32[92,8,128]{2,1,0:T(8,128)S(1)}, f32[92,8,128]{2,1,0:T(8,128)S(1)}, u32[]{:S(2)}, u32[]{:S(2)}) collective-permute-start(f32[92,8,128]{2,1,0:T(8,128)S(1)} %get-tuple-element.25), channel_id=1, source_target_pairs={{1,2},{3,4},{5,6},{7,8},{9,10},{11,12},{13,14},{15,16},{17,18},{19... | collective-permute-start | bytes 1130504 | tf_op jit(solution)/shard_map/ppermute | solution.py:539
  15.1 2.1 %shard_map.79 = (f32[8,16,4,3,8,128]{5,4,3,2,1,0:T(8,128)S(1)}, f32[2,25,16,128]{3,2,1,0:T(8,128)S(1)}) custom-call(f32[16,4,2,8,128]{4,3,2,1,0:T(8,128)S(1)} %get-tuple-element.18.source, f32[22,8,128]{2,1,0:T(8,128)S(1)} %get-tuple-element.21.halo, f32[17,16,128]{2,1,0:T(8,128)S(1)} %get-tuple-element.20.fields), custom_call_target="tpu_custom_call" | custom-call | flops 31457280 | bytes 12582912 | tf_op jit(solution)/shard_map/pallas_call | solution.py:519
  17.2 0.0 collective-permute-done.3.received
  17.2 2.6 %shard_map.80 = (f32[8,4,2,8,128]{4,3,2,1,0:T(8,128)S(1)}, f32[64,64]{1,0:T(8,128)S(1)}, f32[64,64]{1,0:T(8,128)S(1)}) custom-call(f32[8,16,4,3,8,128]{5,4,3,2,1,0:T(8,128)S(1)} %get-tuple-element.22.inner, f32[2,25,16,128]{3,2,1,0:T(8,128)S(1)} %get-tuple-element.23.coefs, f32[4,16,128]{2,1,0:T(8,128)S(1)} %get-tuple-element.24.prior, ...), custom_call_target="tpu_custom_call" | custom-call | flops 31457280 | bytes 12582912 | tf_op jit(solution)/shard_map/pallas_call | solution.py:519
  19.8 1.2 %collective-permute-done.2.received = f32[92,8,128]{2,1,0:T(8,128)S(1)} collective-permute-done((f32[92,8,128]{2,1,0:T(8,128)S(1)}, f32[92,8,128]{2,1,0:T(8,128)S(1)}, u32[]{:S(2)}, u32[]{:S(2)}) %collective-permute-start.2) | collective-permute-done | bytes 376864 | tf_op jit(solution)/shard_map/ppermute | solution.py:539
  21.0 2.8 %shard_map.81 = (f32[8,4,2,8,128]{4,3,2,1,0:T(8,128)S(1)}, f32[32,4,128]{2,1,0:T(4,128)S(1)}) custom-call(f32[8,16,4,3,8,128]{5,4,3,2,1,0:T(8,128)S(1)} %get-tuple-element.22.inner, f32[2,25,16,128]{3,2,1,0:T(8,128)S(1)} %get-tuple-element.23.coefs, f32[4,16,128]{2,1,0:T(8,128)S(1)} %get-tuple-element.24.prior, ...), custom_call_target="tpu_custom_call" | custom-call | tf_op jit(solution)/shard_map/pallas_call | solution.py:519
  23.8 16.2 %all_to_all.10 = f32[32,4,128]{2,1,0:T(4,128)S(1)} all-to-all(f32[32,4,128]{2,1,0:T(4,128)S(1)} %get-tuple-element.29), channel_id=1, replica_groups=mesh['gx'=8,'gy'=32] {'gy'}, dimensions={0} | all-to-all | bytes 131072 | tf_op jit(solution)/shard_map/all_to_all | solution.py:542
  40.0 0.1 shard_map.82
  40.1 13.9 %all_to_all.11 = f32[8,4,128]{2,1,0:T(4,128)S(1)} all-to-all(f32[8,4,128]{2,1,0:T(4,128)S(1)} %shard_map.82), channel_id=1, replica_groups=mesh['gx'=8,'gy'=32] {'gx'}, dimensions={0} | all-to-all | bytes 32768 | tf_op jit(solution)/shard_map/all_to_all | solution.py:542
  54.0 3.2 %shard_map.83 = (f32[4,256,128]{2,1,0:T(8,128)}, f32[16,16]{1,0:T(8,128)}) custom-call(f32[4,8,128]{2,1,0:T(8,128)S(1)} %bitcast.5, f32[8,4,2,8,128]{4,3,2,1,0:T(8,128)S(1)} %get-tuple-element.30.refs_1_, f32[8,4,2,8,128]{4,3,2,1,0:T(8,128)S(1)} %get-tuple-element.31.refs_2_), custom_call_target="tpu_custom_call" | custom-call | tf_op jit(solution)/shard_map/pallas_call | solution.py:519
Async XLA Ops:
  2.0 6.1 %collective-permute-start.1 = (f32[22,8,128]{2,1,0:T(8,128)S(1)}, f32[22,8,128]{2,1,0:T(8,128)S(1)}, u32[]{:S(2)}, u32[]{:S(2)}) collective-permute-start(f32[22,8,128]{2,1,0:T(8,128)S(1)} %get-tuple-element.19), channel_id=1, source_target_pairs={{32,64},{96,128},{160,192},{64,32},{128,96},{192,160},{33,65},{97,... | collective-permute-start | bytes 270344 | tf_op jit(solution)/shard_map/ppermute | solution.py:539
  2.7 7.4 %collective-permute-start = (f32[22,8,128]{2,1,0:T(8,128)S(1)}, f32[22,8,128]{2,1,0:T(8,128)S(1)}, u32[]{:S(2)}, u32[]{:S(2)}) collective-permute-start(f32[22,8,128]{2,1,0:T(8,128)S(1)} %get-tuple-element.19), channel_id=1, source_target_pairs={{0,32},{64,96},{128,160},{192,224},{32,0},{96,64},{160,128},{224,1... | collective-permute-start | bytes 270344 | tf_op jit(solution)/shard_map/ppermute | solution.py:539
  10.2 7.0 %collective-permute-start.3 = (f32[92,8,128]{2,1,0:T(8,128)S(1)}, f32[92,8,128]{2,1,0:T(8,128)S(1)}, u32[]{:S(2)}, u32[]{:S(2)}) collective-permute-start(f32[92,8,128]{2,1,0:T(8,128)S(1)} %get-tuple-element.26), channel_id=1, source_target_pairs={{0,1},{2,3},{4,5},{6,7},{8,9},{10,11},{12,13},{14,15},{16,17},{18,... | collective-permute-start | bytes 1130504 | tf_op jit(solution)/shard_map/ppermute | solution.py:539
  12.1 8.9 %collective-permute-start.2 = (f32[92,8,128]{2,1,0:T(8,128)S(1)}, f32[92,8,128]{2,1,0:T(8,128)S(1)}, u32[]{:S(2)}, u32[]{:S(2)}) collective-permute-start(f32[92,8,128]{2,1,0:T(8,128)S(1)} %get-tuple-element.25), channel_id=1, source_target_pairs={{1,2},{3,4},{5,6},{7,8},{9,10},{11,12},{13,14},{15,16},{17,18},{19... | collective-permute-start | bytes 1130504 | tf_op jit(solution)/shard_map/ppermute | solution.py:539

commit v7 on v6

--- a/solution.py
+++ b/solution.py
@@ -19,6 +19,7 @@
 GROUPS = 3
 EAST, WEST, NORTH, SOUTH, CENTER, RATE, OBS, DERIVED = 0, 4, 8, 12, 16, 20, 21, 25
 X_PARTS = ROWS + 2 * GROUPS
+PAIRS = [(y, y + 8) for y in range(8)] + [(ROWS + 2 * group, ROWS + 2 * group + 1) for group in range(GROUPS)]
 Y_SOURCE, Y_HALO, Y_COEF, Y_COEF_HALO, Y_PARTS = 0, 64, 72, 89, 92
 SLICES = 4
 
@@ -34,7 +35,7 @@
 
 def pack_kernel(
     probes_in, winds_in, diffusivity_in, mixing_in, prior_in, obs_in,
-    source, edges, fields, prior, probes, sems,
+    source, first, second, fields, prior, probes, edges, sems,
 ):
     coef_copies = [
         pltpu.make_async_copy(diffusivity_in, fields.at[pl.ds(0, 4)], sems.at[0]),
@@ -77,6 +78,14 @@
                 held = put(held, value, 2 * level + part)
         edges[y] = held
 
+    inner = lanes % 16 < 8
+    odd_x = is_odd("gx")
+    for index, (low, high) in enumerate(PAIRS):
+        to_east = jnp.where(inner, edges[low], roll_lanes(edges[high], HALO))
+        to_west = jnp.where(inner, roll_lanes(edges[high], -HALO), edges[low])
+        first[index] = jnp.where(odd_x == 0, to_east, to_west)
+        second[index] = jnp.where(odd_x == 0, to_west, to_east)
+
 
 def is_odd(axis):
     return lax.axis_index(axis) % 2
@@ -85,10 +94,11 @@
 def merge_kernel(first, second, source, fields, halo, first_out, second_out):
     inner = lane_ids() % 16 < 8
     odd_x, odd_y = is_odd("gx"), is_odd("gy")
-    for index in range(X_PARTS):
+    for index, (low, high) in enumerate(PAIRS):
         from_east = jnp.where(odd_x == 0, first[index], second[index])
         from_west = jnp.where(odd_x == 0, second[index], first[index])
-        halo[index] = jnp.where(inner, roll_lanes(from_east, -HALO), roll_lanes(from_west, HALO))
+        halo[low] = jnp.where(inner, roll_lanes(from_east, -HALO), roll_lanes(from_west, HALO))
+        halo[high] = jnp.where(inner, from_east, from_west)
     for tile, out in ((1 - odd_y, first_out), (odd_y, second_out)):
         base = pl.multiple_of(8 * tile, 8)
         for y in range(8):
@@ -543,15 +553,15 @@
         return received.reshape((message.shape[0] // 2,) + tile)
 
     flat = (LEVELS, PROBES * ROWS, LANES)
-    source, edges, fields, prior = call(
+    source, first, second, fields, prior = call(
         pack_kernel,
-        [(ROWS, LEVELS, 2) + tile, (X_PARTS,) + tile, (FIELDS, ROWS, LANES), (LEVELS, ROWS, LANES)],
-        [pltpu.VMEM(flat, F32), pltpu.SemaphoreType.DMA((7,))],
+        [(ROWS, LEVELS, 2) + tile, (len(PAIRS),) + tile, (len(PAIRS),) + tile, (FIELDS, ROWS, LANES), (LEVELS, ROWS, LANES)],
+        [pltpu.VMEM(flat, F32), pltpu.VMEM((X_PARTS,) + tile, F32), pltpu.SemaphoreType.DMA((7,))],
         pltpu.HBM,
     )(*(pltpu.with_memory_space_constraint(a, pltpu.HBM) for a in (probes.reshape(flat), winds, diffusivity, mixing, prior_scale, obs_weight)))
     halo, first, second = call(
         merge_kernel, [(X_PARTS,) + tile, (Y_PARTS,) + tile, (Y_PARTS,) + tile]
-    )(swap(edges, "gx", 0), swap(edges, "gx", 1), source, fields)
+    )(swap(first, "gx", 0), swap(second, "gx", 1), source, fields)
     second = swap(second, "gy", 1)
     first = swap(first, "gy", 0)
     field = (ROWS, LEVELS, 3) + tile

time: 57.7 us -> 58.3 us (1.010)
  blocking collectives: 30.1 us -> 33.1 us
  starting transfers between devices: 11 us -> 8.58 us
    all_to_all x2, blocking collectives: 30.1 us -> 33.1 us  [exchange(): received = lax.all_to_all(message, axis, 0, 0)]
    ppermute x4, starting transfers between devices: 11 us -> 8.58 us  [swap(): return lax.ppermute(value, axis, pairs + [(j, i) for i, j in pairs])]
where the time goes in v7:
time: 58.3 us; the launch traced here: 58.1 us
  blocking collectives  33.1 us (57%)
  Pallas kernels  12.4 us (21%)
  starting transfers between devices  8.58 us (15%)
  waiting for transfers between devices  3.08 us (5%)
  between operations  0.85 us (1%)
    all_to_all x2, blocking collectives, exchange(): received = lax.all_to_all(message, axis, 0, 0)  33.1 us
    pallas_call x7, Pallas kernels, run(): pl.pallas_call(kernel, out_shape=[jax.ShapeDtypeStruct(shape, F32) for sh...  12.4 us
    ppermute x4, starting transfers between devices, swap(): return lax.ppermute(value, axis, pairs + [(j, i) for i, j in pairs])  8.58 us
    ppermute x4, waiting for transfers between devices, swap(): return lax.ppermute(value, axis, pairs + [(j, i) for i, j in pairs])  3.08 us
  transfers between devices with their start and end apart: 4, of which 2 were waited for; matrix products, arithmetic and copies ran while one was open for 0% of the time, Pallas kernels for 8%

profile of v7, /device:TPU:1, one launch (start us, length us, event | category | flops | bytes accessed | tf_op | source)
XLA Modules:
  0.0 58.1 jit_solution(7441343622394416548)
XLA Ops:
  0.6 1.5 %shard_map.77 = (f32[16,4,2,8,128]{4,3,2,1,0:T(8,128)S(1)}, f32[11,8,128]{2,1,0:T(8,128)S(1)}, f32[11,8,128]{2,1,0:T(8,128)S(1)}, f32[17,16,128]{2,1,0:T(8,128)S(1)}, f32[4,16,128]{2,1,0:T(8,128)S(1)}) custom-call(f32[4,256,128]{2,1,0:T(8,128)} %bitcast.6, f32[2,4,16,128]{3,2,1,0:T(8,128)} %winds_in.1, f32[4,16,128]{2,1,0:T(8,128)} %diffusivity_in.1, ...), custom_call_target="tpu_custom_call" | custom-call | tf_op jit(solution)/shard_map/pallas_call | solution.py:529
  2.1 2.6 %collective-permute-start = (f32[11,8,128]{2,1,0:T(8,128)S(1)}, f32[11,8,128]{2,1,0:T(8,128)S(1)}, u32[]{:S(2)}, u32[]{:S(2)}) collective-permute-start(f32[11,8,128]{2,1,0:T(8,128)S(1)} %get-tuple-element.20), channel_id=1, source_target_pairs={{0,32},{64,96},{128,160},{192,224},{32,0},{96,64},{160,128},{224,1... | collective-permute-start | bytes 135176 | tf_op jit(solution)/shard_map/ppermute | solution.py:549
  4.7 0.7 %collective-permute-start.1 = (f32[11,8,128]{2,1,0:T(8,128)S(1)}, f32[11,8,128]{2,1,0:T(8,128)S(1)}, u32[]{:S(2)}, u32[]{:S(2)}) collective-permute-start(f32[11,8,128]{2,1,0:T(8,128)S(1)} %get-tuple-element.21), channel_id=1, source_target_pairs={{32,64},{96,128},{160,192},{64,32},{128,96},{192,160},{33,65},{97,... | collective-permute-start | bytes 135176 | tf_op jit(solution)/shard_map/ppermute | solution.py:549
  5.3 0.8 %collective-permute-done.first = f32[11,8,128]{2,1,0:T(8,128)S(1)} collective-permute-done((f32[11,8,128]{2,1,0:T(8,128)S(1)}, f32[11,8,128]{2,1,0:T(8,128)S(1)}, u32[]{:S(2)}, u32[]{:S(2)}) %collective-permute-start) | collective-permute-done | bytes 45088 | tf_op jit(solution)/shard_map/ppermute | solution.py:549
  6.1 0.0 collective-permute-done.1.second
  6.1 0.1 shard_map.78
  6.2 3.5 %collective-permute-start.3 = (f32[92,8,128]{2,1,0:T(8,128)S(1)}, f32[92,8,128]{2,1,0:T(8,128)S(1)}, u32[]{:S(2)}, u32[]{:S(2)}) collective-permute-start(f32[92,8,128]{2,1,0:T(8,128)S(1)} %get-tuple-element.28), channel_id=1, source_target_pairs={{0,1},{2,3},{4,5},{6,7},{8,9},{10,11},{12,13},{14,15},{16,17},{18,... | collective-permute-start | bytes 1130504 | tf_op jit(solution)/shard_map/ppermute | solution.py:549
  9.7 1.9 %collective-permute-start.2 = (f32[92,8,128]{2,1,0:T(8,128)S(1)}, f32[92,8,128]{2,1,0:T(8,128)S(1)}, u32[]{:S(2)}, u32[]{:S(2)}) collective-permute-start(f32[92,8,128]{2,1,0:T(8,128)S(1)} %get-tuple-element.27), channel_id=1, source_target_pairs={{1,2},{3,4},{5,6},{7,8},{9,10},{11,12},{13,14},{15,16},{17,18},{19... | collective-permute-start | bytes 1130504 | tf_op jit(solution)/shard_map/ppermute | solution.py:549
  11.6 2.1 %shard_map.79 = (f32[8,16,4,3,8,128]{5,4,3,2,1,0:T(8,128)S(1)}, f32[2,25,16,128]{3,2,1,0:T(8,128)S(1)}) custom-call(f32[16,4,2,8,128]{4,3,2,1,0:T(8,128)S(1)} %get-tuple-element.19.source, f32[22,8,128]{2,1,0:T(8,128)S(1)} %get-tuple-element.23.halo, f32[17,16,128]{2,1,0:T(8,128)S(1)} %get-tuple-element.22.fields), custom_call_target="tpu_custom_call" | custom-call | flops 31457280 | bytes 12582912 | tf_op jit(solution)/shard_map/pallas_call | solution.py:529
  13.7 0.0 collective-permute-done.3.received
  13.7 2.6 %shard_map.80 = (f32[8,4,2,8,128]{4,3,2,1,0:T(8,128)S(1)}, f32[64,64]{1,0:T(8,128)S(1)}, f32[64,64]{1,0:T(8,128)S(1)}) custom-call(f32[8,16,4,3,8,128]{5,4,3,2,1,0:T(8,128)S(1)} %get-tuple-element.24.inner, f32[2,25,16,128]{3,2,1,0:T(8,128)S(1)} %get-tuple-element.25.coefs, f32[4,16,128]{2,1,0:T(8,128)S(1)} %get-tuple-element.26.prior, ...), custom_call_target="tpu_custom_call" | custom-call | flops 31457280 | bytes 12582912 | tf_op jit(solution)/shard_map/pallas_call | solution.py:529
  16.3 2.3 %collective-permute-done.2.received = f32[92,8,128]{2,1,0:T(8,128)S(1)} collective-permute-done((f32[92,8,128]{2,1,0:T(8,128)S(1)}, f32[92,8,128]{2,1,0:T(8,128)S(1)}, u32[]{:S(2)}, u32[]{:S(2)}) %collective-permute-start.2) | collective-permute-done | bytes 376864 | tf_op jit(solution)/shard_map/ppermute | solution.py:549
  18.6 2.8 %shard_map.81 = (f32[8,4,2,8,128]{4,3,2,1,0:T(8,128)S(1)}, f32[32,4,128]{2,1,0:T(4,128)S(1)}) custom-call(f32[8,16,4,3,8,128]{5,4,3,2,1,0:T(8,128)S(1)} %get-tuple-element.24.inner, f32[2,25,16,128]{3,2,1,0:T(8,128)S(1)} %get-tuple-element.25.coefs, f32[4,16,128]{2,1,0:T(8,128)S(1)} %get-tuple-element.26.prior, ...), custom_call_target="tpu_custom_call" | custom-call | tf_op jit(solution)/shard_map/pallas_call | solution.py:529
  21.4 14.4 %all_to_all.10 = f32[32,4,128]{2,1,0:T(4,128)S(1)} all-to-all(f32[32,4,128]{2,1,0:T(4,128)S(1)} %get-tuple-element.31), channel_id=1, replica_groups=mesh['gx'=8,'gy'=32] {'gy'}, dimensions={0} | all-to-all | bytes 131072 | tf_op jit(solution)/shard_map/all_to_all | solution.py:552
  35.9 0.1 shard_map.82
  36.0 18.7 %all_to_all.11 = f32[8,4,128]{2,1,0:T(4,128)S(1)} all-to-all(f32[8,4,128]{2,1,0:T(4,128)S(1)} %shard_map.82), channel_id=1, replica_groups=mesh['gx'=8,'gy'=32] {'gx'}, dimensions={0} | all-to-all | bytes 32768 | tf_op jit(solution)/shard_map/all_to_all | solution.py:552
  54.7 3.2 %shard_map.83 = (f32[4,256,128]{2,1,0:T(8,128)}, f32[16,16]{1,0:T(8,128)}) custom-call(f32[4,8,128]{2,1,0:T(8,128)S(1)} %bitcast.5, f32[8,4,2,8,128]{4,3,2,1,0:T(8,128)S(1)} %get-tuple-element.32.refs_1_, f32[8,4,2,8,128]{4,3,2,1,0:T(8,128)S(1)} %get-tuple-element.33.refs_2_), custom_call_target="tpu_custom_call" | custom-call | tf_op jit(solution)/shard_map/pallas_call | solution.py:529
Async XLA Ops:
  2.1 4.0 %collective-permute-start = (f32[11,8,128]{2,1,0:T(8,128)S(1)}, f32[11,8,128]{2,1,0:T(8,128)S(1)}, u32[]{:S(2)}, u32[]{:S(2)}) collective-permute-start(f32[11,8,128]{2,1,0:T(8,128)S(1)} %get-tuple-element.20), channel_id=1, source_target_pairs={{0,32},{64,96},{128,160},{192,224},{32,0},{96,64},{160,128},{224,1... | collective-permute-start | bytes 135176 | tf_op jit(solution)/shard_map/ppermute | solution.py:549
  4.7 1.4 %collective-permute-start.1 = (f32[11,8,128]{2,1,0:T(8,128)S(1)}, f32[11,8,128]{2,1,0:T(8,128)S(1)}, u32[]{:S(2)}, u32[]{:S(2)}) collective-permute-start(f32[11,8,128]{2,1,0:T(8,128)S(1)} %get-tuple-element.21), channel_id=1, source_target_pairs={{32,64},{96,128},{160,192},{64,32},{128,96},{192,160},{33,65},{97,... | collective-permute-start | bytes 135176 | tf_op jit(solution)/shard_map/ppermute | solution.py:549
  6.2 7.5 %collective-permute-start.3 = (f32[92,8,128]{2,1,0:T(8,128)S(1)}, f32[92,8,128]{2,1,0:T(8,128)S(1)}, u32[]{:S(2)}, u32[]{:S(2)}) collective-permute-start(f32[92,8,128]{2,1,0:T(8,128)S(1)} %get-tuple-element.28), channel_id=1, source_target_pairs={{0,1},{2,3},{4,5},{6,7},{8,9},{10,11},{12,13},{14,15},{16,17},{18,... | collective-permute-start | bytes 1130504 | tf_op jit(solution)/shard_map/ppermute | solution.py:549
  9.7 8.9 %collective-permute-start.2 = (f32[92,8,128]{2,1,0:T(8,128)S(1)}, f32[92,8,128]{2,1,0:T(8,128)S(1)}, u32[]{:S(2)}, u32[]{:S(2)}) collective-permute-start(f32[92,8,128]{2,1,0:T(8,128)S(1)} %get-tuple-element.27), channel_id=1, source_target_pairs={{1,2},{3,4},{5,6},{7,8},{9,10},{11,12},{13,14},{15,16},{17,18},{19... | collective-permute-start | bytes 1130504 | tf_op jit(solution)/shard_map/ppermute | solution.py:549

commit v8 on v7

--- a/solution.py
+++ b/solution.py
@@ -35,7 +35,7 @@
 
 def pack_kernel(
     probes_in, winds_in, diffusivity_in, mixing_in, prior_in, obs_in,
-    source, first, second, fields, prior, probes, edges, sems,
+    source, second, first, fields, prior, probes, edges, sems,
 ):
     coef_copies = [
         pltpu.make_async_copy(diffusivity_in, fields.at[pl.ds(0, 4)], sems.at[0]),
@@ -91,7 +91,7 @@
     return lax.axis_index(axis) % 2
 
 
-def merge_kernel(first, second, source, fields, halo, first_out, second_out):
+def merge_kernel(second, first, source, fields, halo, first_out, second_out):
     inner = lane_ids() % 16 < 8
     odd_x, odd_y = is_odd("gx"), is_odd("gy")
     for index, (low, high) in enumerate(PAIRS):
@@ -553,7 +553,7 @@
         return received.reshape((message.shape[0] // 2,) + tile)
 
     flat = (LEVELS, PROBES * ROWS, LANES)
-    source, first, second, fields, prior = call(
+    source, second, first, fields, prior = call(
         pack_kernel,
         [(ROWS, LEVELS, 2) + tile, (len(PAIRS),) + tile, (len(PAIRS),) + tile, (FIELDS, ROWS, LANES), (LEVELS, ROWS, LANES)],
         [pltpu.VMEM(flat, F32), pltpu.VMEM((X_PARTS,) + tile, F32), pltpu.SemaphoreType.DMA((7,))],
@@ -561,7 +561,7 @@
     )(*(pltpu.with_memory_space_constraint(a, pltpu.HBM) for a in (probes.reshape(flat), winds, diffusivity, mixing, prior_scale, obs_weight)))
     halo, first, second = call(
         merge_kernel, [(X_PARTS,) + tile, (Y_PARTS,) + tile, (Y_PARTS,) + tile]
-    )(swap(first, "gx", 0), swap(second, "gx", 1), source, fields)
+    )(swap(second, "gx", 1), swap(first, "gx", 0), source, fields)
     second = swap(second, "gy", 1)
     first = swap(first, "gy", 0)
     field = (ROWS, LEVELS, 3) + tile

time: 58.3 us -> 57.2 us (0.981)
  blocking collectives: 33.1 us -> 30.1 us
  starting transfers between devices: 8.58 us -> 11 us
    all_to_all x2, blocking collectives: 33.1 us -> 30.1 us  [exchange(): received = lax.all_to_all(message, axis, 0, 0)]
    ppermute x4, starting transfers between devices: 8.58 us -> 11 us  [swap(): return lax.ppermute(value, axis, pairs + [(j, i) for i, j in pairs])]
where the time goes in v8:
time: 57.2 us; the launch traced here: 57 us
  blocking collectives  30.1 us (53%)
  Pallas kernels  12.4 us (22%)
  starting transfers between devices  11 us (19%)
  waiting for transfers between devices  2.62 us (5%)
  between operations  0.85 us (1%)
    all_to_all x2, blocking collectives, exchange(): received = lax.all_to_all(message, axis, 0, 0)  30.1 us
    pallas_call x7, Pallas kernels, run(): pl.pallas_call(kernel, out_shape=[jax.ShapeDtypeStruct(shape, F32) for sh...  12.4 us
    ppermute x4, starting transfers between devices, swap(): return lax.ppermute(value, axis, pairs + [(j, i) for i, j in pairs])  11 us
    ppermute x4, waiting for transfers between devices, swap(): return lax.ppermute(value, axis, pairs + [(j, i) for i, j in pairs])  2.62 us
  transfers between devices with their start and end apart: 4, of which 2 were waited for; matrix products, arithmetic and copies ran while one was open for 0% of the time, Pallas kernels for 8%

profile of v8, /device:TPU:1, one launch (start us, length us, event | category | flops | bytes accessed | tf_op | source)
XLA Modules:
  0.0 57.0 jit_solution(574911775862433590)
XLA Ops:
  0.6 1.5 %shard_map.77 = (f32[16,4,2,8,128]{4,3,2,1,0:T(8,128)S(1)}, f32[11,8,128]{2,1,0:T(8,128)S(1)}, f32[11,8,128]{2,1,0:T(8,128)S(1)}, f32[17,16,128]{2,1,0:T(8,128)S(1)}, f32[4,16,128]{2,1,0:T(8,128)S(1)}) custom-call(f32[4,256,128]{2,1,0:T(8,128)} %bitcast.6, f32[2,4,16,128]{3,2,1,0:T(8,128)} %winds_in.1, f32[4,16,128]{2,1,0:T(8,128)} %diffusivity_in.1, ...), custom_call_target="tpu_custom_call" | custom-call | tf_op jit(solution)/shard_map/pallas_call | solution.py:529
  2.1 0.7 %collective-permute-start = (f32[11,8,128]{2,1,0:T(8,128)S(1)}, f32[11,8,128]{2,1,0:T(8,128)S(1)}, u32[]{:S(2)}, u32[]{:S(2)}) collective-permute-start(f32[11,8,128]{2,1,0:T(8,128)S(1)} %get-tuple-element.20), channel_id=1, source_target_pairs={{32,64},{96,128},{160,192},{64,32},{128,96},{192,160},{33,65},{97,... | collective-permute-start | bytes 135176 | tf_op jit(solution)/shard_map/ppermute | solution.py:549
  2.8 5.4 %collective-permute-start.1 = (f32[11,8,128]{2,1,0:T(8,128)S(1)}, f32[11,8,128]{2,1,0:T(8,128)S(1)}, u32[]{:S(2)}, u32[]{:S(2)}) collective-permute-start(f32[11,8,128]{2,1,0:T(8,128)S(1)} %get-tuple-element.21), channel_id=1, source_target_pairs={{0,32},{64,96},{128,160},{192,224},{32,0},{96,64},{160,128},{224,1... | collective-permute-start | bytes 135176 | tf_op jit(solution)/shard_map/ppermute | solution.py:549
  8.2 0.0 collective-permute-done.second
  8.2 1.4 %collective-permute-done.1.first = f32[11,8,128]{2,1,0:T(8,128)S(1)} collective-permute-done((f32[11,8,128]{2,1,0:T(8,128)S(1)}, f32[11,8,128]{2,1,0:T(8,128)S(1)}, u32[]{:S(2)}, u32[]{:S(2)}) %collective-permute-start.1) | collective-permute-done | bytes 45088 | tf_op jit(solution)/shard_map/ppermute | solution.py:549
  9.7 0.1 shard_map.78
  9.8 1.9 %collective-permute-start.3 = (f32[92,8,128]{2,1,0:T(8,128)S(1)}, f32[92,8,128]{2,1,0:T(8,128)S(1)}, u32[]{:S(2)}, u32[]{:S(2)}) collective-permute-start(f32[92,8,128]{2,1,0:T(8,128)S(1)} %get-tuple-element.28), channel_id=1, source_target_pairs={{0,1},{2,3},{4,5},{6,7},{8,9},{10,11},{12,13},{14,15},{16,17},{18,... | collective-permute-start | bytes 1130504 | tf_op jit(solution)/shard_map/ppermute | solution.py:549
  11.7 3.0 %collective-permute-start.2 = (f32[92,8,128]{2,1,0:T(8,128)S(1)}, f32[92,8,128]{2,1,0:T(8,128)S(1)}, u32[]{:S(2)}, u32[]{:S(2)}) collective-permute-start(f32[92,8,128]{2,1,0:T(8,128)S(1)} %get-tuple-element.27), channel_id=1, source_target_pairs={{1,2},{3,4},{5,6},{7,8},{9,10},{11,12},{13,14},{15,16},{17,18},{19... | collective-permute-start | bytes 1130504 | tf_op jit(solution)/shard_map/ppermute | solution.py:549
  14.7 2.1 %shard_map.79 = (f32[8,16,4,3,8,128]{5,4,3,2,1,0:T(8,128)S(1)}, f32[2,25,16,128]{3,2,1,0:T(8,128)S(1)}) custom-call(f32[16,4,2,8,128]{4,3,2,1,0:T(8,128)S(1)} %get-tuple-element.19.source, f32[22,8,128]{2,1,0:T(8,128)S(1)} %get-tuple-element.23.halo, f32[17,16,128]{2,1,0:T(8,128)S(1)} %get-tuple-element.22.fields), custom_call_target="tpu_custom_call" | custom-call | flops 31457280 | bytes 12582912 | tf_op jit(solution)/shard_map/pallas_call | solution.py:529
  16.8 0.0 collective-permute-done.3.received
  16.8 2.6 %shard_map.80 = (f32[8,4,2,8,128]{4,3,2,1,0:T(8,128)S(1)}, f32[64,64]{1,0:T(8,128)S(1)}, f32[64,64]{1,0:T(8,128)S(1)}) custom-call(f32[8,16,4,3,8,128]{5,4,3,2,1,0:T(8,128)S(1)} %get-tuple-element.24.inner, f32[2,25,16,128]{3,2,1,0:T(8,128)S(1)} %get-tuple-element.25.coefs, f32[4,16,128]{2,1,0:T(8,128)S(1)} %get-tuple-element.26.prior, ...), custom_call_target="tpu_custom_call" | custom-call | flops 31457280 | bytes 12582912 | tf_op jit(solution)/shard_map/pallas_call | solution.py:529
  19.4 1.2 %collective-permute-done.2.received = f32[92,8,128]{2,1,0:T(8,128)S(1)} collective-permute-done((f32[92,8,128]{2,1,0:T(8,128)S(1)}, f32[92,8,128]{2,1,0:T(8,128)S(1)}, u32[]{:S(2)}, u32[]{:S(2)}) %collective-permute-start.2) | collective-permute-done | bytes 376864 | tf_op jit(solution)/shard_map/ppermute | solution.py:549
  20.6 2.8 %shard_map.81 = (f32[8,4,2,8,128]{4,3,2,1,0:T(8,128)S(1)}, f32[32,4,128]{2,1,0:T(4,128)S(1)}) custom-call(f32[8,16,4,3,8,128]{5,4,3,2,1,0:T(8,128)S(1)} %get-tuple-element.24.inner, f32[2,25,16,128]{3,2,1,0:T(8,128)S(1)} %get-tuple-element.25.coefs, f32[4,16,128]{2,1,0:T(8,128)S(1)} %get-tuple-element.26.prior, ...), custom_call_target="tpu_custom_call" | custom-call | tf_op jit(solution)/shard_map/pallas_call | solution.py:529
  23.4 16.2 %all_to_all.10 = f32[32,4,128]{2,1,0:T(4,128)S(1)} all-to-all(f32[32,4,128]{2,1,0:T(4,128)S(1)} %get-tuple-element.31), channel_id=1, replica_groups=mesh['gx'=8,'gy'=32] {'gy'}, dimensions={0} | all-to-all | bytes 131072 | tf_op jit(solution)/shard_map/all_to_all | solution.py:552
  39.6 0.1 shard_map.82
  39.7 13.9 %all_to_all.11 = f32[8,4,128]{2,1,0:T(4,128)S(1)} all-to-all(f32[8,4,128]{2,1,0:T(4,128)S(1)} %shard_map.82), channel_id=1, replica_groups=mesh['gx'=8,'gy'=32] {'gx'}, dimensions={0} | all-to-all | bytes 32768 | tf_op jit(solution)/shard_map/all_to_all | solution.py:552
  53.6 3.2 %shard_map.83 = (f32[4,256,128]{2,1,0:T(8,128)}, f32[16,16]{1,0:T(8,128)}) custom-call(f32[4,8,128]{2,1,0:T(8,128)S(1)} %bitcast.5, f32[8,4,2,8,128]{4,3,2,1,0:T(8,128)S(1)} %get-tuple-element.32.refs_1_, f32[8,4,2,8,128]{4,3,2,1,0:T(8,128)S(1)} %get-tuple-element.33.refs_2_), custom_call_target="tpu_custom_call" | custom-call | tf_op jit(solution)/shard_map/pallas_call | solution.py:529
Async XLA Ops:
  2.1 6.1 %collective-permute-start = (f32[11,8,128]{2,1,0:T(8,128)S(1)}, f32[11,8,128]{2,1,0:T(8,128)S(1)}, u32[]{:S(2)}, u32[]{:S(2)}) collective-permute-start(f32[11,8,128]{2,1,0:T(8,128)S(1)} %get-tuple-element.20), channel_id=1, source_target_pairs={{32,64},{96,128},{160,192},{64,32},{128,96},{192,160},{33,65},{97,... | collective-permute-start | bytes 135176 | tf_op jit(solution)/shard_map/ppermute | solution.py:549
  2.8 6.9 %collective-permute-start.1 = (f32[11,8,128]{2,1,0:T(8,128)S(1)}, f32[11,8,128]{2,1,0:T(8,128)S(1)}, u32[]{:S(2)}, u32[]{:S(2)}) collective-permute-start(f32[11,8,128]{2,1,0:T(8,128)S(1)} %get-tuple-element.21), channel_id=1, source_target_pairs={{0,32},{64,96},{128,160},{192,224},{32,0},{96,64},{160,128},{224,1... | collective-permute-start | bytes 135176 | tf_op jit(solution)/shard_map/ppermute | solution.py:549
  9.8 7.0 %collective-permute-start.3 = (f32[92,8,128]{2,1,0:T(8,128)S(1)}, f32[92,8,128]{2,1,0:T(8,128)S(1)}, u32[]{:S(2)}, u32[]{:S(2)}) collective-permute-start(f32[92,8,128]{2,1,0:T(8,128)S(1)} %get-tuple-element.28), channel_id=1, source_target_pairs={{0,1},{2,3},{4,5},{6,7},{8,9},{10,11},{12,13},{14,15},{16,17},{18,... | collective-permute-start | bytes 1130504 | tf_op jit(solution)/shard_map/ppermute | solution.py:549
  11.7 8.9 %collective-permute-start.2 = (f32[92,8,128]{2,1,0:T(8,128)S(1)}, f32[92,8,128]{2,1,0:T(8,128)S(1)}, u32[]{:S(2)}, u32[]{:S(2)}) collective-permute-start(f32[92,8,128]{2,1,0:T(8,128)S(1)} %get-tuple-element.27), channel_id=1, source_target_pairs={{1,2},{3,4},{5,6},{7,8},{9,10},{11,12},{13,14},{15,16},{17,18},{19... | collective-permute-start | bytes 1130504 | tf_op jit(solution)/shard_map/ppermute | solution.py:549
